TPU v7x, 256 devices: a whole 4x4x8 slice. The times are simulated.
256 devices in a mesh: row: 8 (over z), col: 32 (over y, x, core).
Axes of the slice: x: 4, y: 4, z: 8, core: 2. Of those that a mesh axis runs over, the one named last changes fastest.
Arguments:
- acts: bfloat16 [2048, 8192], P('col', 'row'), may hold values from -6 to 6
- out_grads: bfloat16 [2048, 28672], P('row', 'col'), may hold values from -0.19921875 to 0.19921875
- weight: bfloat16 [8192, 28672], P('row', 'col'), may hold values from -0.0625 to 0.0625
- momentum: float32 [8192, 28672], P('row', 'col'), may hold values from -40 to 40, as said below
- basis: float32 [28672, 256], P('col'), may hold values from -0.03125 to 0.03125
Outputs:
- new_weight: bfloat16 [8192, 28672], P('row', 'col')
- new_momentum: float32 [8192, 28672], P('row', 'col')
- new_basis: float32 [28672, 256], P('col')
Inputs may be any that keep to these rules, and one draw needn't show every extreme that they name: momentum is a float32 matrix.
All inputs are finite; a program needn't handle non-finite values.
Results may differ from a plain program's by a relative error of at most 0.00065.
Values may be sent and summed in bfloat16 or wider, within the bound.
No kernel may reach another device: no remote copies, remote signals or barrier semaphores. Data moves between devices by JAX's collectives and lax.ppermute only.
A program may use at most 64 MiB of HBM per device.

v0:
```python
import math

import jax
import jax.numpy as jnp
from jax import lax
from jax.sharding import PartitionSpec as P

D = 8192
FF = 28672
RANK = 256


keep_rate = 0.95
step_rate = 0.01
norm_eps = 1e-06


def on_device(acts, out_grads, weight, momentum, basis):
    highest = lax.Precision.HIGHEST
    grads_all = lax.all_gather(out_grads, "row", axis=0, tiled=True)
    grad_tile = lax.dot_general(
        lax.all_gather(acts, "col", axis=0, tiled=True),
        grads_all,
        (((0,), (0,)), ((), ())),
        preferred_element_type=jnp.float32,
    )
    buffer = momentum + grad_tile
    proj = lax.psum(jnp.dot(buffer, basis, precision=highest), "col")
    gram = lax.psum(jnp.dot(proj.T, proj, precision=highest), "row")
    lower = jnp.linalg.cholesky(gram)
    ortho = jax.scipy.linalg.solve_triangular(lower, proj.T, lower=True).T
    partial_back = lax.dot_general(buffer, ortho, (((0,), (0,)), ((), ())), precision=highest)
    back = lax.psum(partial_back, "row")
    norms = lax.psum(jnp.sum(back * back, axis=0), "col")
    new_momentum = buffer - (1.0 - keep_rate) * jnp.dot(ortho, back.T, precision=highest)
    new_basis = back / jnp.sqrt(norms + norm_eps)
    factor = step_rate * math.sqrt(D * FF / RANK)
    new_weight = (
        weight.astype(jnp.float32) - factor * jnp.dot(ortho, new_basis.T, precision=highest)
    ).astype(jnp.bfloat16)
    return (new_weight, new_momentum, new_basis)


def solution(mesh):
    return jax.shard_map(
        on_device,
        mesh=mesh,
        in_specs=(
            P("col", "row"),
            P("row", "col"),
            P("row", "col"),
            P("row", "col"),
            P("col", None),
        ),
        out_specs=(P("row", "col"), P("row", "col"), P("col", None)),
        check_vma=False,
    )
```

profile of v0, /device:TPU:1, one launch (start us, length us, event | category | flops | bytes accessed | tf_op | source)
XLA Modules:
  0.0 558.0 jit_solution(12014669317024410395)
XLA Ops:
  8.7 54.8 %all-gather.5.cloned.1.call-done = bf16[2048,896]{1,0:T(8,128)(2,1)} async-done(((bf16[256,896]{1,0:T(8,128)(2,1)}), bf16[2048,896]{1,0:T(8,128)(2,1)}) %all-gather.5.cloned.1.call-update) | async-done | bytes 3670032 | tf_op jit(solution)/shard_map/all_gather | solution.py:20
  63.5 52.7 %all-gather.3.cloned.1.call-done = bf16[2048,1024]{1,0:T(8,128)(2,1)} async-done(((bf16[64,1024]{1,0:T(8,128)(2,1)}), bf16[2048,1024]{1,0:T(8,128)(2,1)}) %all-gather.3.cloned.1.call-update) | async-done | bytes 4194320 | tf_op jit(solution)/shard_map/all_gather | solution.py:22
  116.2 8.9 %convolution_add_fusion = f32[1024,896]{1,0:T(8,128)S(1)} fusion(f32[1024,896]{1,0:T(8,128)} %param.8, bf16[2048,1024]{1,0:T(8,128)(2,1)} %all-gather.3.cloned.1.call-done, bf16[2048,896]{1,0:T(8,128)(2,1)} %all-gather.5.cloned.1.call-done), kind=kOutput, calls=%fused_computation.4 | convolution fusion | flops 3759013888 | bytes 15204352 | tf_op jit(solution)/shard_map/dot_general | solution.py:21
  125.2 1.8 copy-done.1
  127.0 4.4 fusion.13
  131.5 114.0 %all-reduce.5.cloned.1.call-done = f32[1024,256]{1,0:T(8,128)} async-done(((f32[1024,256]{1,0:T(8,128)}), f32[1024,256]{1,0:T(8,128)}) %all-reduce.5.cloned.1.call-update) | async-done | bytes 1048592 | tf_op jit(solution)/shard_map/psum | solution.py:28
  245.5 4.1 fusion.14
  249.9 67.7 %all-reduce.7.cloned.1.call-done = f32[256,256]{0,1:T(8,128)} async-done(((f32[256,256]{0,1:T(8,128)}), f32[256,256]{0,1:T(8,128)}) %all-reduce.7.cloned.1.call-update) | async-done | bytes 262160 | tf_op jit(solution)/shard_map/psum | solution.py:29
  317.6 1.1 copy.9
  319.7 11.7 %cholesky.50 = f32[128,128]{1,0:T(8,128)S(1)} custom-call(f32[128,128]{1,0:T(8,128)S(1)} %cholesky.118), custom_call_target="Cholesky" | custom-call | tf_op jit(solution)/shard_map/jit(cholesky)/cholesky | solution.py:30
  331.4 9.8 %custom-call.15 = f32[1,128,128]{1,2,0:T(8,128)S(1)} custom-call(f32[1,128,128]{2,1,0:T(8,128)S(1)} %get-tuple-element.24), custom_call_target="InvertDiagBlocksLowerTriangular" | custom-call | tf_op jit(solution)/shard_map/jit(cholesky)/cholesky | solution.py:30
  341.8 11.7 %cholesky.105 = f32[128,128]{1,0:T(8,128)S(1)} custom-call(f32[128,128]{1,0:T(8,128)S(1)} %convolution_subtract_fusion.1), custom_call_target="Cholesky" | custom-call | tf_op jit(solution)/shard_map/jit(cholesky)/cholesky | solution.py:30
  355.6 4.2 while.1
  356.4 1.4 bitcast_dynamic-update-slice_fusion.2
  358.4 1.4 bitcast_dynamic-update-slice_fusion.2
  359.8 19.7 %custom-call.16 = f32[2,128,128]{1,2,0:T(8,128)S(1)} custom-call(f32[2,128,128]{2,1,0:T(8,128)S(1)} %get-tuple-element.10), custom_call_target="InvertDiagBlocksLowerTriangular" | custom-call | tf_op jit(solution)/shard_map/jit(_solve_triangular)/triangular_solve | solution.py:31
  380.1 1.0 convolution_subtract_fusion
  381.8 6.9 %fusion = f32[896,256]{1,0:T(8,128)} fusion(f32[1024,896]{1,0:T(8,128)S(1)} %copy-done.2, f32[128,1024]{1,0:T(8,128)S(1)} %fusion.5, f32[128,1024]{1,0:T(8,128)S(1)} %fusion.1), kind=kOutput, calls=%fused_computation.9 | convolution fusion | flops 2818834432 | bytes 5636096 | tf_op jit(solution)/shard_map/dot_general | solution.py:32
  388.7 74.1 %all-reduce.9.cloned.1.call-done = f32[896,256]{1,0:T(8,128)} async-done(((f32[896,256]{1,0:T(8,128)}), f32[896,256]{1,0:T(8,128)}) %all-reduce.9.cloned.1.call-update) | async-done | bytes 917520 | tf_op jit(solution)/shard_map/psum | solution.py:33
  462.8 1.3 multiply_reduce_fusion
  464.1 67.1 %psum.31 = f32[256]{0:T(256)S(1)} all-reduce(f32[256]{0:T(256)S(1)} %multiply_reduce_fusion), channel_id=1, replica_groups=mesh['row'=8,'col'=32] {'col'}, use_global_device_ids=true, to_apply=%region_8.9 | all-reduce | flops 256 | bytes 2048 | tf_op jit(solution)/shard_map/psum | solution.py:34
  531.3 1.4 broadcast_divide_fusion
  532.7 9.6 %subtract_convert_fusion = bf16[1024,896]{1,0:T(8,128)(2,1)} fusion(bf16[1024,896]{1,0:T(8,128)(2,1)} %param.7, f32[896,256]{1,0:T(8,128)S(1)} %broadcast_divide_fusion, f32[128,1024]{1,0:T(8,128)S(1)} %fusion.5, f32[128,1024]{1,0:T(8,128)S(1)} %fusion.1), kind=kOutput, calls=%fused_computation.3 | convolution fusion | flops 2822504448 | bytes 5636096 | tf_op jit(solution)/shard_map/dot_general | solution.py:39
  542.3 8.7 %multiply_subtract_fusion = f32[1024,896]{1,0:T(8,128)} fusion(f32[1024,896]{1,0:T(8,128)S(1)} %copy-done.3, f32[896,256]{1,0:T(8,128)S(1)} %copy-done.5, f32[128,1024]{1,0:T(8,128)S(1)} %fusion.5, f32[128,1024]{1,0:T(8,128)S(1)} %fusion.1), kind=kOutput, calls=%fused_computation.2 | convolution fusion | flops 2820669440 | bytes 9306112 | tf_op jit(solution)/shard_map/dot_general | solution.py:35
  (42 shorter events, 6.6 us)
Async XLA Ops:
  7.2 119.8 %copy-start = (f32[896,256]{1,0:T(8,128)S(1)}, f32[896,256]{1,0:T(8,128)}, u32[]{:S(2)}) copy-start(f32[896,256]{1,0:T(8,128)} %param.9) | copy-start | bytes 2752516
  7.2 56.4 %all-gather.5.cloned.1.call-start = ((), (), s32[]{:S(2)}) async-start(), calls=%async_computation.1 | async-start | bytes 4128768 | tf_op jit(solution)/shard_map/all_gather | solution.py:20
  7.9 108.3 %all-gather.3.cloned.1.call-start = ((), (), s32[]{:S(2)}) async-start(), calls=%async_computation | async-start | bytes 4325376 | tf_op jit(solution)/shard_map/all_gather | solution.py:22
  8.7 236.9 %all-reduce.5.cloned.1.call-start = ((), (), s32[]{:S(2)}) async-start(), calls=%async_computation.2 | async-start | bytes 2097152 | tf_op jit(solution)/shard_map/psum | solution.py:28
  125.2 1.8 copy-start.1
  131.4 186.2 %all-reduce.7.cloned.1.call-start = ((), (), s32[]{:S(2)}) async-start(), calls=%async_computation.3 | async-start | bytes 524288 | tf_op jit(solution)/shard_map/psum | solution.py:29
  245.5 133.9 %copy-start.4 = (f32[1024,256]{1,0:T(8,128)S(1)}, f32[1024,256]{1,0:T(8,128)}, u32[]{:S(2)}) copy-start(f32[1024,256]{1,0:T(8,128)} %all-reduce.5.cloned.1.call-done) | copy-start | bytes 3145732
  249.7 213.1 %all-reduce.9.cloned.1.call-start = ((), (), s32[]{:S(2)}) async-start(), calls=%async_computation.4 | async-start | bytes 1835008 | tf_op jit(solution)/shard_map/psum | solution.py:33
  379.4 2.3 copy-start.2
  531.3 11.0 %copy-start.3 = (f32[1024,896]{1,0:T(8,128)S(1)}, f32[1024,896]{1,0:T(8,128)}, u32[]{:S(2)}) copy-start(f32[1024,896]{1,0:T(8,128)} %copy-done.1) | copy-start | bytes 11010052
  531.3 11.0 %copy-start.5 = (f32[896,256]{1,0:T(8,128)S(1)}, f32[896,256]{1,0:T(8,128)}, u32[]{:S(2)}) copy-start(f32[896,256]{1,0:T(8,128)} %all-reduce.9.cloned.1.call-done) | copy-start | bytes 2752516
  532.7 18.4 %copy-start.6 = (f32[896,256]{1,0:T(8,128)}, f32[896,256]{1,0:T(8,128)S(1)}, u32[]{:S(2)}) copy-start(f32[896,256]{1,0:T(8,128)S(1)} %broadcast_divide_fusion) | copy-start | bytes 2752516
Sparse Core Ops, SparseCore 0:
  9.8 53.6 all-gather.4
  66.1 50.0 all-gather.2
  131.5 113.9 all-reduce.4
  249.8 67.7 all-reduce.6
  388.9 73.8 all-reduce.8
where the time goes:
time: 565 us; the launch traced here: 558 us
  waiting for transfers between devices  365 us (65%)
  blocking collectives  67.1 us (12%)
  other arithmetic  57.4 us (10%)
  matrix products  45.5 us (8%)
  between operations  15.7 us (3%)
  local copies, waits for them, and re-layouts  6.96 us (1%)
    psum x1, waiting for transfers between devices, on_device(): proj = lax.psum(jnp.dot(buffer, basis, precision=highest), 'col')  114 us
    psum x1, waiting for transfers between devices, on_device(): back = lax.psum(partial_back, 'row')  74.1 us
    psum x1, waiting for transfers between devices, on_device(): gram = lax.psum(jnp.dot(proj.T, proj, precision=highest), 'row')  67.7 us
    psum x1, blocking collectives, on_device(): norms = lax.psum(jnp.sum(back * back, axis=0), 'col')  67.1 us
    all_gather x1, waiting for transfers between devices, on_device(): grads_all = lax.all_gather(out_grads, 'row', axis=0, tiled=True)  54.8 us
    all_gather x1, waiting for transfers between devices, on_device(): lax.all_gather(acts, 'col', axis=0, tiled=True)  52.7 us
    another operation x6, other arithmetic, on_device(): lower = jnp.linalg.cholesky(gram)  34 us
    another operation x3, other arithmetic, on_device(): ortho = jax.scipy.linalg.solve_triangular(lower, proj.T, lower=True).T  19.7 us
  transfers between devices with their start and end apart: 5, of which 5 were waited for; matrix products, arithmetic and copies ran while one was open for 0% of the time, Pallas kernels for 0%

commit v1 on v0

v1 whole, which is shorter than its diff:
```python
import math

import jax
import jax.numpy as jnp
from jax import lax
from jax.experimental import pallas as pl
from jax.experimental.pallas import tpu as pltpu
from jax.sharding import PartitionSpec as P

D = 8192
FF = 28672
RANK = 256

keep_rate = 0.95
step_rate = 0.01
norm_eps = 1e-06

ROWS = 8
COLS = 32
CHIPS = 16
VMEM_LIMIT = 48 * 1024 * 1024
BLOCK = 32
STEP = 16

UP = [(i, (i + 1) % ROWS) for i in range(ROWS)]
DOWN = [(i, (i - 1) % ROWS) for i in range(ROWS)]
CORE_SWAP = [(i, i ^ 1) for i in range(COLS)]
SAME_CORE = [[2 * i + k for i in range(CHIPS)] for k in range(2)]


def split(x):
    high = x.astype(jnp.bfloat16)
    low = (x - high.astype(jnp.float32)).astype(jnp.bfloat16)
    return high, low


def dot3(a, b, dims):
    a_high, a_low = split(a)
    b_high, b_low = split(b)

    def mul(x, y):
        return lax.dot_general(x, y, (dims, ((), ())), preferred_element_type=jnp.float32)

    return mul(a_high, b_high) + (mul(a_high, b_low) + mul(a_low, b_high))


def spread(x, axis, size, groups=None):
    copies = jnp.broadcast_to(x[None], (size,) + x.shape)
    return lax.all_to_all(copies, axis, 0, 0, axis_index_groups=groups)


def whole(x):
    return pl.BlockSpec(x.shape, lambda *_: (0,) * len(x.shape))


def across(height, width):
    return pl.BlockSpec((height, width), lambda i, *_: (i, 0))


def proj_kernel(place, acts, *refs):
    weights, (local, proj) = refs[:-2], refs[-2:]
    rank = proj.shape[1]
    total = local[...]
    for n, w in enumerate(weights):
        tokens = w.shape[0]
        start = pl.multiple_of(place[n] * tokens, tokens)
        high, low = split(w[...])
        both = lax.dot_general(
            acts[pl.ds(start, tokens), :],
            jnp.concatenate([high, low], axis=1),
            (((0,), (0,)), ((), ())),
            preferred_element_type=jnp.float32,
        )
        total += both[:, :rank] + both[:, rank:]
    proj[...] = total


def proj_part(place, acts, weights, local):
    tokens, rows = acts.shape
    rank = local.shape[1]
    tile = 256
    return pl.pallas_call(
        proj_kernel,
        grid_spec=pltpu.PrefetchScalarGridSpec(
            num_scalar_prefetch=1,
            grid=(rows // tile,),
            in_specs=[pl.BlockSpec((tokens, tile), lambda i, _: (0, i))]
            + [whole(w) for w in weights]
            + [across(tile, rank)],
            out_specs=across(tile, rank),
        ),
        out_shape=jax.ShapeDtypeStruct((rows, rank), jnp.float32),
        compiler_params=pltpu.CompilerParams(vmem_limit_bytes=VMEM_LIMIT),
        cost_estimate=pl.CostEstimate(
            flops=4 * tokens * rows * rank, bytes_accessed=2 * tokens * rows + 16 * rows * rank, transcendentals=0
        ),
        name="proj_part",
    )(place, acts, *weights, local)


def grad_kernel(place, acts, *refs):
    pieces, (momentum, buffer) = refs[:-2], refs[-2:]
    total = momentum[...]
    for n, g in enumerate(pieces):
        tokens = g.shape[0]
        start = pl.multiple_of(place[n] * tokens, tokens)
        total += lax.dot_general(
            acts[pl.ds(start, tokens), :],
            g[...],
            (((0,), (0,)), ((), ())),
            preferred_element_type=jnp.float32,
        )
    buffer[...] = total


def add_grad(place, acts, pieces, momentum):
    rows, cols = momentum.shape
    tokens = acts.shape[0]
    tile = 256
    return pl.pallas_call(
        grad_kernel,
        grid_spec=pltpu.PrefetchScalarGridSpec(
            num_scalar_prefetch=1,
            grid=(rows // tile,),
            in_specs=[pl.BlockSpec((tokens, tile), lambda i, _: (0, i))]
            + [whole(g) for g in pieces]
            + [across(tile, cols)],
            out_specs=across(tile, cols),
        ),
        out_shape=jax.ShapeDtypeStruct((rows, cols), jnp.float32),
        compiler_params=pltpu.CompilerParams(vmem_limit_bytes=VMEM_LIMIT),
        cost_estimate=pl.CostEstimate(
            flops=2 * tokens * rows * cols,
            bytes_accessed=2 * tokens * (rows + cols) + 8 * rows * cols,
            transcendentals=0,
        ),
        name="add_grad",
    )(place, acts, *pieces, momentum)


def factor_kernel(gram, inverse, work):
    n = gram.shape[0]
    lanes = 128
    repeat = n // lanes
    work[...] = gram[...]
    rows = lax.broadcasted_iota(jnp.int32, (BLOCK, lanes), 0)
    row = lax.broadcasted_iota(jnp.int32, (BLOCK, n), 0)
    lane = lax.broadcasted_iota(jnp.int32, (BLOCK, n), 1)
    for first in range(0, n, BLOCK):
        last = first + BLOCK
        part = work[first:last, :]
        pivots = jnp.ones((BLOCK, lanes), jnp.float32)
        for j in range(0, BLOCK, STEP):
            at = first + j
            cols = [jnp.broadcast_to(part[:, at + k : at + k + 1], (BLOCK, lanes)) for k in range(STEP)]
            unit = jnp.where(lane - first == row, 1.0, 0.0)
            part = jnp.where((lane >= at) & (lane < at + STEP), unit, part)
            ratios = []
            for k in range(STEP):
                here = j + k
                pivot = cols[k][here : here + 1, :]
                pivots = jnp.where(rows == here, pivot, pivots)
                ratio = jnp.where(rows > here, cols[k] * (1.0 / pivot), 0.0)
                ratios.append(ratio)
                for m in range(k + 1, STEP):
                    cols[m] = cols[m] - ratio * cols[m][here : here + 1, :]
            for k in range(STEP):
                here = j + k
                part = part - jnp.concatenate([ratios[k]] * repeat, axis=1) * part[here : here + 1, :]
        part = part * jnp.concatenate([lax.rsqrt(pivots)] * repeat, axis=1)
        inverse[first:last, :] = jnp.where(lane < last, part, 0.0)
        if last < n:
            rest = work[last:, :]
            lane_rest = lax.broadcasted_iota(jnp.int32, rest.shape, 1)
            rest = jnp.where((lane_rest >= first) & (lane_rest < last), 0.0, rest)
            work[last:, :] = rest - lax.dot_general(
                part[:, last:],
                part,
                (((0,), (0,)), ((), ())),
                precision=lax.Precision.HIGHEST,
                preferred_element_type=jnp.float32,
            )


def inverse_factor(gram):
    n = gram.shape[0]
    return pl.pallas_call(
        factor_kernel,
        out_shape=jax.ShapeDtypeStruct((n, n), jnp.float32),
        scratch_shapes=[pltpu.VMEM((n, n), jnp.float32)],
        cost_estimate=pl.CostEstimate(flops=10**10, bytes_accessed=8 * n * n, transcendentals=0),
        name="inverse_factor",
    )(gram)


def update_kernel(buffer, weight, ortho, cross, inverse, scale, new_momentum, new_weight, new_basis, back):
    factor = step_rate * math.sqrt(D * FF / RANK)
    last = ((1,), (1,))

    @pl.when(pl.program_id(0) == 0)
    def _():
        height = back.shape[0] // cross.shape[0]
        for n in range(cross.shape[0]):
            span = slice(n * height, (n + 1) * height)
            back[span, :] = dot3(cross[n, :height, :], inverse[...], last)
        new_basis[...] = back[...] * scale[...]

    left = ortho[...]
    right = back[...]
    fix = lax.dot_general(
        left.astype(jnp.bfloat16),
        right.astype(jnp.bfloat16),
        (last, ((), ())),
        preferred_element_type=jnp.float32,
    )
    new_momentum[...] = buffer[...] - (1.0 - keep_rate) * fix
    step = dot3(left * scale[...], right, last)
    new_weight[...] = (weight[...].astype(jnp.float32) - factor * step).astype(jnp.bfloat16)


def update(buffer, weight, ortho, cross, inverse, scale):
    rows, cols = buffer.shape
    rank = ortho.shape[1]
    tile = 256
    return pl.pallas_call(
        update_kernel,
        grid=(rows // tile,),
        in_specs=[
            across(tile, cols),
            across(tile, cols),
            across(tile, rank),
            whole(cross),
            whole(inverse),
            whole(scale),
        ],
        out_specs=[across(tile, cols), across(tile, cols), pl.BlockSpec((cols, rank), lambda i: (0, 0))],
        out_shape=[
            jax.ShapeDtypeStruct((rows, cols), jnp.float32),
            jax.ShapeDtypeStruct((rows, cols), jnp.bfloat16),
            jax.ShapeDtypeStruct((cols, rank), jnp.float32),
        ],
        scratch_shapes=[pltpu.VMEM((cols, rank), jnp.float32)],
        compiler_params=pltpu.CompilerParams(vmem_limit_bytes=VMEM_LIMIT),
        name="update",
    )(buffer, weight, ortho, cross, inverse, scale)


def in_order(core, mine, other, axis):
    first = core == 0
    return jnp.stack([jnp.where(first, mine, other), jnp.where(first, other, mine)], axis=axis)


def on_device(acts, out_grads, weight, momentum, basis):
    high = lax.Precision.HIGH
    highest = lax.Precision.HIGHEST
    row = lax.axis_index("row")
    col = lax.axis_index("col")
    core = col % 2
    rank = basis.shape[1]

    with jax.named_scope("gather_acts"):
        acts_all = lax.all_gather(acts, "col", axis=0, tiled=True)

    with jax.named_scope("gather_grads"):
        pieces, places = [out_grads], [row]
        up = down = out_grads
        for step in range(1, ROWS // 2):
            up = lax.ppermute(up, "row", UP)
            down = lax.ppermute(down, "row", DOWN)
            pieces += [up, down]
            places += [row - step, row + step]
        cut = out_grads.shape[0] // 2
        far_up = lax.ppermute(up[:cut], "row", UP)
        far_down = lax.ppermute(down[cut:], "row", DOWN)
        pieces.append(jnp.concatenate([far_up, far_down], axis=0))
        places.append(row + ROWS // 2)
        place = jnp.stack(places).astype(jnp.int32) % ROWS

    with jax.named_scope("proj"):
        local = jnp.dot(momentum, basis, precision=high)
        weights = [jnp.dot(g.astype(jnp.float32), basis, precision=high) for g in pieces]
        part = proj_part(place, acts_all, weights, local)

    with jax.named_scope("sum_proj"):
        cut = part.shape[0] // 2
        halves = part.reshape(2, cut, rank)
        away = lax.dynamic_index_in_dim(halves, 1 - core, 0, keepdims=False)
        mine = lax.dynamic_index_in_dim(halves, core, 0, keepdims=False)
        mine = mine + lax.ppermute(away, "col", CORE_SWAP)
        shares = mine.reshape(CHIPS, cut // CHIPS, rank)
        shares = lax.all_to_all(shares, "col", 0, 0, axis_index_groups=SAME_CORE)
        buffer = add_grad(place, acts_all, pieces, momentum)
        shares, buffer = lax.optimization_barrier((shares, buffer))
        mine = spread(jnp.sum(shares, axis=0), "col", CHIPS, SAME_CORE).reshape(cut, rank)
        other = lax.ppermute(mine, "col", CORE_SWAP)
        proj = in_order(core, mine, other, 0).reshape(2 * cut, rank)

    with jax.named_scope("cross"):
        cross = lax.dot_general(buffer, proj, (((0,), (0,)), ((), ())), precision=high)
        share = lax.psum_scatter(cross, "row", scatter_dimension=0, tiled=True)

    with jax.named_scope("gram"):
        width = rank // COLS
        slab = lax.dynamic_slice_in_dim(proj, col * width, width, axis=1)
        gram = lax.dot_general(slab, proj, (((0,), (0,)), ((), ())), precision=highest)
        gram = jnp.sum(spread(gram, "row", ROWS), axis=0)
        gram = spread(gram, "col", COLS).reshape(rank, rank)

    inverse = inverse_factor(gram)
    share, inverse = lax.optimization_barrier((share, inverse))
    ortho = lax.dot_general(proj, inverse, (((1,), (1,)), ((), ())), precision=highest)

    with jax.named_scope("gather_cross"):
        filled = jnp.pad(share, ((0, 128 - share.shape[0]), (0, 0)))
        cross_all = lax.all_gather(filled, "row", axis=0)

    with jax.named_scope("norms"):
        back = lax.dot_general(share, inverse, (((1,), (1,)), ((), ())), precision=highest)
        norms = jnp.sum(back * back, axis=0, keepdims=True)
        norms = jnp.sum(spread(norms, ("row", "col"), ROWS * COLS), axis=0)
        scale = 1.0 / jnp.sqrt(norms + norm_eps)

    new_momentum, new_weight, new_basis = update(buffer, weight, ortho, cross_all, inverse, scale)
    return (new_weight, new_momentum, new_basis)


def solution(mesh):
    return jax.shard_map(
        on_device,
        mesh=mesh,
        in_specs=(
            P("col", "row"),
            P("row", "col"),
            P("row", "col"),
            P("row", "col"),
            P("col", None),
        ),
        out_specs=(P("row", "col"), P("row", "col"), P("col", None)),
        check_vma=False,
    )
```

time: 565 us -> 221 us (0.39)
  waiting for transfers between devices: 365 us -> 54.5 us
  other arithmetic: 57.4 us -> 2.39 us
  Pallas kernels: 0 us -> 30.7 us
  starting transfers between devices: 0.37 us -> 29 us
  matrix products: 45.5 us -> 22.7 us
  blocking collectives: 67.1 us -> 45.3 us
  local copies, waits for them, and re-layouts: 6.96 us -> 19.3 us
    psum x3 -> x0, waiting for transfers between devices: 256 us -> none  [the longest x1 114 us: on_device(): proj = lax.psum(jnp.dot(buffer, basis, precision=highest), 'col')]
    all_gather x2, waiting for transfers between devices: 108 us -> 16.8 us  [the longest x1 10.1 us: on_device(): acts_all = lax.all_gather(acts, 'col', axis=0, tiled=True)]
    psum x1 -> x0, blocking collectives: 67.1 us -> none  [on_device(): norms = lax.psum(jnp.sum(back * back, axis=0), 'col')]
    another operation x9 -> x2, other arithmetic: 53.7 us -> 0.14 us  [in_order(): jnp.stack([jnp.where(first, mine, other), jnp.where(first, other, mine)],...]
    all_to_all x0 -> x3, blocking collectives: none -> 45.3 us  [spread(): return lax.all_to_all(copies, axis, 0, 0, axis_index_groups=groups)]
    pallas_call x0 -> x4, Pallas kernels: none -> 30.7 us  [the longest x1 9.46 us: inverse_factor(): pl.pallas_call(factor_kernel, out_shape=jax.ShapeDtypeStruct((n, n), jnp....]
    ppermute x0 -> x10, waiting for transfers between devices: none -> 22 us  [the longest x3 17.3 us: on_device(): up = lax.ppermute(up, 'row', UP)]
    dot_general x6 -> x13, matrix products: 42.7 us -> 22.7 us  [the longest x8 10.3 us: on_device(): jnp.dot(g.astype(jnp.float32), basis, precision=high)]
  transfers between devices with their start and end apart: 5 -> 15, of which waited for: 5 -> 9; matrix products, arithmetic and copies ran while one was open for 0% -> 9% of each run, Pallas kernels for 0% -> 8%
where the time goes in v1:
time: 221 us; the launch traced here: 218 us
  waiting for transfers between devices  54.5 us (25%)
  blocking collectives  45.3 us (20%)
  Pallas kernels  30.7 us (14%)
  starting transfers between devices  29 us (13%)
  matrix products  22.7 us (10%)
  local copies, waits for them, and re-layouts  19.3 us (9%)
  between operations  14 us (6%)
  other arithmetic  2.39 us (1%)
    all_to_all x3, blocking collectives, spread(): return lax.all_to_all(copies, axis, 0, 0, axis_index_groups=groups)  45.3 us
    ppermute x3, waiting for transfers between devices, on_device(): up = lax.ppermute(up, 'row', UP)  17.3 us
    unnamed x53, local copies, waits for them, and re-layouts  15.8 us
    all_to_all x1, waiting for transfers between devices, spread(): return lax.all_to_all(copies, axis, 0, 0, axis_index_groups=groups)  14.9 us
    dot_general x8, matrix products, on_device(): jnp.dot(g.astype(jnp.float32), basis, precision=high)  10.3 us
    all_gather x1, waiting for transfers between devices, on_device(): acts_all = lax.all_gather(acts, 'col', axis=0, tiled=True)  10.1 us
    pallas_call x1, Pallas kernels, inverse_factor(): pl.pallas_call(factor_kernel, out_shape=jax.ShapeDtypeStruct((n, n), jnp....  9.46 us
    ppermute x3, starting transfers between devices, on_device(): down = lax.ppermute(down, 'row', DOWN)  9.42 us
  transfers between devices with their start and end apart: 15, of which 9 were waited for; matrix products, arithmetic and copies ran while one was open for 9% of the time, Pallas kernels for 8%

profile of v1, /device:TPU:1, one launch (start us, length us, event | category | flops | bytes accessed | tf_op | source)
XLA Modules:
  0.0 218.0 jit_solution(12990859288174432592)
XLA Ops:
  7.9 2.5 %collective-permute-start = (bf16[256,896]{1,0:T(8,128)(2,1)}, bf16[256,896]{1,0:T(8,128)(2,1)S(1)}, u32[]{:S(2)}, u32[]{:S(2)}) collective-permute-start(bf16[256,896]{1,0:T(8,128)(2,1)} %refs_0_.1), channel_id=1, source_target_pairs={{0,32},{32,64},{64,96},{96,128},{128,160},{160,192},{192,224},{224... | collective-permute-start | bytes 1376264 | tf_op jit(solution)/shard_map/gather_grads/ppermute | solution.py:268
  10.5 4.0 %collective-permute-start.1 = (bf16[256,896]{1,0:T(8,128)(2,1)}, bf16[256,896]{1,0:T(8,128)(2,1)S(1)}, u32[]{:S(2)}, u32[]{:S(2)}) collective-permute-start(bf16[256,896]{1,0:T(8,128)(2,1)} %refs_0_.1), channel_id=1, source_target_pairs={{0,224},{32,0},{64,32},{96,64},{128,96},{160,128},{192,160},{224,1... | collective-permute-start | bytes 1376264 | tf_op jit(solution)/shard_map/gather_grads/ppermute | solution.py:269
  14.6 2.2 fusion.5.refs_0_
  16.8 3.8 %fusion.13.refs_8_ = f32[1024,256]{1,0:T(8,128)S(1)} fusion(f32[1024,896]{1,0:T(8,128)} %refs_8_.1, f32[896,256]{1,0:T(8,128)S(1)} %copy-done), kind=kOutput, calls=%fused_computation.25 | convolution fusion | flops 1409286144 | bytes 5636096 | tf_op jit(solution)/shard_map/proj/dot_general | solution.py:280
  20.6 4.2 %collective-permute-done.refs_1_ = bf16[256,896]{1,0:T(8,128)(2,1)S(1)} collective-permute-done((bf16[256,896]{1,0:T(8,128)(2,1)}, bf16[256,896]{1,0:T(8,128)(2,1)S(1)}, u32[]{:S(2)}, u32[]{:S(2)}) %collective-permute-start) | collective-permute-done | bytes 458784 | tf_op jit(solution)/shard_map/gather_grads/ppermute | solution.py:268
  24.9 2.7 %collective-permute-start.3 = (bf16[256,896]{1,0:T(8,128)(2,1)S(1)}, bf16[256,896]{1,0:T(8,128)(2,1)S(1)}, u32[]{:S(2)}, u32[]{:S(2)}) collective-permute-start(bf16[256,896]{1,0:T(8,128)(2,1)S(1)} %collective-permute-done.1.refs_2_), channel_id=1, source_target_pairs={{0,224},{32,0},{64,32},{96,64},{128,96},{160,128},{192,160},{224,1... | collective-permute-start | bytes 1376264 | tf_op jit(solution)/shard_map/gather_grads/ppermute | solution.py:269
  29.9 7.0 %collective-permute-done.2.refs_3_ = bf16[256,896]{1,0:T(8,128)(2,1)S(1)} collective-permute-done((bf16[256,896]{1,0:T(8,128)(2,1)S(1)}, bf16[256,896]{1,0:T(8,128)(2,1)S(1)}, u32[]{:S(2)}, u32[]{:S(2)}) %collective-permute-start.2) | collective-permute-done | bytes 458784 | tf_op jit(solution)/shard_map/gather_grads/ppermute | solution.py:268
  36.9 2.7 %collective-permute-start.5 = (bf16[256,896]{1,0:T(8,128)(2,1)S(1)}, bf16[256,896]{1,0:T(8,128)(2,1)S(1)}, u32[]{:S(2)}, u32[]{:S(2)}) collective-permute-start(bf16[256,896]{1,0:T(8,128)(2,1)S(1)} %collective-permute-done.3.refs_4_), channel_id=1, source_target_pairs={{0,224},{32,0},{64,32},{96,64},{128,96},{160,128},{192,160},{224,1... | collective-permute-start | bytes 1376264 | tf_op jit(solution)/shard_map/gather_grads/ppermute | solution.py:269
  41.9 6.0 %collective-permute-done.4.refs_5_ = bf16[256,896]{1,0:T(8,128)(2,1)S(1)} collective-permute-done((bf16[256,896]{1,0:T(8,128)(2,1)S(1)}, bf16[256,896]{1,0:T(8,128)(2,1)S(1)}, u32[]{:S(2)}, u32[]{:S(2)}) %collective-permute-start.4) | collective-permute-done | bytes 458784 | tf_op jit(solution)/shard_map/gather_grads/ppermute | solution.py:268
  48.1 2.9 %collective-permute-start.7 = (bf16[128,896]{1,0:T(8,128)(2,1)S(1)}, bf16[128,896]{1,0:T(8,128)(2,1)S(1)}, u32[]{:S(2)}, u32[]{:S(2)}) collective-permute-start(bf16[128,896]{1,0:T(8,128)(2,1)S(1)} %slice.9), channel_id=1, source_target_pairs={{0,224},{32,0},{64,32},{96,64},{128,96},{160,128},{192,160},{224,1... | collective-permute-start | bytes 688136 | tf_op jit(solution)/shard_map/gather_grads/ppermute | solution.py:274
  55.8 10.1 %all-gather.4.cloned.1.call-done.acts = bf16[2048,1024]{1,0:T(8,128)(2,1)} async-done(((bf16[64,1024]{1,0:T(8,128)(2,1)}), bf16[2048,1024]{1,0:T(8,128)(2,1)}) %all-gather.4.cloned.1.call-update) | async-done | bytes 4194320 | tf_op jit(solution)/shard_map/gather_acts/all_gather | solution.py:262
  73.5 5.4 %proj_part.1 = f32[1024,256]{1,0:T(8,128)S(1)} custom-call(s32[8]{0:T(128)S(1)} %and_select_fusion.place, bf16[2048,1024]{1,0:T(8,128)(2,1)} %all-gather.4.cloned.1.call-done.acts, f32[256,256]{1,0:T(8,128)S(1)} %copy-done.17, f32[256,256]{1,0:T(8,128)S(1)} %copy-done.18, f32[256,256]{1,0:T(8,128)S(1)} %copy-done.19, f32[256,256]{1,0:T(8,128)S(1)} %copy-done.20, ...), custom_call_target="tpu_custom_call" | custom-call | flops 2147483648 | bytes 8388608 | tf_op jit(solution)/shard_map/proj/proj_part/pallas_call | solution.py:82
  80.1 2.0 collective-permute-done.8
  84.0 4.7 %all-to-all-start = ((f32[16,32,256]{2,1,0:T(8,128)}), f32[16,32,256]{2,1,0:T(8,128)S(1)}, u32[]{:S(2)}, u32[]{:S(2)}) async-start(f32[16,32,256]{2,1,0:T(8,128)} %bitcast.58), calls=%async_computation | async-start | bytes 1048576 | tf_op jit(solution)/shard_map/sum_proj/all_to_all | solution.py:291
  93.8 8.9 %add_grad.1.buffer = f32[1024,896]{1,0:T(8,128)} custom-call(s32[8]{0:T(128)S(1)} %and_select_fusion.place, bf16[2048,1024]{1,0:T(8,128)(2,1)} %all-gather.4.cloned.1.call-done.acts, bf16[256,896]{1,0:T(8,128)(2,1)S(1)} %copy-done.6, bf16[256,896]{1,0:T(8,128)(2,1)S(1)} %copy-done.8, bf16[256,896]{1,0:T(8,128)(2,1)S(1)} %copy-done.10, ...), custom_call_target="tpu_custom_call" | custom-call | flops 3758096384 | bytes 15204352 | tf_op jit(solution)/shard_map/sum_proj/add_grad/pallas_call | solution.py:120
  102.8 17.0 %all_to_all.25 = f32[16,32,256]{2,1,0:T(8,128)S(1)} all-to-all(f32[16,32,256]{2,1,0:T(8,128)S(1)} %broadcast_in_dim.8), channel_id=1, replica_groups={{0,2,4,6,8,10,12,14,16,18,20,22,24,26,28,30},{1,3,5,7,9,11,13,15,17,19,..., dimensions={0} | all-to-all | bytes 1048576 | tf_op jit(solution)/shard_map/sum_proj/all_to_all | solution.py:49
  123.8 4.1 %fusion.14 = f32[896,256]{1,0:T(8,128)} fusion(f32[1024,896]{1,0:T(8,128)S(1)} %copy-done.25, f32[1024,256]{1,0:T(8,128)S(1)} %bitcast.54), kind=kOutput, calls=%fused_computation.26 | convolution fusion | flops 1409286144 | bytes 5636096 | tf_op jit(solution)/shard_map/cross/dot_general | solution.py:299
  129.0 14.7 %all_to_all.26 = f32[8,8,256]{2,1,0:T(8,128)S(1)} all-to-all(f32[8,8,256]{2,1,0:T(8,128)S(1)} %broadcast_in_dim.9), channel_id=1, replica_groups=mesh['row'=8,'col'=32] {'row'}, dimensions={0} | all-to-all | bytes 131072 | tf_op jit(solution)/shard_map/gram/all_to_all | solution.py:49
  143.8 13.7 %all_to_all.27 = f32[32,8,256]{2,1,0:T(8,128)} all-to-all(f32[32,8,256]{2,1,0:T(8,128)S(1)} %broadcast_in_dim.10), channel_id=1, replica_groups=mesh['row'=8,'col'=32] {'col'}, dimensions={0} | all-to-all | bytes 524288 | tf_op jit(solution)/shard_map/gram/all_to_all | solution.py:49
  157.5 9.5 %inverse_factor.1.inverse = f32[256,256]{1,0:T(8,128)} custom-call(f32[256,256]{1,0:T(8,128)} %bitcast.59), custom_call_target="tpu_custom_call" | custom-call | flops 10000000000 | bytes 524288 | tf_op jit(solution)/shard_map/inverse_factor/pallas_call | solution.py:187
  170.8 7.0 %all-to-all-start.4 = ((f32[256,1,256]{2,1,0:T(1,128)}), f32[256,1,256]{2,1,0:T(1,128)S(1)}, u32[]{:S(2)}, u32[]{:S(2)}) async-start(f32[256,1,256]{2,1,0:T(1,128)} %broadcast_in_dim.11), calls=%async_computation.5 | async-start | bytes 524288 | tf_op jit(solution)/shard_map/norms/all_to_all | solution.py:49
  179.9 14.9 %all-to-all-done.4 = f32[256,1,256]{2,1,0:T(1,128)S(1)} async-done(((f32[256,1,256]{2,1,0:T(1,128)}), f32[256,1,256]{2,1,0:T(1,128)S(1)}, u32[]{:S(2)}, u32[]{:S(2)}) %all-to-all-start.4) | async-done | bytes 262176 | tf_op jit(solution)/shard_map/norms/all_to_all | solution.py:49
  195.1 6.7 %all-gather.6.cloned.1.call-done = f32[1024,256]{1,0:T(8,128)} async-done(((f32[128,256]{1,0:T(8,128)}), f32[1024,256]{1,0:T(8,128)}) %all-gather.6.cloned.1.call-update) | async-done | bytes 1048592 | tf_op jit(solution)/shard_map/gather_cross/all_gather | solution.py:315
  204.5 6.9 %update.1 = (f32[1024,896]{1,0:T(8,128)}, bf16[1024,896]{1,0:T(8,128)(2,1)}, f32[896,256]{1,0:T(8,128)}) custom-call(f32[1024,896]{1,0:T(8,128)} %add_grad.1.buffer, bf16[1024,896]{1,0:T(8,128)(2,1)S(1)} %copy-done.15, f32[1024,256]{1,0:T(8,128)S(1)} %fusion.15.ortho, f32[8,128,256]{2,1,0:T(8,128)S(1)} %bitcast.52, f32[256,256]{1,0:T(8,128)S(1)} %copy-done.5, ...), custom_call_target="tpu_custom_call" | custom-call | tf_op jit(solution)/shard_map/update/pallas_call | solution.py:225
  (100 shorter events, 40.2 us)
Async XLA Ops:
  7.2 7.4 %copy-start = (f32[896,256]{1,0:T(8,128)S(1)}, f32[896,256]{1,0:T(8,128)}, u32[]{:S(2)}) copy-start(f32[896,256]{1,0:T(8,128)} %param.9) | copy-start | bytes 2752516
  7.2 58.7 %all-gather.4.cloned.1.call-start = ((), (), s32[]{:S(2)}) async-start(), calls=%async_computation.6 | async-start | bytes 4325376 | tf_op jit(solution)/shard_map/gather_acts/all_gather | solution.py:262
  7.9 16.9 %collective-permute-start = (bf16[256,896]{1,0:T(8,128)(2,1)}, bf16[256,896]{1,0:T(8,128)(2,1)S(1)}, u32[]{:S(2)}, u32[]{:S(2)}) collective-permute-start(bf16[256,896]{1,0:T(8,128)(2,1)} %refs_0_.1), channel_id=1, source_target_pairs={{0,32},{32,64},{64,96},{96,128},{128,160},{160,192},{192,224},{224... | collective-permute-start | bytes 1376264 | tf_op jit(solution)/shard_map/gather_grads/ppermute | solution.py:268
  10.5 14.4 %collective-permute-start.1 = (bf16[256,896]{1,0:T(8,128)(2,1)}, bf16[256,896]{1,0:T(8,128)(2,1)S(1)}, u32[]{:S(2)}, u32[]{:S(2)}) collective-permute-start(bf16[256,896]{1,0:T(8,128)(2,1)} %refs_0_.1), channel_id=1, source_target_pairs={{0,224},{32,0},{64,32},{96,64},{128,96},{160,128},{192,160},{224,1... | collective-permute-start | bytes 1376264 | tf_op jit(solution)/shard_map/gather_grads/ppermute | solution.py:269
  24.9 12.0 %copy-start.7 = (bf16[256,896]{1,0:T(8,128)(2,1)}, bf16[256,896]{1,0:T(8,128)(2,1)S(1)}, u32[]{:S(2)}) copy-start(bf16[256,896]{1,0:T(8,128)(2,1)S(1)} %collective-permute-done.refs_1_) | copy-start | bytes 1376260
  24.9 12.0 %collective-permute-start.2 = (bf16[256,896]{1,0:T(8,128)(2,1)S(1)}, bf16[256,896]{1,0:T(8,128)(2,1)S(1)}, u32[]{:S(2)}, u32[]{:S(2)}) collective-permute-start(bf16[256,896]{1,0:T(8,128)(2,1)S(1)} %collective-permute-done.refs_1_), channel_id=1, source_target_pairs={{0,32},{32,64},{64,96},{96,128},{128,160},{160,192},{192,224},{224... | collective-permute-start | bytes 1376264 | tf_op jit(solution)/shard_map/gather_grads/ppermute | solution.py:268
  24.9 23.3 %copy-start.9 = (bf16[256,896]{1,0:T(8,128)(2,1)}, bf16[256,896]{1,0:T(8,128)(2,1)S(1)}, u32[]{:S(2)}) copy-start(bf16[256,896]{1,0:T(8,128)(2,1)S(1)} %collective-permute-done.1.refs_2_) | copy-start | bytes 1376260
  24.9 12.0 %collective-permute-start.3 = (bf16[256,896]{1,0:T(8,128)(2,1)S(1)}, bf16[256,896]{1,0:T(8,128)(2,1)S(1)}, u32[]{:S(2)}, u32[]{:S(2)}) collective-permute-start(bf16[256,896]{1,0:T(8,128)(2,1)S(1)} %collective-permute-done.1.refs_2_), channel_id=1, source_target_pairs={{0,224},{32,0},{64,32},{96,64},{128,96},{160,128},{192,160},{224,1... | collective-permute-start | bytes 1376264 | tf_op jit(solution)/shard_map/gather_grads/ppermute | solution.py:269
  36.9 16.5 %copy-start.11 = (bf16[256,896]{1,0:T(8,128)(2,1)}, bf16[256,896]{1,0:T(8,128)(2,1)S(1)}, u32[]{:S(2)}) copy-start(bf16[256,896]{1,0:T(8,128)(2,1)S(1)} %collective-permute-done.2.refs_3_) | copy-start | bytes 1376260
  36.9 11.1 %collective-permute-start.4 = (bf16[256,896]{1,0:T(8,128)(2,1)S(1)}, bf16[256,896]{1,0:T(8,128)(2,1)S(1)}, u32[]{:S(2)}, u32[]{:S(2)}) collective-permute-start(bf16[256,896]{1,0:T(8,128)(2,1)S(1)} %collective-permute-done.2.refs_3_), channel_id=1, source_target_pairs={{0,32},{32,64},{64,96},{96,128},{128,160},{160,192},{192,224},{224... | collective-permute-start | bytes 1376264 | tf_op jit(solution)/shard_map/gather_grads/ppermute | solution.py:268
  36.9 16.4 %copy-start.13 = (bf16[256,896]{1,0:T(8,128)(2,1)}, bf16[256,896]{1,0:T(8,128)(2,1)S(1)}, u32[]{:S(2)}) copy-start(bf16[256,896]{1,0:T(8,128)(2,1)S(1)} %collective-permute-done.3.refs_4_) | copy-start | bytes 1376260
  36.9 11.2 %collective-permute-start.5 = (bf16[256,896]{1,0:T(8,128)(2,1)S(1)}, bf16[256,896]{1,0:T(8,128)(2,1)S(1)}, u32[]{:S(2)}, u32[]{:S(2)}) collective-permute-start(bf16[256,896]{1,0:T(8,128)(2,1)S(1)} %collective-permute-done.3.refs_4_), channel_id=1, source_target_pairs={{0,224},{32,0},{64,32},{96,64},{128,96},{160,128},{192,160},{224,1... | collective-permute-start | bytes 1376264 | tf_op jit(solution)/shard_map/gather_grads/ppermute | solution.py:269
  48.0 6.6 %collective-permute-start.6 = (bf16[128,896]{1,0:T(8,128)(2,1)S(1)}, bf16[128,896]{1,0:T(8,128)(2,1)S(1)}, u32[]{:S(2)}, u32[]{:S(2)}) collective-permute-start(bf16[128,896]{1,0:T(8,128)(2,1)S(1)} %slice.8), channel_id=1, source_target_pairs={{0,32},{32,64},{64,96},{96,128},{128,160},{160,192},{192,224},{224... | collective-permute-start | bytes 688136 | tf_op jit(solution)/shard_map/gather_grads/ppermute | solution.py:273
  48.1 7.7 %copy-start.1 = (bf16[256,896]{1,0:T(8,128)(2,1)}, bf16[256,896]{1,0:T(8,128)(2,1)S(1)}, u32[]{:S(2)}) copy-start(bf16[256,896]{1,0:T(8,128)(2,1)S(1)} %collective-permute-done.5.refs_6_) | copy-start | bytes 1376260
  48.1 6.4 %collective-permute-start.7 = (bf16[128,896]{1,0:T(8,128)(2,1)S(1)}, bf16[128,896]{1,0:T(8,128)(2,1)S(1)}, u32[]{:S(2)}, u32[]{:S(2)}) collective-permute-start(bf16[128,896]{1,0:T(8,128)(2,1)S(1)} %slice.9), channel_id=1, source_target_pairs={{0,224},{32,0},{64,32},{96,64},{128,96},{160,128},{192,160},{224,1... | collective-permute-start | bytes 688136 | tf_op jit(solution)/shard_map/gather_grads/ppermute | solution.py:274
  79.0 9.7 %copy-start.2 = (bf16[256,896]{1,0:T(8,128)(2,1)S(1)}, bf16[256,896]{1,0:T(8,128)(2,1)}, u32[]{:S(2)}) copy-start(bf16[256,896]{1,0:T(8,128)(2,1)} %copy-done.1) | copy-start | bytes 1376260
  79.0 9.7 %copy-start.4 = (bf16[256,896]{1,0:T(8,128)(2,1)S(1)}, bf16[256,896]{1,0:T(8,128)(2,1)}, u32[]{:S(2)}) copy-start(bf16[256,896]{1,0:T(8,128)(2,1)} %copy-done.3) | copy-start | bytes 1376260
  79.8 2.3 %collective-permute-start.8 = (f32[512,256]{1,0:T(8,128)}, f32[512,256]{1,0:T(8,128)}, u32[]{:S(2)}, u32[]{:S(2)}) collective-permute-start(f32[512,256]{1,0:T(8,128)} %dynamic-slice_bitcast_fusion), channel_id=1, source_target_pairs={{0,1},{1,0},{2,3},{3,2},{4,5},{5,4},{6,7},{7,6},{8,9},{9,8},{10,11... | collective-permute-start | bytes 1572872 | tf_op jit(solution)/shard_map/sum_proj/ppermute | solution.py:289
  84.0 18.7 %all-to-all-start = ((f32[16,32,256]{2,1,0:T(8,128)}), f32[16,32,256]{2,1,0:T(8,128)S(1)}, u32[]{:S(2)}, u32[]{:S(2)}) async-start(f32[16,32,256]{2,1,0:T(8,128)} %bitcast.58), calls=%async_computation | async-start | bytes 1048576 | tf_op jit(solution)/shard_map/sum_proj/all_to_all | solution.py:291
  88.7 78.3 %reduce-scatter.2.cloned.1.call-start = ((), (), s32[]{:S(2)}) async-start(), calls=%async_computation.7 | async-start | bytes 1032192 | tf_op jit(solution)/shard_map/cross/reduce_scatter | solution.py:300
  119.8 3.5 %collective-permute-start.9 = (f32[512,256]{1,0:T(8,128)S(1)}, f32[512,256]{1,0:T(8,128)S(1)}, u32[]{:S(2)}, u32[]{:S(2)}) collective-permute-start(f32[512,256]{1,0:T(8,128)S(1)} %bitcast.57), channel_id=1, source_target_pairs={{0,1},{1,0},{2,3},{3,2},{4,5},{5,4},{6,7},{7,6},{8,9},{9,8},{10,11... | collective-permute-start | bytes 1572872 | tf_op jit(solution)/shard_map/sum_proj/ppermute | solution.py:295
  127.9 73.9 %all-gather.6.cloned.1.call-start = ((), (), s32[]{:S(2)}) async-start(), calls=%async_computation.8 | async-start | bytes 1179648 | tf_op jit(solution)/shard_map/gather_cross/all_gather | solution.py:315
  166.9 34.9 %copy-start.5 = (f32[256,256]{1,0:T(8,128)S(1)}, f32[256,256]{1,0:T(8,128)}, u32[]{:S(2)}) copy-start(f32[256,256]{1,0:T(8,128)} %inverse_factor.1.inverse) | copy-start | bytes 786436
  170.8 23.9 %all-to-all-start.4 = ((f32[256,1,256]{2,1,0:T(1,128)}), f32[256,1,256]{2,1,0:T(1,128)S(1)}, u32[]{:S(2)}, u32[]{:S(2)}) async-start(f32[256,1,256]{2,1,0:T(1,128)} %broadcast_in_dim.11), calls=%async_computation.5 | async-start | bytes 524288 | tf_op jit(solution)/shard_map/norms/all_to_all | solution.py:49
  (17 other events, 18.7 us)
Sparse Core Ops, SparseCore 0:
  10.6 55.2 all-gather.3
  128.0 32.3 reduce-scatter.1
  168.7 33.0 all-gather.5

commit v2 on v1

--- a/solution.py
+++ b/solution.py
@@ -26,6 +26,8 @@
 DOWN = [(i, (i - 1) % ROWS) for i in range(ROWS)]
 CORE_SWAP = [(i, i ^ 1) for i in range(COLS)]
 SAME_CORE = [[2 * i + k for i in range(CHIPS)] for k in range(2)]
+GROUPS = COLS // ROWS
+MIXERS = [[GROUPS * i + k for i in range(ROWS)] for k in range(GROUPS)]
 
 
 def split(x):
@@ -55,47 +57,6 @@
 
 def across(height, width):
     return pl.BlockSpec((height, width), lambda i, *_: (i, 0))
-
-
-def proj_kernel(place, acts, *refs):
-    weights, (local, proj) = refs[:-2], refs[-2:]
-    rank = proj.shape[1]
-    total = local[...]
-    for n, w in enumerate(weights):
-        tokens = w.shape[0]
-        start = pl.multiple_of(place[n] * tokens, tokens)
-        high, low = split(w[...])
-        both = lax.dot_general(
-            acts[pl.ds(start, tokens), :],
-            jnp.concatenate([high, low], axis=1),
-            (((0,), (0,)), ((), ())),
-            preferred_element_type=jnp.float32,
-        )
-        total += both[:, :rank] + both[:, rank:]
-    proj[...] = total
-
-
-def proj_part(place, acts, weights, local):
-    tokens, rows = acts.shape
-    rank = local.shape[1]
-    tile = 256
-    return pl.pallas_call(
-        proj_kernel,
-        grid_spec=pltpu.PrefetchScalarGridSpec(
-            num_scalar_prefetch=1,
-            grid=(rows // tile,),
-            in_specs=[pl.BlockSpec((tokens, tile), lambda i, _: (0, i))]
-            + [whole(w) for w in weights]
-            + [across(tile, rank)],
-            out_specs=across(tile, rank),
-        ),
-        out_shape=jax.ShapeDtypeStruct((rows, rank), jnp.float32),
-        compiler_params=pltpu.CompilerParams(vmem_limit_bytes=VMEM_LIMIT),
-        cost_estimate=pl.CostEstimate(
-            flops=4 * tokens * rows * rank, bytes_accessed=2 * tokens * rows + 16 * rows * rank, transcendentals=0
-        ),
-        name="proj_part",
-    )(place, acts, *weights, local)
 
 
 def grad_kernel(place, acts, *refs):
@@ -261,25 +222,40 @@
     with jax.named_scope("gather_acts"):
         acts_all = lax.all_gather(acts, "col", axis=0, tiled=True)
 
-    with jax.named_scope("gather_grads"):
-        pieces, places = [out_grads], [row]
-        up = down = out_grads
-        for step in range(1, ROWS // 2):
+    pieces, places = [out_grads], [row]
+    up = down = out_grads
+
+    def turn(step, *others):
+        nonlocal up, down
+        with jax.named_scope("gather_grads"):
             up = lax.ppermute(up, "row", UP)
             down = lax.ppermute(down, "row", DOWN)
-            pieces += [up, down]
-            places += [row - step, row + step]
+            pieces.extend([up, down])
+            places.extend([row - step, row + step])
+            up, down, *others = lax.optimization_barrier((up, down, *others))
+            return others
+
+    with jax.named_scope("proj"):
+        small = jnp.dot(out_grads.astype(jnp.float32), basis, precision=high)
+        small = small.reshape(GROUPS, ROWS, -1, rank).swapaxes(0, 1).reshape(COLS, -1, rank)
+        small = jnp.sum(lax.all_to_all(small, "col", 0, 0), axis=0)
+        mixed = acts.reshape(ROWS, -1, acts.shape[1])
+        small, mixed = turn(1, small, mixed)
+        mixed = lax.all_to_all(mixed, "col", 0, 0, axis_index_groups=MIXERS)
+        small, mixed = turn(2, small, mixed)
+        local = jnp.dot(momentum, basis, precision=high)
+        small = spread(small, "row", ROWS).reshape(-1, rank)
+        mixed = mixed.reshape(-1, acts.shape[1]).astype(jnp.float32)
+        part = local + lax.dot_general(mixed, small, (((0,), (0,)), ((), ())), precision=high)
+        (part,) = turn(3, part)
+
+    with jax.named_scope("gather_grads"):
         cut = out_grads.shape[0] // 2
         far_up = lax.ppermute(up[:cut], "row", UP)
         far_down = lax.ppermute(down[cut:], "row", DOWN)
         pieces.append(jnp.concatenate([far_up, far_down], axis=0))
         places.append(row + ROWS // 2)
         place = jnp.stack(places).astype(jnp.int32) % ROWS
-
-    with jax.named_scope("proj"):
-        local = jnp.dot(momentum, basis, precision=high)
-        weights = [jnp.dot(g.astype(jnp.float32), basis, precision=high) for g in pieces]
-        part = proj_part(place, acts_all, weights, local)
 
     with jax.named_scope("sum_proj"):
         cut = part.shape[0] // 2

time: 221 us -> 208 us (0.941)
  blocking collectives: 45.3 us -> 70 us
  waiting for transfers between devices: 54.5 us -> 30.4 us
  local copies, waits for them, and re-layouts: 19.3 us -> 9.63 us
  matrix products: 22.7 us -> 16.7 us
  Pallas kernels: 30.7 us -> 25.5 us
  starting transfers between devices: 29 us -> 33.8 us
    all_to_all x0 -> x2, blocking collectives: none -> 27.1 us  [the longest x1 16.7 us: on_device(): small = jnp.sum(lax.all_to_all(small, 'col', 0, 0), axis=0)]
    ppermute x6, waiting for transfers between devices: 17.3 us -> 4.28 us  [the longest x3 4.27 us: turn(): up = lax.ppermute(up, 'row', UP)]
    unnamed x53 -> x18, local copies, waits for them, and re-layouts: 15.8 us -> 4.11 us
    all_gather x1, waiting for transfers between devices: 10.1 us -> 0.02 us  [on_device(): acts_all = lax.all_gather(acts, 'col', axis=0, tiled=True)]
    dot_general x8 -> x2, matrix products: 10.3 us -> 3.23 us  [the longest x1 1.71 us: on_device(): lax.dot_general(mixed, small, (((0,), (0,)), ((), ())), precision=high)]
    pallas_call x1 -> x0, Pallas kernels: 5.44 us -> none  [proj_part(): pl.pallas_call(proj_kernel, grid_spec=pltpu.PrefetchScalarGridSpec(num_sc...]
    all_to_all x1 -> x2, starting transfers between devices: 7.05 us -> 10.9 us  [spread(): return lax.all_to_all(copies, axis, 0, 0, axis_index_groups=groups)]
    all_to_all x3, blocking collectives: 45.3 us -> 43 us  [spread(): return lax.all_to_all(copies, axis, 0, 0, axis_index_groups=groups)]
  transfers between devices with their start and end apart: 15 -> 16, of which waited for: 9 -> 6; matrix products, arithmetic and copies ran while one was open for 9% -> 10% of each run, Pallas kernels for 8% -> 9%
where the time goes in v2:
time: 208 us; the launch traced here: 204 us
  blocking collectives  70 us (34%)
  starting transfers between devices  33.8 us (16%)
  waiting for transfers between devices  30.4 us (15%)
  Pallas kernels  25.5 us (12%)
  matrix products  16.7 us (8%)
  between operations  14 us (7%)
  local copies, waits for them, and re-layouts  9.63 us (5%)
  other arithmetic  4.46 us (2%)
    all_to_all x3, blocking collectives, spread(): return lax.all_to_all(copies, axis, 0, 0, axis_index_groups=groups)  43 us
    all_to_all x1, blocking collectives, on_device(): small = jnp.sum(lax.all_to_all(small, 'col', 0, 0), axis=0)  16.7 us
    all_to_all x2, waiting for transfers between devices, spread(): return lax.all_to_all(copies, axis, 0, 0, axis_index_groups=groups)  14.9 us
    all_to_all x2, starting transfers between devices, spread(): return lax.all_to_all(copies, axis, 0, 0, axis_index_groups=groups)  10.9 us
    ppermute x3, starting transfers between devices, turn(): down = lax.ppermute(down, 'row', DOWN)  10.7 us
    all_to_all x1, blocking collectives, on_device(): mixed = lax.all_to_all(mixed, 'col', 0, 0, axis_index_groups=MIXERS)  10.3 us
    pallas_call x1, Pallas kernels, inverse_factor(): pl.pallas_call(factor_kernel, out_shape=jax.ShapeDtypeStruct((n, n), jnp....  9.46 us
    pallas_call x1, Pallas kernels, add_grad(): pl.pallas_call(grad_kernel, grid_spec=pltpu.PrefetchScalarGridSpec(num_sc...  9.14 us
  transfers between devices with their start and end apart: 16, of which 6 were waited for; matrix products, arithmetic and copies ran while one was open for 10% of the time, Pallas kernels for 9%

profile of v2, /device:TPU:1, one launch (start us, length us, event | category | flops | bytes accessed | tf_op | source)
XLA Modules:
  0.0 204.5 jit_solution(2917094672977247033)
XLA Ops:
  7.9 6.5 %collective-permute-start.1 = (bf16[256,896]{1,0:T(8,128)(2,1)}, bf16[256,896]{1,0:T(8,128)(2,1)S(1)}, u32[]{:S(2)}, u32[]{:S(2)}) collective-permute-start(bf16[256,896]{1,0:T(8,128)(2,1)} %refs_0_.1), channel_id=1, source_target_pairs={{0,224},{32,0},{64,32},{96,64},{128,96},{160,128},{192,160},{224,1... | collective-permute-start | bytes 1376264 | tf_op jit(solution)/shard_map/proj/gather_grads/ppermute | solution.py:232
  16.0 16.7 %all_to_all.40 = f32[32,8,256]{2,1,0:T(8,128)S(1)} all-to-all(f32[32,8,256]{2,1,0:T(8,128)S(1)} %bitcast.54), channel_id=1, replica_groups=mesh['row'=8,'col'=32] {'col'}, dimensions={0} | all-to-all | bytes 524288 | tf_op jit(solution)/shard_map/proj/all_to_all | solution.py:241
  32.9 3.0 %collective-permute-start.3 = (bf16[256,896]{1,0:T(8,128)(2,1)S(1)}, bf16[256,896]{1,0:T(8,128)(2,1)}, u32[]{:S(2)}, u32[]{:S(2)}) collective-permute-start(bf16[256,896]{1,0:T(8,128)(2,1)S(1)} %collective-permute-done.1.refs_2_), channel_id=1, source_target_pairs={{0,224},{32,0},{64,32},{96,64},{128,96},{160,128},{192,160},{224,1... | collective-permute-start | bytes 1376264 | tf_op jit(solution)/shard_map/proj/gather_grads/ppermute | solution.py:232
  35.9 10.3 %all_to_all.41 = bf16[8,8,1024]{2,1,0:T(8,128)(2,1)S(1)} all-to-all(bf16[8,8,1024]{2,1,0:T(8,128)(2,1)} %bitcast.57), channel_id=1, replica_groups={{0,4,8,12,16,20,24,28},{1,5,9,13,17,21,25,29},{2,6,10,14,18,22,26,30},{..., dimensions={0} | all-to-all | bytes 262144 | tf_op jit(solution)/shard_map/proj/all_to_all | solution.py:244
  47.2 3.8 %all-to-all-start.2 = ((f32[8,8,256]{2,1,0:T(8,128)}), f32[8,8,256]{2,1,0:T(8,128)S(1)}, u32[]{:S(2)}, u32[]{:S(2)}) async-start(f32[8,8,256]{2,1,0:T(8,128)} %broadcast_in_dim.10), calls=%async_computation.2 | async-start | bytes 131072 | tf_op jit(solution)/shard_map/proj/all_to_all | solution.py:51
  53.7 4.9 %fusion.7 = f32[1024,256]{1,0:T(8,128)} fusion(f32[1024,896]{1,0:T(8,128)} %refs_8_.1, f32[896,256]{1,0:T(8,128)S(1)} %copy-done), kind=kOutput, calls=%fused_computation.19 | convolution fusion | flops 1409286144 | bytes 5636096 | tf_op jit(solution)/shard_map/proj/dot_general | solution.py:246
  60.4 3.9 %collective-permute-done.4.refs_5_ = bf16[256,896]{1,0:T(8,128)(2,1)S(1)} collective-permute-done((bf16[256,896]{1,0:T(8,128)(2,1)}, bf16[256,896]{1,0:T(8,128)(2,1)S(1)}, u32[]{:S(2)}, u32[]{:S(2)}) %collective-permute-start.4) | collective-permute-done | bytes 458784 | tf_op jit(solution)/shard_map/proj/gather_grads/ppermute | solution.py:231
  65.1 2.5 %collective-permute-start.6 = (f32[512,256]{1,0:T(8,128)}, f32[512,256]{1,0:T(8,128)S(1)}, u32[]{:S(2)}, u32[]{:S(2)}) collective-permute-start(f32[512,256]{1,0:T(8,128)} %dynamic-slice_bitcast_fusion), channel_id=1, source_target_pairs={{0,1},{1,0},{2,3},{3,2},{4,5},{5,4},{6,7},{7,6},{8,9},{9,8},{10,11... | collective-permute-start | bytes 1572872 | tf_op jit(solution)/shard_map/sum_proj/ppermute | solution.py:265
  69.1 1.8 collective-permute-start.8
  71.0 1.9 bitcast_add_fusion
  72.9 4.2 %all-to-all-start.3 = ((f32[16,32,256]{2,1,0:T(8,128)}), f32[16,32,256]{2,1,0:T(8,128)}, u32[]{:S(2)}, u32[]{:S(2)}) async-start(f32[16,32,256]{2,1,0:T(8,128)} %bitcast.8), calls=%async_computation.3 | async-start | bytes 1048576 | tf_op jit(solution)/shard_map/sum_proj/all_to_all | solution.py:267
  77.2 2.2 %collective-permute-done.7 = bf16[128,896]{1,0:T(8,128)(2,1)} collective-permute-done((bf16[128,896]{1,0:T(8,128)(2,1)}, bf16[128,896]{1,0:T(8,128)(2,1)}, u32[]{:S(2)}, u32[]{:S(2)}) %collective-permute-start.7) | collective-permute-done | bytes 229408 | tf_op jit(solution)/shard_map/gather_grads/ppermute | solution.py:254
  81.4 9.1 %add_grad.1.buffer = f32[1024,896]{1,0:T(8,128)} custom-call(s32[8]{0:T(128)S(1)} %and_select_fusion.place, bf16[2048,1024]{1,0:T(8,128)(2,1)} %all-gather.4.cloned.1.call-done.acts, bf16[256,896]{1,0:T(8,128)(2,1)S(1)} %copy-done.2, bf16[256,896]{1,0:T(8,128)(2,1)S(1)} %copy-done.6, bf16[256,896]{1,0:T(8,128)(2,1)S(1)} %collective-permute-done.1.refs_2_, ...), custom_call_target="tpu_custom_call" | custom-call | flops 3758096384 | bytes 15204352 | tf_op jit(solution)/shard_map/sum_proj/add_grad/pallas_call | solution.py:81
  91.7 14.6 %all_to_all.42 = f32[16,32,256]{2,1,0:T(8,128)S(1)} all-to-all(f32[16,32,256]{2,1,0:T(8,128)S(1)} %broadcast_in_dim.11), channel_id=1, replica_groups={{0,2,4,6,8,10,12,14,16,18,20,22,24,26,28,30},{1,3,5,7,9,11,13,15,17,19,..., dimensions={0} | all-to-all | bytes 1048576 | tf_op jit(solution)/shard_map/sum_proj/all_to_all | solution.py:51
  106.3 2.0 collective-permute-start.9
  110.4 4.1 %fusion.8 = f32[896,256]{1,0:T(8,128)} fusion(f32[1024,896]{1,0:T(8,128)S(1)} %copy-done.7, f32[1024,256]{1,0:T(8,128)S(1)} %bitcast.49), kind=kOutput, calls=%fused_computation.20 | convolution fusion | flops 1409286144 | bytes 5636096 | tf_op jit(solution)/shard_map/cross/dot_general | solution.py:275
  115.6 14.7 %all_to_all.43 = f32[8,8,256]{2,1,0:T(8,128)S(1)} all-to-all(f32[8,8,256]{2,1,0:T(8,128)S(1)} %broadcast_in_dim.12), channel_id=1, replica_groups=mesh['row'=8,'col'=32] {'row'}, dimensions={0} | all-to-all | bytes 131072 | tf_op jit(solution)/shard_map/gram/all_to_all | solution.py:51
  130.3 13.7 %all_to_all.44 = f32[32,8,256]{2,1,0:T(8,128)} all-to-all(f32[32,8,256]{2,1,0:T(8,128)S(1)} %broadcast_in_dim.13), channel_id=1, replica_groups=mesh['row'=8,'col'=32] {'col'}, dimensions={0} | all-to-all | bytes 524288 | tf_op jit(solution)/shard_map/gram/all_to_all | solution.py:51
  144.0 9.5 %inverse_factor.1.inverse = f32[256,256]{1,0:T(8,128)} custom-call(f32[256,256]{1,0:T(8,128)} %bitcast.58), custom_call_target="tpu_custom_call" | custom-call | flops 10000000000 | bytes 524288 | tf_op jit(solution)/shard_map/inverse_factor/pallas_call | solution.py:148
  157.4 7.0 %all-to-all-start.7 = ((f32[256,1,256]{2,1,0:T(1,128)}), f32[256,1,256]{2,1,0:T(1,128)S(1)}, u32[]{:S(2)}, u32[]{:S(2)}) async-start(f32[256,1,256]{2,1,0:T(1,128)} %broadcast_in_dim.14), calls=%async_computation.8 | async-start | bytes 524288 | tf_op jit(solution)/shard_map/norms/all_to_all | solution.py:51
  164.4 2.0 fusion.9.ortho
  166.4 14.9 %all-to-all-done.7 = f32[256,1,256]{2,1,0:T(1,128)S(1)} async-done(((f32[256,1,256]{2,1,0:T(1,128)}), f32[256,1,256]{2,1,0:T(1,128)S(1)}, u32[]{:S(2)}, u32[]{:S(2)}) %all-to-all-start.7) | async-done | bytes 262176 | tf_op jit(solution)/shard_map/norms/all_to_all | solution.py:51
  181.6 6.7 %all-gather.6.cloned.1.call-done = f32[1024,256]{1,0:T(8,128)} async-done(((f32[128,256]{1,0:T(8,128)}), f32[1024,256]{1,0:T(8,128)}) %all-gather.6.cloned.1.call-update) | async-done | bytes 1048592 | tf_op jit(solution)/shard_map/gather_cross/all_gather | solution.py:291
  191.1 6.9 %update.1 = (f32[1024,896]{1,0:T(8,128)}, bf16[1024,896]{1,0:T(8,128)(2,1)}, f32[896,256]{1,0:T(8,128)}) custom-call(f32[1024,896]{1,0:T(8,128)} %add_grad.1.buffer, bf16[1024,896]{1,0:T(8,128)(2,1)S(1)} %copy-done.3, f32[1024,256]{1,0:T(8,128)S(1)} %fusion.9.ortho, f32[8,128,256]{2,1,0:T(8,128)S(1)} %bitcast.47, f32[256,256]{1,0:T(8,128)S(1)} %copy-done.1, ...), custom_call_target="tpu_custom_call" | custom-call | tf_op jit(solution)/shard_map/update/pallas_call | solution.py:186
  (65 shorter events, 23.5 us)
Async XLA Ops:
  7.2 7.2 %copy-start = (f32[896,256]{1,0:T(8,128)S(1)}, f32[896,256]{1,0:T(8,128)}, u32[]{:S(2)}) copy-start(f32[896,256]{1,0:T(8,128)} %param.9) | copy-start | bytes 2752516
  7.2 73.2 %all-gather.4.cloned.1.call-start = ((), (), s32[]{:S(2)}) async-start(), calls=%async_computation.9 | async-start | bytes 4325376 | tf_op jit(solution)/shard_map/gather_acts/all_gather | solution.py:223
  7.9 24.8 %collective-permute-start.1 = (bf16[256,896]{1,0:T(8,128)(2,1)}, bf16[256,896]{1,0:T(8,128)(2,1)S(1)}, u32[]{:S(2)}, u32[]{:S(2)}) collective-permute-start(bf16[256,896]{1,0:T(8,128)(2,1)} %refs_0_.1), channel_id=1, source_target_pairs={{0,224},{32,0},{64,32},{96,64},{128,96},{160,128},{192,160},{224,1... | collective-permute-start | bytes 1376264 | tf_op jit(solution)/shard_map/proj/gather_grads/ppermute | solution.py:232
  14.4 18.4 %collective-permute-start = (bf16[256,896]{1,0:T(8,128)(2,1)}, bf16[256,896]{1,0:T(8,128)(2,1)S(1)}, u32[]{:S(2)}, u32[]{:S(2)}) collective-permute-start(bf16[256,896]{1,0:T(8,128)(2,1)} %refs_0_.1), channel_id=1, source_target_pairs={{0,32},{32,64},{64,96},{96,128},{128,160},{160,192},{192,224},{224... | collective-permute-start | bytes 1376264 | tf_op jit(solution)/shard_map/proj/gather_grads/ppermute | solution.py:231
  32.8 27.6 %copy-start.5 = (bf16[256,896]{1,0:T(8,128)(2,1)}, bf16[256,896]{1,0:T(8,128)(2,1)S(1)}, u32[]{:S(2)}) copy-start(bf16[256,896]{1,0:T(8,128)(2,1)S(1)} %collective-permute-done.refs_1_) | copy-start | bytes 1376260
  32.8 13.8 %collective-permute-start.2 = (bf16[256,896]{1,0:T(8,128)(2,1)S(1)}, bf16[256,896]{1,0:T(8,128)(2,1)}, u32[]{:S(2)}, u32[]{:S(2)}) collective-permute-start(bf16[256,896]{1,0:T(8,128)(2,1)S(1)} %collective-permute-done.refs_1_), channel_id=1, source_target_pairs={{0,32},{32,64},{64,96},{96,128},{128,160},{160,192},{192,224},{224... | collective-permute-start | bytes 1376264 | tf_op jit(solution)/shard_map/proj/gather_grads/ppermute | solution.py:231
  32.9 13.7 %collective-permute-start.3 = (bf16[256,896]{1,0:T(8,128)(2,1)S(1)}, bf16[256,896]{1,0:T(8,128)(2,1)}, u32[]{:S(2)}, u32[]{:S(2)}) collective-permute-start(bf16[256,896]{1,0:T(8,128)(2,1)S(1)} %collective-permute-done.1.refs_2_), channel_id=1, source_target_pairs={{0,224},{32,0},{64,32},{96,64},{128,96},{160,128},{192,160},{224,1... | collective-permute-start | bytes 1376264 | tf_op jit(solution)/shard_map/proj/gather_grads/ppermute | solution.py:232
  47.2 11.4 %all-to-all-start.2 = ((f32[8,8,256]{2,1,0:T(8,128)}), f32[8,8,256]{2,1,0:T(8,128)S(1)}, u32[]{:S(2)}, u32[]{:S(2)}) async-start(f32[8,8,256]{2,1,0:T(8,128)} %broadcast_in_dim.10), calls=%async_computation.2 | async-start | bytes 131072 | tf_op jit(solution)/shard_map/proj/all_to_all | solution.py:51
  51.0 13.3 %collective-permute-start.4 = (bf16[256,896]{1,0:T(8,128)(2,1)}, bf16[256,896]{1,0:T(8,128)(2,1)S(1)}, u32[]{:S(2)}, u32[]{:S(2)}) collective-permute-start(bf16[256,896]{1,0:T(8,128)(2,1)} %collective-permute-done.2.refs_3_), channel_id=1, source_target_pairs={{0,32},{32,64},{64,96},{96,128},{128,160},{160,192},{192,224},{224... | collective-permute-start | bytes 1376264 | tf_op jit(solution)/shard_map/proj/gather_grads/ppermute | solution.py:231
  52.5 11.8 %collective-permute-start.5 = (bf16[256,896]{1,0:T(8,128)(2,1)}, bf16[256,896]{1,0:T(8,128)(2,1)S(1)}, u32[]{:S(2)}, u32[]{:S(2)}) collective-permute-start(bf16[256,896]{1,0:T(8,128)(2,1)} %collective-permute-done.3.refs_4_), channel_id=1, source_target_pairs={{0,224},{32,0},{64,32},{96,64},{128,96},{160,128},{192,160},{224,1... | collective-permute-start | bytes 1376264 | tf_op jit(solution)/shard_map/proj/gather_grads/ppermute | solution.py:232
  60.4 3.9 %copy-start.8 = (f32[1024,256]{1,0:T(8,128)}, f32[1024,256]{1,0:T(8,128)S(1)}, u32[]{:S(2)}) copy-start(f32[1024,256]{1,0:T(8,128)S(1)} %fusion) | copy-start | bytes 3145732
  60.4 20.0 %copy-start.2 = (bf16[256,896]{1,0:T(8,128)(2,1)S(1)}, bf16[256,896]{1,0:T(8,128)(2,1)}, u32[]{:S(2)}) copy-start(bf16[256,896]{1,0:T(8,128)(2,1)} %refs_0_.1) | copy-start | bytes 1376260
  65.1 5.9 %collective-permute-start.6 = (f32[512,256]{1,0:T(8,128)}, f32[512,256]{1,0:T(8,128)S(1)}, u32[]{:S(2)}, u32[]{:S(2)}) collective-permute-start(f32[512,256]{1,0:T(8,128)} %dynamic-slice_bitcast_fusion), channel_id=1, source_target_pairs={{0,1},{1,0},{2,3},{3,2},{4,5},{5,4},{6,7},{7,6},{8,9},{9,8},{10,11... | collective-permute-start | bytes 1572872 | tf_op jit(solution)/shard_map/sum_proj/ppermute | solution.py:265
  69.1 8.1 %collective-permute-start.8 = (bf16[128,896]{1,0:T(8,128)(2,1)}, bf16[128,896]{1,0:T(8,128)(2,1)S(1)}, u32[]{:S(2)}, u32[]{:S(2)}) collective-permute-start(bf16[128,896]{1,0:T(8,128)(2,1)} %slice.7), channel_id=1, source_target_pairs={{0,224},{32,0},{64,32},{96,64},{128,96},{160,128},{192,160},{224,1... | collective-permute-start | bytes 688136 | tf_op jit(solution)/shard_map/gather_grads/ppermute | solution.py:255
  71.0 8.4 %collective-permute-start.7 = (bf16[128,896]{1,0:T(8,128)(2,1)}, bf16[128,896]{1,0:T(8,128)(2,1)}, u32[]{:S(2)}, u32[]{:S(2)}) collective-permute-start(bf16[128,896]{1,0:T(8,128)(2,1)} %slice.6), channel_id=1, source_target_pairs={{0,32},{32,64},{64,96},{96,128},{128,160},{160,192},{192,224},{224... | collective-permute-start | bytes 688136 | tf_op jit(solution)/shard_map/gather_grads/ppermute | solution.py:254
  72.9 17.7 %all-to-all-start.3 = ((f32[16,32,256]{2,1,0:T(8,128)}), f32[16,32,256]{2,1,0:T(8,128)}, u32[]{:S(2)}, u32[]{:S(2)}) async-start(f32[16,32,256]{2,1,0:T(8,128)} %bitcast.8), calls=%async_computation.3 | async-start | bytes 1048576 | tf_op jit(solution)/shard_map/sum_proj/all_to_all | solution.py:267
  77.1 76.4 %reduce-scatter.2.cloned.1.call-start = ((), (), s32[]{:S(2)}) async-start(), calls=%async_computation.10 | async-start | bytes 1032192 | tf_op jit(solution)/shard_map/cross/reduce_scatter | solution.py:276
  106.3 3.5 %collective-permute-start.9 = (f32[512,256]{1,0:T(8,128)S(1)}, f32[512,256]{1,0:T(8,128)S(1)}, u32[]{:S(2)}, u32[]{:S(2)}) collective-permute-start(f32[512,256]{1,0:T(8,128)S(1)} %bitcast.52), channel_id=1, source_target_pairs={{0,1},{1,0},{2,3},{3,2},{4,5},{5,4},{6,7},{7,6},{8,9},{9,8},{10,11... | collective-permute-start | bytes 1572872 | tf_op jit(solution)/shard_map/sum_proj/ppermute | solution.py:271
  108.3 2.0 copy-start.7
  114.5 73.9 %all-gather.6.cloned.1.call-start = ((), (), s32[]{:S(2)}) async-start(), calls=%async_computation.11 | async-start | bytes 1179648 | tf_op jit(solution)/shard_map/gather_cross/all_gather | solution.py:291
  153.5 34.9 %copy-start.1 = (f32[256,256]{1,0:T(8,128)S(1)}, f32[256,256]{1,0:T(8,128)}, u32[]{:S(2)}) copy-start(f32[256,256]{1,0:T(8,128)} %inverse_factor.1.inverse) | copy-start | bytes 786436
  157.4 23.9 %all-to-all-start.7 = ((f32[256,1,256]{2,1,0:T(1,128)}), f32[256,1,256]{2,1,0:T(1,128)S(1)}, u32[]{:S(2)}, u32[]{:S(2)}) async-start(f32[256,1,256]{2,1,0:T(1,128)} %broadcast_in_dim.14), calls=%async_computation.8 | async-start | bytes 524288 | tf_op jit(solution)/shard_map/norms/all_to_all | solution.py:51
  188.3 1.5 copy-start.3
  189.8 1.2 copy-start.4
  (1 other events, 1.0 us)
Sparse Core Ops, SparseCore 0:
  10.6 55.2 all-gather.3
  114.6 32.3 reduce-scatter.1
  155.2 33.0 all-gather.5

commit v3 on v2

v3 whole, which is shorter than its diff:
```python
import math

import jax
import jax.numpy as jnp
from jax import lax
from jax.experimental import pallas as pl
from jax.experimental.pallas import tpu as pltpu
from jax.sharding import PartitionSpec as P

D = 8192
FF = 28672
RANK = 256

keep_rate = 0.95
step_rate = 0.01
norm_eps = 1e-06

ROWS = 8
COLS = 32
CHIPS = 16
VMEM_LIMIT = 24 * 1024 * 1024
VMEM_MOST = 60 * 1024 * 1024
BLOCK = 64
STEP = 16
TILES = 4

UP = [(i, (i + 1) % ROWS) for i in range(ROWS)]
DOWN = [(i, (i - 1) % ROWS) for i in range(ROWS)]
CORE_SWAP = [(i, i ^ 1) for i in range(COLS)]
SAME_CORE = [[2 * i + k for i in range(CHIPS)] for k in range(2)]
GROUPS = COLS // ROWS
MIXERS = [[GROUPS * i + k for i in range(ROWS)] for k in range(GROUPS)]


def split(x):
    high = x.astype(jnp.bfloat16)
    low = (x - high.astype(jnp.float32)).astype(jnp.bfloat16)
    return high, low


def dot3(a, b, dims):
    a_high, a_low = split(a)
    b_high, b_low = split(b)

    def mul(x, y):
        return lax.dot_general(x, y, (dims, ((), ())), preferred_element_type=jnp.float32)

    return mul(a_high, b_high) + (mul(a_high, b_low) + mul(a_low, b_high))


def spread(x, axis, size, groups=None):
    copies = jnp.broadcast_to(x[None], (size,) + x.shape)
    return lax.all_to_all(copies, axis, 0, 0, axis_index_groups=groups)


def in_vmem():
    return pl.BlockSpec(memory_space=pltpu.VMEM)


def grad_kernel(place, acts, *refs):
    pieces, (momentum, buffer, left, right, total, sems) = refs[:-6], refs[-6:]
    tokens = right.shape[0] // len(pieces)
    rows = total.shape[0]
    tile = rows // TILES
    fetches = []
    for n, g in enumerate(pieces):
        span = pl.ds(pl.multiple_of(place[n] * tokens, tokens), tokens)
        fetches.append(pltpu.make_async_copy(g, right.at[span, :], sems.at[n]))
    spans = [pl.ds(n * tile, tile) for n in range(TILES)]
    lefts = [pltpu.make_async_copy(acts.at[:, at], left.at[n], sems.at[len(pieces) + n]) for n, at in enumerate(spans)]
    olds = [
        pltpu.make_async_copy(momentum.at[at, :], total.at[at, :], sems.at[len(pieces) + TILES + n])
        for n, at in enumerate(spans)
    ]
    news = [
        pltpu.make_async_copy(total.at[at, :], buffer.at[at, :], sems.at[len(pieces) + 2 * TILES + n])
        for n, at in enumerate(spans)
    ]
    lefts[0].start()
    for copy in fetches:
        copy.start()
    olds[0].start()
    for n in range(1, TILES):
        lefts[n].start()
        olds[n].start()
    for copy in fetches:
        copy.wait()
    for n in range(TILES):
        lefts[n].wait()
        grad = lax.dot_general(
            left[n], right[...], (((0,), (0,)), ((), ())), preferred_element_type=jnp.float32
        )
        olds[n].wait()
        total[spans[n], :] += grad
        news[n].start()
    for copy in news:
        copy.wait()


def add_grad(place, acts, pieces, momentum):
    rows, cols = momentum.shape
    tokens = acts.shape[0]
    anywhere = pl.BlockSpec(memory_space=pl.ANY)
    return pl.pallas_call(
        grad_kernel,
        in_specs=[pl.BlockSpec(memory_space=pltpu.SMEM)] + [anywhere] * (len(pieces) + 2),
        out_specs=anywhere,
        out_shape=jax.ShapeDtypeStruct((rows, cols), jnp.float32),
        scratch_shapes=[
            pltpu.VMEM((TILES, tokens, rows // TILES), jnp.bfloat16),
            pltpu.VMEM((tokens, cols), jnp.bfloat16),
            pltpu.VMEM((rows, cols), jnp.float32),
            pltpu.SemaphoreType.DMA((len(pieces) + 3 * TILES,)),
        ],
        compiler_params=pltpu.CompilerParams(vmem_limit_bytes=VMEM_MOST),
        cost_estimate=pl.CostEstimate(
            flops=2 * tokens * rows * cols,
            bytes_accessed=2 * tokens * (rows + cols) + 8 * rows * cols,
            transcendentals=0,
        ),
        name="add_grad",
    )(place, acts, *pieces, momentum)


def cross_kernel(core, buffer, mine, other, cross, held, sems):
    cut = mine.shape[0]
    tile = held.shape[1]
    copies, sides = [], []
    for n in range(held.shape[0]):
        half, at = divmod(n * tile, cut)
        side = core[0] if half == 0 else 1 - core[0]
        start = pl.multiple_of(side * cut + at, tile)
        copies.append(pltpu.make_async_copy(buffer.at[pl.ds(start, tile), :], held.at[n], sems.at[n]))
        sides.append((mine, other)[half][at : at + tile, :])
    for copy in copies:
        copy.start()
    total = None
    for n, copy in enumerate(copies):
        copy.wait()
        term = dot3(held[n], sides[n], ((0,), (0,)))
        total = term if total is None else total + term
    cross[...] = total


def cross_part(core, buffer, mine, other):
    rows, cols = buffer.shape
    return pl.pallas_call(
        cross_kernel,
        in_specs=[pl.BlockSpec(memory_space=pltpu.SMEM), pl.BlockSpec(memory_space=pl.ANY)] + [in_vmem()] * 2,
        out_specs=in_vmem(),
        out_shape=jax.ShapeDtypeStruct((cols, mine.shape[1]), jnp.float32),
        scratch_shapes=[
            pltpu.VMEM((TILES, rows // TILES, cols), jnp.float32),
            pltpu.SemaphoreType.DMA((TILES,)),
        ],
        compiler_params=pltpu.CompilerParams(vmem_limit_bytes=VMEM_MOST),
        name="cross",
    )(core, buffer, mine, other)


def factor_kernel(gram, inverse, work):
    n = gram.shape[0]
    lanes = 128
    repeat = n // lanes
    work[...] = gram[...]
    rows = lax.broadcasted_iota(jnp.int32, (BLOCK, lanes), 0)
    row = lax.broadcasted_iota(jnp.int32, (BLOCK, n), 0)
    lane = lax.broadcasted_iota(jnp.int32, (BLOCK, n), 1)
    for first in range(0, n, BLOCK):
        last = first + BLOCK
        part = work[first:last, :]
        pivots = jnp.ones((BLOCK, lanes), jnp.float32)
        for j in range(0, BLOCK, STEP):
            at = first + j
            cols = [jnp.broadcast_to(part[:, at + k : at + k + 1], (BLOCK, lanes)) for k in range(STEP)]
            unit = jnp.where(lane - first == row, 1.0, 0.0)
            part = jnp.where((lane >= at) & (lane < at + STEP), unit, part)
            ratios = []
            for k in range(STEP):
                here = j + k
                pivot = cols[k][here : here + 1, :]
                pivots = jnp.where(rows == here, pivot, pivots)
                ratio = jnp.where(rows > here, cols[k] * (1.0 / pivot), 0.0)
                ratios.append(ratio)
                for m in range(k + 1, STEP):
                    cols[m] = cols[m] - ratio * cols[m][here : here + 1, :]
            for k in range(STEP):
                here = j + k
                part = part - jnp.concatenate([ratios[k]] * repeat, axis=1) * part[here : here + 1, :]
        part = part * jnp.concatenate([lax.rsqrt(pivots)] * repeat, axis=1)
        inverse[first:last, :] = jnp.where(lane < last, part, 0.0)
        if last < n:
            rest = work[last:, :]
            lane_rest = lax.broadcasted_iota(jnp.int32, rest.shape, 1)
            rest = jnp.where((lane_rest >= first) & (lane_rest < last), 0.0, rest)
            work[last:, :] = rest - lax.dot_general(
                part[:, last:],
                part,
                (((0,), (0,)), ((), ())),
                precision=lax.Precision.HIGHEST,
                preferred_element_type=jnp.float32,
            )


def inverse_factor(gram):
    n = gram.shape[0]
    return pl.pallas_call(
        factor_kernel,
        out_shape=jax.ShapeDtypeStruct((n, n), jnp.float32),
        scratch_shapes=[pltpu.VMEM((n, n), jnp.float32)],
        cost_estimate=pl.CostEstimate(flops=10**10, bytes_accessed=8 * n * n, transcendentals=0),
        name="inverse_factor",
    )(gram)


def back_kernel(place, inverse, s0, s1, s2, s3, s4, s5, s6, s7, back, norms):
    for n, share in enumerate((s0, s1, s2, s3, s4, s5, s6, s7)):
        height = share.shape[0]
        start = pl.multiple_of(place[n] * height, height)
        back[pl.ds(start, height), :] = dot3(share[...], inverse[...], ((1,), (1,)))
    whole = back[...]
    norms[...] = jnp.sum(whole * whole, axis=0, keepdims=True)


def back_and_norms(place, inverse, shares):
    rank = inverse.shape[0]
    cols = len(shares) * shares[0].shape[0]
    return pl.pallas_call(
        back_kernel,
        in_specs=[pl.BlockSpec(memory_space=pltpu.SMEM)] + [in_vmem()] * (1 + len(shares)),
        out_specs=[in_vmem()] * 2,
        out_shape=[
            jax.ShapeDtypeStruct((cols, rank), jnp.float32),
            jax.ShapeDtypeStruct((1, rank), jnp.float32),
        ],
        compiler_params=pltpu.CompilerParams(vmem_limit_bytes=VMEM_LIMIT),
        name="back_and_norms",
    )(place, inverse, *shares)


def momentum_kernel(buffer, ortho, back, new_momentum):
    fix = lax.dot_general(
        ortho[...].astype(jnp.bfloat16),
        back[...].astype(jnp.bfloat16),
        (((1,), (1,)), ((), ())),
        preferred_element_type=jnp.float32,
    )
    new_momentum[...] = buffer[...] - (1.0 - keep_rate) * fix


def update_momentum(buffer, ortho, back):
    rows, cols = buffer.shape
    rank = ortho.shape[1]
    tile = rows // TILES
    part = lambda width: pl.BlockSpec((tile, width), lambda i: (i, 0))
    return pl.pallas_call(
        momentum_kernel,
        grid=(TILES,),
        in_specs=[part(cols), part(rank), pl.BlockSpec(back.shape, lambda i: (0, 0))],
        out_specs=part(cols),
        out_shape=jax.ShapeDtypeStruct((rows, cols), jnp.float32),
        compiler_params=pltpu.CompilerParams(vmem_limit_bytes=VMEM_LIMIT),
        name="update_momentum",
    )(buffer, ortho, back)


def weight_kernel(weight, ortho, back, scale, new_weight, new_basis, basis, stepped, sems):
    factor = step_rate * math.sqrt(D * FF / RANK)
    right = back[...]
    basis[...] = right * scale[...]
    stores = []

    def store(source, target):
        copy = pltpu.make_async_copy(source, target, sems.at[len(stores)])
        copy.start()
        stores.append(copy)

    store(basis, new_basis)
    tile = weight.shape[0] // TILES
    for n in range(TILES):
        span = slice(n * tile, (n + 1) * tile)
        step = dot3(ortho[span, :] * scale[...], right, ((1,), (1,)))
        stepped[span, :] = (weight[span, :].astype(jnp.float32) - factor * step).astype(jnp.bfloat16)
        store(stepped.at[span, :], new_weight.at[span, :])
    for copy in stores:
        copy.wait()


def update_weight(weight, ortho, back, scale):
    rows, cols = weight.shape
    rank = ortho.shape[1]
    return pl.pallas_call(
        weight_kernel,
        in_specs=[in_vmem()] * 4,
        out_specs=[pl.BlockSpec(memory_space=pl.ANY)] * 2,
        out_shape=[
            jax.ShapeDtypeStruct((rows, cols), jnp.bfloat16),
            jax.ShapeDtypeStruct((cols, rank), jnp.float32),
        ],
        scratch_shapes=[
            pltpu.VMEM((cols, rank), jnp.float32),
            pltpu.VMEM((rows, cols), jnp.bfloat16),
            pltpu.SemaphoreType.DMA((1 + TILES,)),
        ],
        compiler_params=pltpu.CompilerParams(vmem_limit_bytes=VMEM_LIMIT),
        name="update_weight",
    )(weight, ortho, back, scale)


def call(kernel, name, shape, *args, scalars=0):
    many = isinstance(shape, list)
    return pl.pallas_call(
        kernel,
        in_specs=[pl.BlockSpec(memory_space=pltpu.SMEM)] * scalars + [in_vmem()] * (len(args) - scalars),
        out_specs=[in_vmem()] * len(shape) if many else in_vmem(),
        out_shape=[jax.ShapeDtypeStruct(x, jnp.float32) for x in shape]
        if many
        else jax.ShapeDtypeStruct(shape, jnp.float32),
        compiler_params=pltpu.CompilerParams(vmem_limit_bytes=VMEM_LIMIT),
        name=name,
    )(*args)


def sum_kernel(shares, copies):
    total = shares[0]
    for n in range(1, shares.shape[0]):
        total = total + shares[n]
    for n in range(copies.shape[0]):
        copies[n] = total


def sum_copies(shares, count):
    return call(sum_kernel, "sum_copies", (count,) + shares.shape[1:], shares)


def pick_kernel(core, part, other, mine):
    cut = mine.shape[0]
    span = pl.ds(pl.multiple_of(core[0] * cut, cut), cut)
    mine[...] = part[span, :] + other[span, :]


def gram_kernel(col, mine, other, copies):
    gram = jnp.zeros((mine.shape[1], mine.shape[1]), jnp.float32)
    for half in (mine, other):
        gram = gram + lax.dot_general(
            half[...],
            half[...],
            (((0,), (0,)), ((), ())),
            precision=lax.Precision.HIGHEST,
            preferred_element_type=jnp.float32,
        )
    copies[0] = jnp.zeros(copies.shape[1:], jnp.float32)
    height = copies.shape[1]
    for n in range(COLS):

        @pl.when(col[0] == n)
        def _():
            for m in range(copies.shape[0]):
                copies[m] = gram[n * height : (n + 1) * height, :]


def part_kernel(local, mixed, small, part):
    high, low = split(small[...])
    rank = small.shape[1]
    both = lax.dot_general(
        mixed[...],
        jnp.concatenate([high, low], axis=1),
        (((0,), (0,)), ((), ())),
        preferred_element_type=jnp.float32,
    )
    part[...] = local[...] + (both[:, :rank] + both[:, rank:])


def proj_part(local, mixed, small):
    return pl.pallas_call(
        part_kernel,
        in_specs=[in_vmem()] * 3,
        out_specs=in_vmem(),
        out_shape=jax.ShapeDtypeStruct(local.shape, jnp.float32),
        compiler_params=pltpu.CompilerParams(vmem_limit_bytes=VMEM_LIMIT),
        name="proj_part",
    )(local, mixed, small)


def on_device(acts, out_grads, weight, momentum, basis):
    high = lax.Precision.HIGH
    highest = lax.Precision.HIGHEST
    row = lax.axis_index("row")
    col = lax.axis_index("col")
    core = (col % 2).reshape(1)
    rank = basis.shape[1]

    with jax.named_scope("gather_acts"):
        acts_all = lax.all_gather(acts, "col", axis=0, tiled=True)

    pieces, places = [out_grads], [row]
    up = down = out_grads

    def turn(step, *others):
        nonlocal up, down
        with jax.named_scope("gather_grads"):
            up = lax.ppermute(up, "row", UP)
            down = lax.ppermute(down, "row", DOWN)
            pieces.extend([up, down])
            places.extend([row - step, row + step])
            up, down, *others = lax.optimization_barrier((up, down, *others))
            return others

    with jax.named_scope("proj"):
        small = jnp.dot(out_grads.astype(jnp.float32), basis, precision=high)
        small = small.reshape(GROUPS, ROWS, -1, rank).swapaxes(0, 1).reshape(COLS, -1, rank)
        small = sum_copies(lax.all_to_all(small, "col", 0, 0), ROWS)
        mixed = acts.reshape(ROWS, -1, acts.shape[1])
        local = jnp.dot(momentum, basis, precision=high)
        small, mixed, local = turn(1, small, mixed, local)
        mixed = lax.all_to_all(mixed, "col", 0, 0, axis_index_groups=MIXERS)
        small, mixed = turn(2, small, mixed)
        small = lax.all_to_all(small, "row", 0, 0).reshape(-1, rank)
        part = proj_part(local, mixed.reshape(-1, acts.shape[1]), small)
        (part,) = turn(3, part)

    with jax.named_scope("gather_grads"):
        pieces.append(lax.ppermute(up, "row", UP))
        places.append(row + ROWS // 2)
        place = jnp.stack(places).astype(jnp.int32) % ROWS

    with jax.named_scope("sum_proj"):
        cut = part.shape[0] // 2
        other = lax.ppermute(part, "col", CORE_SWAP)
        mine = call(pick_kernel, "pick", (cut, rank), core, part, other, scalars=1)
        shares = mine.reshape(CHIPS, cut // CHIPS, rank)
        shares = lax.all_to_all(shares, "col", 0, 0, axis_index_groups=SAME_CORE)
        buffer = add_grad(place, acts_all, pieces, momentum)
        mine = sum_copies(shares, CHIPS)
        mine = lax.all_to_all(mine, "col", 0, 0, axis_index_groups=SAME_CORE).reshape(cut, rank)
        mine, buffer = lax.optimization_barrier((mine, buffer))
        other = lax.ppermute(mine, "col", CORE_SWAP)

    with jax.named_scope("cross"):
        cross = cross_part(core, buffer, mine, other)
        cross, mine, other = lax.optimization_barrier((cross, mine, other))
        share = lax.psum_scatter(cross, "row", scatter_dimension=0, tiled=True)

    with jax.named_scope("gram"):
        height = rank // COLS
        gram = call(gram_kernel, "gram", (ROWS, height, rank), col.reshape(1), mine, other, scalars=1)
        gram = sum_copies(lax.all_to_all(gram, "row", 0, 0), COLS)
        gram = lax.all_to_all(gram, "col", 0, 0).reshape(rank, rank)

    inverse = inverse_factor(gram)
    share, inverse = lax.optimization_barrier((share, inverse))
    first = core[0] == 0
    proj = jnp.concatenate([jnp.where(first, mine, other), jnp.where(first, other, mine)], axis=0)
    ortho = lax.dot_general(proj, inverse, (((1,), (1,)), ((), ())), precision=highest)

    with jax.named_scope("gather_cross"):
        parts = [share]
        up = down = share
        for _ in range(1, ROWS // 2):
            up = lax.ppermute(up, "row", UP)
            down = lax.ppermute(down, "row", DOWN)
            parts += [up, down]
        parts.append(lax.ppermute(up, "row", UP))

    back, norms = back_and_norms(place, inverse, parts)

    with jax.named_scope("norms"):
        norms = jnp.sum(spread(norms, "col", COLS), axis=0)
        scale = 1.0 / jnp.sqrt(norms + norm_eps)

    new_momentum = update_momentum(buffer, ortho, back)
    new_weight, new_basis = update_weight(weight, ortho, back, scale)
    return (new_weight, new_momentum, new_basis)


def solution(mesh):
    return jax.shard_map(
        on_device,
        mesh=mesh,
        in_specs=(
            P("col", "row"),
            P("row", "col"),
            P("row", "col"),
            P("row", "col"),
            P("col", None),
        ),
        out_specs=(P("row", "col"), P("row", "col"), P("col", None)),
        check_vma=False,
    )
```

time: 208 us -> 203 us (0.976); the launches traced: 204 us -> 203 us
  blocking collectives: 70 us -> 50.3 us
  starting transfers between devices: 33.8 us -> 50 us
  Pallas kernels: 25.5 us -> 36.4 us
  matrix products: 16.7 us -> 7.51 us
  other arithmetic: 4.46 us -> 1.47 us
    all_to_all x4 -> x3, blocking collectives: 59.7 us -> 40.5 us  [the longest x1 17.8 us: on_device(): gram = lax.all_to_all(gram, 'col', 0, 0).reshape(rank, rank)]
    all_to_all x2 -> x1, waiting for transfers between devices: 14.9 us -> 0.32 us  [spread(): return lax.all_to_all(copies, axis, 0, 0, axis_index_groups=groups)]
    ppermute x3 -> x9, waiting for transfers between devices: 2.21 us -> 13.9 us  [the longest x3 7.6 us: on_device(): up = lax.ppermute(up, 'row', UP)]
    all_to_all x0 -> x2, starting transfers between devices: none -> 11.6 us  [the longest x1 8.04 us: on_device(): small = sum_copies(lax.all_to_all(small, 'col', 0, 0), ROWS)]
    pallas_call x2 -> x11, Pallas kernels: 16 us -> 27.3 us  [the longest x1 9.59 us: add_grad(): pl.pallas_call(grad_kernel, in_specs=[pl.BlockSpec(memory_space=pltpu.SME...]
    all_to_all x1, waiting for transfers between devices: 0.01 us -> 9.38 us  [on_device(): shares = lax.all_to_all(shares, 'col', 0, 0, axis_index_groups=SAME_CORE)]
    ppermute x3 -> x9, starting transfers between devices: 4.33 us -> 12.9 us  [the longest x3 7.81 us: on_device(): down = lax.ppermute(down, 'row', DOWN)]
    dot_general x4 -> x0, matrix products: 8.3 us -> none  [the longest x1 4.06 us: on_device(): lax.dot_general(buffer, proj, (((0,), (0,)), ((), ())), precision=high)]
  transfers between devices with their start and end apart: 16 -> 22, of which waited for: 6 -> 10; matrix products, arithmetic and copies ran while one was open for 10% -> 5% of each run, Pallas kernels for 9% -> 12%
where the time goes in v3:
time: 203 us
  blocking collectives  50.3 us (25%)
  starting transfers between devices  50 us (25%)
  Pallas kernels  36.4 us (18%)
  waiting for transfers between devices  32 us (16%)
  between operations  14.3 us (7%)
  local copies, waits for them, and re-layouts  10.5 us (5%)
  matrix products  7.51 us (4%)
    all_to_all x1, blocking collectives, on_device(): gram = lax.all_to_all(gram, 'col', 0, 0).reshape(rank, rank)  17.8 us
    all_to_all x1, blocking collectives, on_device(): small = lax.all_to_all(small, 'row', 0, 0).reshape(-1, rank)  12 us
    all_to_all x1, blocking collectives, on_device(): gram = sum_copies(lax.all_to_all(gram, 'row', 0, 0), COLS)  10.7 us
    all_to_all x1, blocking collectives, on_device(): mixed = lax.all_to_all(mixed, 'col', 0, 0, axis_index_groups=MIXERS)  9.81 us
    pallas_call x1, Pallas kernels, add_grad(): pl.pallas_call(grad_kernel, in_specs=[pl.BlockSpec(memory_space=pltpu.SME...  9.59 us
    all_to_all x1, waiting for transfers between devices, on_device(): shares = lax.all_to_all(shares, 'col', 0, 0, axis_index_groups=SAME_CORE)  9.38 us
    ppermute x3, starting transfers between devices, turn(): down = lax.ppermute(down, 'row', DOWN)  9.36 us
    unnamed x38, local copies, waits for them, and re-layouts  9.08 us
  transfers between devices with their start and end apart: 22, of which 10 were waited for; matrix products, arithmetic and copies ran while one was open for 5% of the time, Pallas kernels for 12%

profile of v3, /device:TPU:1, one launch (start us, length us, event | category | flops | bytes accessed | tf_op | source)
XLA Modules:
  0.0 202.5 jit_solution(13505502473178889087)
XLA Ops:
  10.5 4.0 %collective-permute-start.1 = (bf16[256,896]{1,0:T(8,128)(2,1)}, bf16[256,896]{1,0:T(8,128)(2,1)}, u32[]{:S(2)}, u32[]{:S(2)}) collective-permute-start(bf16[256,896]{1,0:T(8,128)(2,1)} %refs_0_.1), channel_id=1, source_target_pairs={{0,224},{32,0},{64,32},{96,64},{128,96},{160,128},{192,160},{224,1... | collective-permute-start | bytes 1376264 | tf_op jit(solution)/shard_map/proj/gather_grads/ppermute | solution.py:403
  16.7 8.0 %all-to-all-start = ((f32[32,8,256]{2,1,0:T(8,128)}), f32[32,8,256]{2,1,0:T(8,128)S(1)}, u32[]{:S(2)}, u32[]{:S(2)}) async-start(f32[32,8,256]{2,1,0:T(8,128)} %bitcast.3), calls=%async_computation | async-start | bytes 524288 | tf_op jit(solution)/shard_map/proj/all_to_all | solution.py:412
  24.8 3.9 %fusion.7.local = f32[1024,256]{1,0:T(8,128)S(1)} fusion(f32[1024,896]{1,0:T(8,128)} %refs_8_.1, f32[896,256]{1,0:T(8,128)S(1)} %copy-done), kind=kOutput, calls=%fused_computation.13 | convolution fusion | flops 1409286144 | bytes 5636096 | tf_op jit(solution)/shard_map/proj/dot_general | solution.py:414
  28.7 5.3 %all-to-all-done.shares = f32[32,8,256]{2,1,0:T(8,128)S(1)} async-done(((f32[32,8,256]{2,1,0:T(8,128)}), f32[32,8,256]{2,1,0:T(8,128)S(1)}, u32[]{:S(2)}, u32[]{:S(2)}) %all-to-all-start) | async-done | bytes 262176 | tf_op jit(solution)/shard_map/proj/all_to_all | solution.py:412
  34.1 2.7 %collective-permute-start.3 = (bf16[256,896]{1,0:T(8,128)(2,1)}, bf16[256,896]{1,0:T(8,128)(2,1)S(1)}, u32[]{:S(2)}, u32[]{:S(2)}) collective-permute-start(bf16[256,896]{1,0:T(8,128)(2,1)} %collective-permute-done.1.refs_2_), channel_id=1, source_target_pairs={{0,224},{32,0},{64,32},{96,64},{128,96},{160,128},{192,160},{224,1... | collective-permute-start | bytes 1376264 | tf_op jit(solution)/shard_map/proj/gather_grads/ppermute | solution.py:403
  36.8 9.8 %all_to_all.40 = bf16[8,8,1024]{2,1,0:T(8,128)(2,1)S(1)} all-to-all(bf16[8,8,1024]{2,1,0:T(8,128)(2,1)S(1)} %bitcast.36), channel_id=1, replica_groups={{0,4,8,12,16,20,24,28},{1,5,9,13,17,21,25,29},{2,6,10,14,18,22,26,30},{..., dimensions={0} | all-to-all | bytes 262144 | tf_op jit(solution)/shard_map/proj/all_to_all | solution.py:416
  47.6 2.7 %collective-permute-start.5 = (bf16[256,896]{1,0:T(8,128)(2,1)S(1)}, bf16[256,896]{1,0:T(8,128)(2,1)S(1)}, u32[]{:S(2)}, u32[]{:S(2)}) collective-permute-start(bf16[256,896]{1,0:T(8,128)(2,1)S(1)} %collective-permute-done.3.refs_4_), channel_id=1, source_target_pairs={{0,224},{32,0},{64,32},{96,64},{128,96},{160,128},{192,160},{224,1... | collective-permute-start | bytes 1376264 | tf_op jit(solution)/shard_map/proj/gather_grads/ppermute | solution.py:403
  50.3 12.0 %all_to_all.41 = f32[8,8,256]{2,1,0:T(8,128)S(1)} all-to-all(f32[8,8,256]{2,1,0:T(8,128)S(1)} %sum_copies.3), channel_id=1, replica_groups=mesh['row'=8,'col'=32] {'row'}, dimensions={0} | all-to-all | bytes 131072 | tf_op jit(solution)/shard_map/proj/all_to_all | solution.py:418
  62.8 3.4 %collective-permute-start.6 = (f32[1024,256]{1,0:T(8,128)S(1)}, f32[1024,256]{1,0:T(8,128)S(1)}, u32[]{:S(2)}, u32[]{:S(2)}) collective-permute-start(f32[1024,256]{1,0:T(8,128)S(1)} %proj_part.1.part), channel_id=1, source_target_pairs={{0,1},{1,0},{2,3},{3,2},{4,5},{5,4},{6,7},{7,6},{8,9},{9,8},{10,11... | collective-permute-start | bytes 3145736 | tf_op jit(solution)/shard_map/sum_proj/ppermute | solution.py:429
  69.3 3.6 %all-to-all-start.3 = ((f32[16,32,256]{2,1,0:T(8,128)}), f32[16,32,256]{2,1,0:T(8,128)S(1)}, u32[]{:S(2)}, u32[]{:S(2)}) async-start(f32[16,32,256]{2,1,0:T(8,128)} %bitcast.7), calls=%async_computation.3 | async-start | bytes 1048576 | tf_op jit(solution)/shard_map/sum_proj/all_to_all | solution.py:432
  74.4 9.4 %all-to-all-done.3.shares = f32[16,32,256]{2,1,0:T(8,128)S(1)} async-done(((f32[16,32,256]{2,1,0:T(8,128)}), f32[16,32,256]{2,1,0:T(8,128)S(1)}, u32[]{:S(2)}, u32[]{:S(2)}) %all-to-all-start.3) | async-done | bytes 524320 | tf_op jit(solution)/shard_map/sum_proj/all_to_all | solution.py:432
  84.7 3.6 %all-to-all-start.4 = ((f32[16,32,256]{2,1,0:T(8,128)}), f32[16,32,256]{2,1,0:T(8,128)S(1)}, u32[]{:S(2)}, u32[]{:S(2)}) async-start(f32[16,32,256]{2,1,0:T(8,128)} %sum_copies.4), calls=%async_computation.4 | async-start | bytes 1048576 | tf_op jit(solution)/shard_map/sum_proj/all_to_all | solution.py:435
  89.8 9.6 %add_grad.1.buffer = f32[1024,896]{1,0:T(8,128)} custom-call(s32[8]{0:T(128)} %and_select_fusion.place, bf16[2048,1024]{1,0:T(8,128)(2,1)} %all-gather.2.cloned.1.call-done.acts, bf16[256,896]{1,0:T(8,128)(2,1)} %refs_0_.1, bf16[256,896]{1,0:T(8,128)(2,1)} %copy-done.13, bf16[256,896]{1,0:T(8,128)(2,1)} %collective-permute-done.1.refs_2_, ...), custom_call_target="tpu_custom_call" | custom-call | flops 3758096384 | bytes 15204352 | tf_op jit(solution)/shard_map/sum_proj/add_grad/pallas_call | solution.py:104
  103.4 6.7 %cross.1 = f32[896,256]{1,0:T(8,128)} custom-call(s32[1]{0:T(128)} %bitcast.core, f32[1024,896]{1,0:T(8,128)} %add_grad.1.buffer, f32[512,256]{1,0:T(8,128)} %bitcast.28, f32[512,256]{1,0:T(8,128)} %copy-done.5), custom_call_target="tpu_custom_call" | custom-call | tf_op jit(solution)/shard_map/cross/cross/pallas_call | solution.py:147
  113.6 10.7 %all_to_all.42.shares = f32[8,8,256]{2,1,0:T(8,128)S(1)} all-to-all(f32[8,8,256]{2,1,0:T(8,128)S(1)} %gram.1), channel_id=1, replica_groups=mesh['row'=8,'col'=32] {'row'}, dimensions={0} | all-to-all | bytes 131072 | tf_op jit(solution)/shard_map/gram/all_to_all | solution.py:447
  124.3 17.8 %all_to_all.43 = f32[32,8,256]{2,1,0:T(8,128)} all-to-all(f32[32,8,256]{2,1,0:T(8,128)S(1)} %sum_copies.5), channel_id=1, replica_groups=mesh['row'=8,'col'=32] {'col'}, dimensions={0} | all-to-all | bytes 524288 | tf_op jit(solution)/shard_map/gram/all_to_all | solution.py:448
  142.2 9.0 %inverse_factor.1.inverse = f32[256,256]{1,0:T(8,128)} custom-call(f32[256,256]{1,0:T(8,128)} %bitcast.37), custom_call_target="tpu_custom_call" | custom-call | flops 10000000000 | bytes 524288 | tf_op jit(solution)/shard_map/inverse_factor/pallas_call | solution.py:207
  153.9 3.3 %collective-permute-done.9.s1 = f32[112,256]{1,0:T(8,128)S(1)} collective-permute-done((f32[112,256]{1,0:T(8,128)}, f32[112,256]{1,0:T(8,128)S(1)}, u32[]{:S(2)}, u32[]{:S(2)}) %collective-permute-start.9) | collective-permute-done | bytes 114720 | tf_op jit(solution)/shard_map/gather_cross/ppermute | solution.py:460
  157.1 2.7 %collective-permute-start.12 = (f32[112,256]{1,0:T(8,128)S(1)}, f32[112,256]{1,0:T(8,128)S(1)}, u32[]{:S(2)}, u32[]{:S(2)}) collective-permute-start(f32[112,256]{1,0:T(8,128)S(1)} %collective-permute-done.10.s2), channel_id=1, source_target_pairs={{0,224},{32,0},{64,32},{96,64},{128,96},{160,128},{192,160},{224,1... | collective-permute-start | bytes 344072 | tf_op jit(solution)/shard_map/gather_cross/ppermute | solution.py:461
  162.0 2.7 %collective-permute-start.14 = (f32[112,256]{1,0:T(8,128)S(1)}, f32[112,256]{1,0:T(8,128)S(1)}, u32[]{:S(2)}, u32[]{:S(2)}) collective-permute-start(f32[112,256]{1,0:T(8,128)S(1)} %collective-permute-done.12.s4), channel_id=1, source_target_pairs={{0,224},{32,0},{64,32},{96,64},{128,96},{160,128},{192,160},{224,1... | collective-permute-start | bytes 344072 | tf_op jit(solution)/shard_map/gather_cross/ppermute | solution.py:461
  167.7 4.0 %collective-permute-done.15.s7 = f32[112,256]{1,0:T(8,128)S(1)} collective-permute-done((f32[112,256]{1,0:T(8,128)S(1)}, f32[112,256]{1,0:T(8,128)S(1)}, u32[]{:S(2)}, u32[]{:S(2)}) %collective-permute-start.15) | collective-permute-done | bytes 114720 | tf_op jit(solution)/shard_map/gather_cross/ppermute | solution.py:463
  176.0 8.0 %all-to-all-start.7 = ((f32[32,1,256]{2,1,0:T(1,128)}), f32[32,1,256]{2,1,0:T(1,128)S(1)}, u32[]{:S(2)}, u32[]{:S(2)}) async-start(f32[32,1,256]{2,1,0:T(1,128)} %broadcast_in_dim.9), calls=%async_computation.8 | async-start | bytes 65536 | tf_op jit(solution)/shard_map/norms/all_to_all | solution.py:53
  188.2 2.9 %update_momentum.1 = f32[1024,896]{1,0:T(8,128)} custom-call(f32[1024,896]{1,0:T(8,128)S(1)} %copy-done.1, f32[1024,256]{1,0:T(8,128)S(1)} %fusion.ortho, f32[896,256]{1,0:T(8,128)S(1)} %get-tuple-element.43.back), custom_call_target="tpu_custom_call" | custom-call | tf_op jit(solution)/shard_map/update_momentum/pallas_call | solution.py:256
  192.9 2.8 %update_weight.1 = (bf16[1024,896]{1,0:T(8,128)(2,1)}, f32[896,256]{1,0:T(8,128)}) custom-call(bf16[1024,896]{1,0:T(8,128)(2,1)S(1)} %copy-done.8, f32[1024,256]{1,0:T(8,128)S(1)} %fusion.ortho, f32[896,256]{1,0:T(8,128)S(1)} %get-tuple-element.43.back, f32[1,256]{1,0:T(1,128)S(1)} %bitcast.33), custom_call_target="tpu_custom_call" | custom-call | tf_op jit(solution)/shard_map/update_weight/pallas_call | solution.py:292
  (86 shorter events, 39.9 us)
Async XLA Ops:
  7.2 81.9 %all-gather.2.cloned.1.call-start = ((), (), s32[]{:S(2)}) async-start(), calls=%async_computation.9 | async-start | bytes 4325376 | tf_op jit(solution)/shard_map/gather_acts/all_gather | solution.py:394
  7.9 26.1 %collective-permute-start = (bf16[256,896]{1,0:T(8,128)(2,1)}, bf16[256,896]{1,0:T(8,128)(2,1)S(1)}, u32[]{:S(2)}, u32[]{:S(2)}) collective-permute-start(bf16[256,896]{1,0:T(8,128)(2,1)} %refs_0_.1), channel_id=1, source_target_pairs={{0,32},{32,64},{64,96},{96,128},{128,160},{160,192},{192,224},{224... | collective-permute-start | bytes 1376264 | tf_op jit(solution)/shard_map/proj/gather_grads/ppermute | solution.py:402
  10.5 23.6 %collective-permute-start.1 = (bf16[256,896]{1,0:T(8,128)(2,1)}, bf16[256,896]{1,0:T(8,128)(2,1)}, u32[]{:S(2)}, u32[]{:S(2)}) collective-permute-start(bf16[256,896]{1,0:T(8,128)(2,1)} %refs_0_.1), channel_id=1, source_target_pairs={{0,224},{32,0},{64,32},{96,64},{128,96},{160,128},{192,160},{224,1... | collective-permute-start | bytes 1376264 | tf_op jit(solution)/shard_map/proj/gather_grads/ppermute | solution.py:403
  16.7 17.2 %all-to-all-start = ((f32[32,8,256]{2,1,0:T(8,128)}), f32[32,8,256]{2,1,0:T(8,128)S(1)}, u32[]{:S(2)}, u32[]{:S(2)}) async-start(f32[32,8,256]{2,1,0:T(8,128)} %bitcast.3), calls=%async_computation | async-start | bytes 524288 | tf_op jit(solution)/shard_map/proj/all_to_all | solution.py:412
  34.0 28.3 %copy-start.13 = (bf16[256,896]{1,0:T(8,128)(2,1)}, bf16[256,896]{1,0:T(8,128)(2,1)S(1)}, u32[]{:S(2)}) copy-start(bf16[256,896]{1,0:T(8,128)(2,1)S(1)} %collective-permute-done.refs_1_) | copy-start | bytes 1376260
  34.0 13.5 %collective-permute-start.2 = (bf16[256,896]{1,0:T(8,128)(2,1)S(1)}, bf16[256,896]{1,0:T(8,128)(2,1)S(1)}, u32[]{:S(2)}, u32[]{:S(2)}) collective-permute-start(bf16[256,896]{1,0:T(8,128)(2,1)S(1)} %collective-permute-done.refs_1_), channel_id=1, source_target_pairs={{0,32},{32,64},{64,96},{96,128},{128,160},{160,192},{192,224},{224... | collective-permute-start | bytes 1376264 | tf_op jit(solution)/shard_map/proj/gather_grads/ppermute | solution.py:402
  34.1 13.4 %collective-permute-start.3 = (bf16[256,896]{1,0:T(8,128)(2,1)}, bf16[256,896]{1,0:T(8,128)(2,1)S(1)}, u32[]{:S(2)}, u32[]{:S(2)}) collective-permute-start(bf16[256,896]{1,0:T(8,128)(2,1)} %collective-permute-done.1.refs_2_), channel_id=1, source_target_pairs={{0,224},{32,0},{64,32},{96,64},{128,96},{160,128},{192,160},{224,1... | collective-permute-start | bytes 1376264 | tf_op jit(solution)/shard_map/proj/gather_grads/ppermute | solution.py:403
  47.5 15.3 %collective-permute-start.4 = (bf16[256,896]{1,0:T(8,128)(2,1)S(1)}, bf16[256,896]{1,0:T(8,128)(2,1)S(1)}, u32[]{:S(2)}, u32[]{:S(2)}) collective-permute-start(bf16[256,896]{1,0:T(8,128)(2,1)S(1)} %collective-permute-done.2.refs_3_), channel_id=1, source_target_pairs={{0,32},{32,64},{64,96},{96,128},{128,160},{160,192},{192,224},{224... | collective-permute-start | bytes 1376264 | tf_op jit(solution)/shard_map/proj/gather_grads/ppermute | solution.py:402
  47.6 15.2 %collective-permute-start.5 = (bf16[256,896]{1,0:T(8,128)(2,1)S(1)}, bf16[256,896]{1,0:T(8,128)(2,1)S(1)}, u32[]{:S(2)}, u32[]{:S(2)}) collective-permute-start(bf16[256,896]{1,0:T(8,128)(2,1)S(1)} %collective-permute-done.3.refs_4_), channel_id=1, source_target_pairs={{0,224},{32,0},{64,32},{96,64},{128,96},{160,128},{192,160},{224,1... | collective-permute-start | bytes 1376264 | tf_op jit(solution)/shard_map/proj/gather_grads/ppermute | solution.py:403
  62.8 5.6 %collective-permute-start.6 = (f32[1024,256]{1,0:T(8,128)S(1)}, f32[1024,256]{1,0:T(8,128)S(1)}, u32[]{:S(2)}, u32[]{:S(2)}) collective-permute-start(f32[1024,256]{1,0:T(8,128)S(1)} %proj_part.1.part), channel_id=1, source_target_pairs={{0,1},{1,0},{2,3},{3,2},{4,5},{5,4},{6,7},{7,6},{8,9},{9,8},{10,11... | collective-permute-start | bytes 3145736 | tf_op jit(solution)/shard_map/sum_proj/ppermute | solution.py:429
  69.3 14.5 %all-to-all-start.3 = ((f32[16,32,256]{2,1,0:T(8,128)}), f32[16,32,256]{2,1,0:T(8,128)S(1)}, u32[]{:S(2)}, u32[]{:S(2)}) async-start(f32[16,32,256]{2,1,0:T(8,128)} %bitcast.7), calls=%async_computation.3 | async-start | bytes 1048576 | tf_op jit(solution)/shard_map/sum_proj/all_to_all | solution.py:432
  72.9 16.2 %collective-permute-start.7 = (bf16[256,896]{1,0:T(8,128)(2,1)S(1)}, bf16[256,896]{1,0:T(8,128)(2,1)S(1)}, u32[]{:S(2)}, u32[]{:S(2)}) collective-permute-start(bf16[256,896]{1,0:T(8,128)(2,1)S(1)} %collective-permute-done.4.refs_5_), channel_id=1, source_target_pairs={{0,32},{32,64},{64,96},{96,128},{128,160},{160,192},{192,224},{224... | collective-permute-start | bytes 1376264 | tf_op jit(solution)/shard_map/gather_grads/ppermute | solution.py:423
  84.7 14.7 %all-to-all-start.4 = ((f32[16,32,256]{2,1,0:T(8,128)}), f32[16,32,256]{2,1,0:T(8,128)S(1)}, u32[]{:S(2)}, u32[]{:S(2)}) async-start(f32[16,32,256]{2,1,0:T(8,128)} %sum_copies.4), calls=%async_computation.4 | async-start | bytes 1048576 | tf_op jit(solution)/shard_map/sum_proj/all_to_all | solution.py:435
  88.3 62.9 %reduce-scatter.2.cloned.1.call-start = ((), (), s32[]{:S(2)}) async-start(), calls=%async_computation.10 | async-start | bytes 1032192 | tf_op jit(solution)/shard_map/cross/reduce_scatter | solution.py:442
  99.4 3.2 %collective-permute-start.8 = (f32[512,256]{1,0:T(8,128)S(1)}, f32[512,256]{1,0:T(8,128)S(1)}, u32[]{:S(2)}, u32[]{:S(2)}) collective-permute-start(f32[512,256]{1,0:T(8,128)S(1)} %bitcast.27), channel_id=1, source_target_pairs={{0,1},{1,0},{2,3},{3,2},{4,5},{5,4},{6,7},{7,6},{8,9},{9,8},{10,11... | collective-permute-start | bytes 1572872 | tf_op jit(solution)/shard_map/sum_proj/ppermute | solution.py:437
  142.2 29.5 %copy-start.11 = (s32[8]{0:T(128)S(1)}, s32[8]{0:T(128)}, u32[]{:S(2)}) copy-start(s32[8]{0:T(128)} %and_select_fusion.place) | copy-start | bytes 100
  151.2 5.9 %collective-permute-start.9 = (f32[112,256]{1,0:T(8,128)}, f32[112,256]{1,0:T(8,128)S(1)}, u32[]{:S(2)}, u32[]{:S(2)}) collective-permute-start(f32[112,256]{1,0:T(8,128)} %reduce-scatter.2.cloned.1.call-done.s0), channel_id=1, source_target_pairs={{0,32},{32,64},{64,96},{96,128},{128,160},{160,192},{192,224},{224... | collective-permute-start | bytes 344072 | tf_op jit(solution)/shard_map/gather_cross/ppermute | solution.py:460
  151.4 5.7 %collective-permute-start.10 = (f32[112,256]{1,0:T(8,128)}, f32[112,256]{1,0:T(8,128)S(1)}, u32[]{:S(2)}, u32[]{:S(2)}) collective-permute-start(f32[112,256]{1,0:T(8,128)} %reduce-scatter.2.cloned.1.call-done.s0), channel_id=1, source_target_pairs={{0,224},{32,0},{64,32},{96,64},{128,96},{160,128},{192,160},{224,1... | collective-permute-start | bytes 344072 | tf_op jit(solution)/shard_map/gather_cross/ppermute | solution.py:461
  157.1 4.9 %collective-permute-start.11 = (f32[112,256]{1,0:T(8,128)S(1)}, f32[112,256]{1,0:T(8,128)S(1)}, u32[]{:S(2)}, u32[]{:S(2)}) collective-permute-start(f32[112,256]{1,0:T(8,128)S(1)} %collective-permute-done.9.s1), channel_id=1, source_target_pairs={{0,32},{32,64},{64,96},{96,128},{128,160},{160,192},{192,224},{224... | collective-permute-start | bytes 344072 | tf_op jit(solution)/shard_map/gather_cross/ppermute | solution.py:460
  157.1 4.9 %collective-permute-start.12 = (f32[112,256]{1,0:T(8,128)S(1)}, f32[112,256]{1,0:T(8,128)S(1)}, u32[]{:S(2)}, u32[]{:S(2)}) collective-permute-start(f32[112,256]{1,0:T(8,128)S(1)} %collective-permute-done.10.s2), channel_id=1, source_target_pairs={{0,224},{32,0},{64,32},{96,64},{128,96},{160,128},{192,160},{224,1... | collective-permute-start | bytes 344072 | tf_op jit(solution)/shard_map/gather_cross/ppermute | solution.py:461
  162.0 4.9 %collective-permute-start.13 = (f32[112,256]{1,0:T(8,128)S(1)}, f32[112,256]{1,0:T(8,128)S(1)}, u32[]{:S(2)}, u32[]{:S(2)}) collective-permute-start(f32[112,256]{1,0:T(8,128)S(1)} %collective-permute-done.11.s3), channel_id=1, source_target_pairs={{0,32},{32,64},{64,96},{96,128},{128,160},{160,192},{192,224},{224... | collective-permute-start | bytes 344072 | tf_op jit(solution)/shard_map/gather_cross/ppermute | solution.py:460
  162.0 5.7 %collective-permute-start.14 = (f32[112,256]{1,0:T(8,128)S(1)}, f32[112,256]{1,0:T(8,128)S(1)}, u32[]{:S(2)}, u32[]{:S(2)}) collective-permute-start(f32[112,256]{1,0:T(8,128)S(1)} %collective-permute-done.12.s4), channel_id=1, source_target_pairs={{0,224},{32,0},{64,32},{96,64},{128,96},{160,128},{192,160},{224,1... | collective-permute-start | bytes 344072 | tf_op jit(solution)/shard_map/gather_cross/ppermute | solution.py:461
  166.8 4.9 %collective-permute-start.15 = (f32[112,256]{1,0:T(8,128)S(1)}, f32[112,256]{1,0:T(8,128)S(1)}, u32[]{:S(2)}, u32[]{:S(2)}) collective-permute-start(f32[112,256]{1,0:T(8,128)S(1)} %collective-permute-done.13.s5), channel_id=1, source_target_pairs={{0,32},{32,64},{64,96},{96,128},{128,160},{160,192},{192,224},{224... | collective-permute-start | bytes 344072 | tf_op jit(solution)/shard_map/gather_cross/ppermute | solution.py:463
  176.0 15.4 %all-to-all-start.7 = ((f32[32,1,256]{2,1,0:T(1,128)}), f32[32,1,256]{2,1,0:T(1,128)S(1)}, u32[]{:S(2)}, u32[]{:S(2)}) async-start(f32[32,1,256]{2,1,0:T(1,128)} %broadcast_in_dim.9), calls=%async_computation.8 | async-start | bytes 65536 | tf_op jit(solution)/shard_map/norms/all_to_all | solution.py:53
  (17 other events, 149.9 us)
Sparse Core Ops, SparseCore 0:
  10.6 55.2 all-gather.1
  110.2 32.2 reduce-scatter.1

commit v4 on v3

--- a/solution.py
+++ b/solution.py
@@ -122,40 +122,12 @@
     )(place, acts, *pieces, momentum)
 
 
-def cross_kernel(core, buffer, mine, other, cross, held, sems):
+def cross_kernel(core, buffer, mine, other, cross):
     cut = mine.shape[0]
-    tile = held.shape[1]
-    copies, sides = [], []
-    for n in range(held.shape[0]):
-        half, at = divmod(n * tile, cut)
-        side = core[0] if half == 0 else 1 - core[0]
-        start = pl.multiple_of(side * cut + at, tile)
-        copies.append(pltpu.make_async_copy(buffer.at[pl.ds(start, tile), :], held.at[n], sems.at[n]))
-        sides.append((mine, other)[half][at : at + tile, :])
-    for copy in copies:
-        copy.start()
-    total = None
-    for n, copy in enumerate(copies):
-        copy.wait()
-        term = dot3(held[n], sides[n], ((0,), (0,)))
-        total = term if total is None else total + term
-    cross[...] = total
-
-
-def cross_part(core, buffer, mine, other):
-    rows, cols = buffer.shape
-    return pl.pallas_call(
-        cross_kernel,
-        in_specs=[pl.BlockSpec(memory_space=pltpu.SMEM), pl.BlockSpec(memory_space=pl.ANY)] + [in_vmem()] * 2,
-        out_specs=in_vmem(),
-        out_shape=jax.ShapeDtypeStruct((cols, mine.shape[1]), jnp.float32),
-        scratch_shapes=[
-            pltpu.VMEM((TILES, rows // TILES, cols), jnp.float32),
-            pltpu.SemaphoreType.DMA((TILES,)),
-        ],
-        compiler_params=pltpu.CompilerParams(vmem_limit_bytes=VMEM_MOST),
-        name="cross",
-    )(core, buffer, mine, other)
+    here = pl.ds(pl.multiple_of(core[0] * cut, cut), cut)
+    there = pl.ds(pl.multiple_of((1 - core[0]) * cut, cut), cut)
+    first = ((0,), (0,))
+    cross[...] = dot3(buffer[here, :], mine[...], first) + dot3(buffer[there, :], other[...], first)
 
 
 def factor_kernel(gram, inverse, work):
@@ -213,29 +185,21 @@
     )(gram)
 
 
-def back_kernel(place, inverse, s0, s1, s2, s3, s4, s5, s6, s7, back, norms):
+def back_kernel(inverse, s0, s1, s2, s3, s4, s5, s6, s7, back, norms):
+    row = lax.axis_index("row")
     for n, share in enumerate((s0, s1, s2, s3, s4, s5, s6, s7)):
         height = share.shape[0]
-        start = pl.multiple_of(place[n] * height, height)
+        shift = (n + 1) // 2 if n % 2 == 0 else ROWS - (n + 1) // 2
+        start = pl.multiple_of(lax.rem(row + shift, ROWS) * height, height)
         back[pl.ds(start, height), :] = dot3(share[...], inverse[...], ((1,), (1,)))
     whole = back[...]
     norms[...] = jnp.sum(whole * whole, axis=0, keepdims=True)
 
 
-def back_and_norms(place, inverse, shares):
+def back_and_norms(inverse, shares):
     rank = inverse.shape[0]
     cols = len(shares) * shares[0].shape[0]
-    return pl.pallas_call(
-        back_kernel,
-        in_specs=[pl.BlockSpec(memory_space=pltpu.SMEM)] + [in_vmem()] * (1 + len(shares)),
-        out_specs=[in_vmem()] * 2,
-        out_shape=[
-            jax.ShapeDtypeStruct((cols, rank), jnp.float32),
-            jax.ShapeDtypeStruct((1, rank), jnp.float32),
-        ],
-        compiler_params=pltpu.CompilerParams(vmem_limit_bytes=VMEM_LIMIT),
-        name="back_and_norms",
-    )(place, inverse, *shares)
+    return call(back_kernel, "back_and_norms", [(cols, rank), (1, rank)], inverse, *shares)
 
 
 def momentum_kernel(buffer, ortho, back, new_momentum):
@@ -407,13 +371,13 @@
             return others
 
     with jax.named_scope("proj"):
+        mixed = acts.reshape(ROWS, -1, acts.shape[1])
+        mixed = lax.all_to_all(mixed, "col", 0, 0, axis_index_groups=MIXERS)
         small = jnp.dot(out_grads.astype(jnp.float32), basis, precision=high)
         small = small.reshape(GROUPS, ROWS, -1, rank).swapaxes(0, 1).reshape(COLS, -1, rank)
-        small = sum_copies(lax.all_to_all(small, "col", 0, 0), ROWS)
-        mixed = acts.reshape(ROWS, -1, acts.shape[1])
         local = jnp.dot(momentum, basis, precision=high)
         small, mixed, local = turn(1, small, mixed, local)
-        mixed = lax.all_to_all(mixed, "col", 0, 0, axis_index_groups=MIXERS)
+        small = sum_copies(lax.all_to_all(small, "col", 0, 0), ROWS)
         small, mixed = turn(2, small, mixed)
         small = lax.all_to_all(small, "row", 0, 0).reshape(-1, rank)
         part = proj_part(local, mixed.reshape(-1, acts.shape[1]), small)
@@ -437,7 +401,7 @@
         other = lax.ppermute(mine, "col", CORE_SWAP)
 
     with jax.named_scope("cross"):
-        cross = cross_part(core, buffer, mine, other)
+        cross = call(cross_kernel, "cross", (buffer.shape[1], rank), core, buffer, mine, other, scalars=1)
         cross, mine, other = lax.optimization_barrier((cross, mine, other))
         share = lax.psum_scatter(cross, "row", scatter_dimension=0, tiled=True)
 
@@ -462,7 +426,7 @@
             parts += [up, down]
         parts.append(lax.ppermute(up, "row", UP))
 
-    back, norms = back_and_norms(place, inverse, parts)
+    back, norms = back_and_norms(inverse, parts)
 
     with jax.named_scope("norms"):
         norms = jnp.sum(spread(norms, "col", COLS), axis=0)

time: 203 us -> 199 us (0.980)
  blocking collectives: 50.3 us -> 57 us
  Pallas kernels: 36.4 us -> 31.6 us
  waiting for transfers between devices: 32 us -> 27.5 us
    pallas_call x2 -> x0, Pallas kernels: 8.46 us -> none  [the longest x1 6.66 us: cross_part(): pl.pallas_call(cross_kernel, in_specs=[pl.BlockSpec(memory_space=pltpu.SM...]
    all_to_all x1, blocking collectives: 9.81 us -> 15.2 us  [on_device(): small = sum_copies(lax.all_to_all(small, 'col', 0, 0), ROWS)]
    pallas_call x5 -> x7, Pallas kernels: 3.2 us -> 7.04 us  [call(): pl.pallas_call(kernel, in_specs=[pl.BlockSpec(memory_space=pltpu.SMEM)] *...]
    all_to_all x1, starting transfers between devices: 8 us -> 10.8 us  [spread(): return lax.all_to_all(copies, axis, 0, 0, axis_index_groups=groups)]
    all_to_all x1, waiting for transfers between devices: 5.28 us -> 2.7 us  [on_device(): mixed = lax.all_to_all(mixed, 'col', 0, 0, axis_index_groups=MIXERS)]
    unnamed x38 -> x26, local copies, waits for them, and re-layouts: 9.08 us -> 8.22 us
  transfers between devices with their start and end apart: 22 -> 22, of which waited for: 10 -> 9; matrix products, arithmetic and copies ran while one was open for 5% -> 4% of each run, Pallas kernels for 12% -> 13%
where the time goes in v4:
time: 199 us; the launch traced here: 198 us
  blocking collectives  57 us (29%)
  starting transfers between devices  50.8 us (26%)
  Pallas kernels  31.6 us (16%)
  waiting for transfers between devices  27.5 us (14%)
  between operations  14.3 us (7%)
  local copies, waits for them, and re-layouts  8.95 us (4%)
  matrix products  6.42 us (3%)
    all_to_all x1, blocking collectives, on_device(): gram = lax.all_to_all(gram, 'col', 0, 0).reshape(rank, rank)  17.8 us
    all_to_all x1, blocking collectives, on_device(): small = sum_copies(lax.all_to_all(small, 'col', 0, 0), ROWS)  15.2 us
    all_to_all x1, blocking collectives, on_device(): small = lax.all_to_all(small, 'row', 0, 0).reshape(-1, rank)  12.7 us
    all_to_all x1, blocking collectives, on_device(): gram = sum_copies(lax.all_to_all(gram, 'row', 0, 0), COLS)  11.2 us
    all_to_all x1, starting transfers between devices, spread(): return lax.all_to_all(copies, axis, 0, 0, axis_index_groups=groups)  10.8 us
    pallas_call x1, Pallas kernels, add_grad(): pl.pallas_call(grad_kernel, in_specs=[pl.BlockSpec(memory_space=pltpu.SME...  9.59 us
    ppermute x3, starting transfers between devices, turn(): down = lax.ppermute(down, 'row', DOWN)  9.36 us
    pallas_call x1, Pallas kernels, inverse_factor(): pl.pallas_call(factor_kernel, out_shape=jax.ShapeDtypeStruct((n, n), jnp....  8.92 us
  transfers between devices with their start and end apart: 22, of which 9 were waited for; matrix products, arithmetic and copies ran while one was open for 4% of the time, Pallas kernels for 13%

profile of v4, /device:TPU:1, one launch (start us, length us, event | category | flops | bytes accessed | tf_op | source)
XLA Modules:
  0.0 198.0 jit_solution(1967243660925824820)
XLA Ops:
  10.5 4.0 %collective-permute-start.1 = (bf16[256,896]{1,0:T(8,128)(2,1)}, bf16[256,896]{1,0:T(8,128)(2,1)}, u32[]{:S(2)}, u32[]{:S(2)}) collective-permute-start(bf16[256,896]{1,0:T(8,128)(2,1)} %refs_0_.1), channel_id=1, source_target_pairs={{0,224},{32,0},{64,32},{96,64},{128,96},{160,128},{192,160},{224,1... | collective-permute-start | bytes 1376264 | tf_op jit(solution)/shard_map/proj/gather_grads/ppermute | solution.py:367
  14.5 6.7 %all-to-all-start = ((bf16[8,8,1024]{2,1,0:T(8,128)(2,1)}), bf16[8,8,1024]{2,1,0:T(8,128)(2,1)S(1)}, u32[]{:S(2)}, u32[]{:S(2)}) async-start(bf16[8,8,1024]{2,1,0:T(8,128)(2,1)} %bitcast.37), calls=%async_computation | async-start | bytes 262144 | tf_op jit(solution)/shard_map/proj/all_to_all | solution.py:375
  21.2 3.8 %fusion.7.local = f32[1024,256]{1,0:T(8,128)S(1)} fusion(f32[1024,896]{1,0:T(8,128)} %refs_8_.1, f32[896,256]{1,0:T(8,128)S(1)} %copy-done), kind=kOutput, calls=%fused_computation.13 | convolution fusion | flops 1409286144 | bytes 5636096 | tf_op jit(solution)/shard_map/proj/dot_general | solution.py:378
  25.5 2.7 %all-to-all-done = bf16[8,8,1024]{2,1,0:T(8,128)(2,1)S(1)} async-done(((bf16[8,8,1024]{2,1,0:T(8,128)(2,1)}), bf16[8,8,1024]{2,1,0:T(8,128)(2,1)S(1)}, u32[]{:S(2)}, u32[]{:S(2)}) %all-to-all-start) | async-done | bytes 131104 | tf_op jit(solution)/shard_map/proj/all_to_all | solution.py:375
  28.2 2.7 %collective-permute-start.3 = (bf16[256,896]{1,0:T(8,128)(2,1)}, bf16[256,896]{1,0:T(8,128)(2,1)S(1)}, u32[]{:S(2)}, u32[]{:S(2)}) collective-permute-start(bf16[256,896]{1,0:T(8,128)(2,1)} %collective-permute-done.1.refs_2_), channel_id=1, source_target_pairs={{0,224},{32,0},{64,32},{96,64},{128,96},{160,128},{192,160},{224,1... | collective-permute-start | bytes 1376264 | tf_op jit(solution)/shard_map/proj/gather_grads/ppermute | solution.py:367
  30.9 15.2 %all_to_all.40.shares = f32[32,8,256]{2,1,0:T(8,128)S(1)} all-to-all(f32[32,8,256]{2,1,0:T(8,128)S(1)} %bitcast.36), channel_id=1, replica_groups=mesh['row'=8,'col'=32] {'col'}, dimensions={0} | all-to-all | bytes 524288 | tf_op jit(solution)/shard_map/proj/all_to_all | solution.py:380
  46.3 2.7 %collective-permute-start.5 = (bf16[256,896]{1,0:T(8,128)(2,1)S(1)}, bf16[256,896]{1,0:T(8,128)(2,1)S(1)}, u32[]{:S(2)}, u32[]{:S(2)}) collective-permute-start(bf16[256,896]{1,0:T(8,128)(2,1)S(1)} %collective-permute-done.3.refs_4_), channel_id=1, source_target_pairs={{0,224},{32,0},{64,32},{96,64},{128,96},{160,128},{192,160},{224,1... | collective-permute-start | bytes 1376264 | tf_op jit(solution)/shard_map/proj/gather_grads/ppermute | solution.py:367
  49.0 12.7 %all_to_all.41 = f32[8,8,256]{2,1,0:T(8,128)S(1)} all-to-all(f32[8,8,256]{2,1,0:T(8,128)S(1)} %sum_copies.3), channel_id=1, replica_groups=mesh['row'=8,'col'=32] {'row'}, dimensions={0} | all-to-all | bytes 131072 | tf_op jit(solution)/shard_map/proj/all_to_all | solution.py:382
  67.3 3.6 %all-to-all-start.3 = ((f32[16,32,256]{2,1,0:T(8,128)}), f32[16,32,256]{2,1,0:T(8,128)S(1)}, u32[]{:S(2)}, u32[]{:S(2)}) async-start(f32[16,32,256]{2,1,0:T(8,128)} %bitcast.7), calls=%async_computation.3 | async-start | bytes 1048576 | tf_op jit(solution)/shard_map/sum_proj/all_to_all | solution.py:396
  70.9 2.8 %collective-permute-start.7 = (bf16[256,896]{1,0:T(8,128)(2,1)S(1)}, bf16[256,896]{1,0:T(8,128)(2,1)S(1)}, u32[]{:S(2)}, u32[]{:S(2)}) collective-permute-start(bf16[256,896]{1,0:T(8,128)(2,1)S(1)} %copy-done.10), channel_id=1, source_target_pairs={{0,32},{32,64},{64,96},{96,128},{128,160},{160,192},{192,224},{224... | collective-permute-start | bytes 1376264 | tf_op jit(solution)/shard_map/gather_grads/ppermute | solution.py:387
  73.8 8.3 %all-to-all-done.3.shares = f32[16,32,256]{2,1,0:T(8,128)S(1)} async-done(((f32[16,32,256]{2,1,0:T(8,128)}), f32[16,32,256]{2,1,0:T(8,128)S(1)}, u32[]{:S(2)}, u32[]{:S(2)}) %all-to-all-start.3) | async-done | bytes 524320 | tf_op jit(solution)/shard_map/sum_proj/all_to_all | solution.py:396
  82.9 3.6 %all-to-all-start.4 = ((f32[16,32,256]{2,1,0:T(8,128)}), f32[16,32,256]{2,1,0:T(8,128)S(1)}, u32[]{:S(2)}, u32[]{:S(2)}) async-start(f32[16,32,256]{2,1,0:T(8,128)} %sum_copies.4), calls=%async_computation.4 | async-start | bytes 1048576 | tf_op jit(solution)/shard_map/sum_proj/all_to_all | solution.py:399
  88.0 9.6 %add_grad.1.buffer = f32[1024,896]{1,0:T(8,128)} custom-call(s32[8]{0:T(128)} %and_select_fusion.place, bf16[2048,1024]{1,0:T(8,128)(2,1)} %all-gather.2.cloned.1.call-done.acts, bf16[256,896]{1,0:T(8,128)(2,1)} %refs_0_.1, bf16[256,896]{1,0:T(8,128)(2,1)} %collective-permute-done.refs_1_, bf16[256,896]{1,0:T(8,128)(2,1)} %collective-permute-done.1.refs_2_, ...), custom_call_target="tpu_custom_call" | custom-call | flops 3758096384 | bytes 15204352 | tf_op jit(solution)/shard_map/sum_proj/add_grad/pallas_call | solution.py:104
  102.6 2.6 %cross.1 = f32[896,256]{1,0:T(8,128)} custom-call(s32[1]{0:T(128)} %bitcast.core, f32[1024,896]{1,0:T(8,128)S(1)} %copy-done.1, f32[512,256]{1,0:T(8,128)S(1)} %bitcast.28, f32[512,256]{1,0:T(8,128)S(1)} %collective-permute-done.8.other), custom_call_target="tpu_custom_call" | custom-call | tf_op jit(solution)/shard_map/cross/cross/pallas_call | solution.py:276
  106.6 11.2 %all_to_all.42.shares = f32[8,8,256]{2,1,0:T(8,128)S(1)} all-to-all(f32[8,8,256]{2,1,0:T(8,128)S(1)} %gram.1), channel_id=1, replica_groups=mesh['row'=8,'col'=32] {'row'}, dimensions={0} | all-to-all | bytes 131072 | tf_op jit(solution)/shard_map/gram/all_to_all | solution.py:411
  117.9 17.8 %all_to_all.43 = f32[32,8,256]{2,1,0:T(8,128)} all-to-all(f32[32,8,256]{2,1,0:T(8,128)S(1)} %sum_copies.5), channel_id=1, replica_groups=mesh['row'=8,'col'=32] {'col'}, dimensions={0} | all-to-all | bytes 524288 | tf_op jit(solution)/shard_map/gram/all_to_all | solution.py:412
  135.7 8.9 %inverse_factor.1.inverse = f32[256,256]{1,0:T(8,128)} custom-call(f32[256,256]{1,0:T(8,128)} %bitcast.38), custom_call_target="tpu_custom_call" | custom-call | flops 10000000000 | bytes 524288 | tf_op jit(solution)/shard_map/inverse_factor/pallas_call | solution.py:179
  147.3 3.3 %collective-permute-done.9.s1 = f32[112,256]{1,0:T(8,128)S(1)} collective-permute-done((f32[112,256]{1,0:T(8,128)}, f32[112,256]{1,0:T(8,128)S(1)}, u32[]{:S(2)}, u32[]{:S(2)}) %collective-permute-start.9) | collective-permute-done | bytes 114720 | tf_op jit(solution)/shard_map/gather_cross/ppermute | solution.py:424
  150.5 2.7 %collective-permute-start.12 = (f32[112,256]{1,0:T(8,128)S(1)}, f32[112,256]{1,0:T(8,128)S(1)}, u32[]{:S(2)}, u32[]{:S(2)}) collective-permute-start(f32[112,256]{1,0:T(8,128)S(1)} %collective-permute-done.10.s2), channel_id=1, source_target_pairs={{0,224},{32,0},{64,32},{96,64},{128,96},{160,128},{192,160},{224,1... | collective-permute-start | bytes 344072 | tf_op jit(solution)/shard_map/gather_cross/ppermute | solution.py:425
  155.4 2.7 %collective-permute-start.14 = (f32[112,256]{1,0:T(8,128)S(1)}, f32[112,256]{1,0:T(8,128)S(1)}, u32[]{:S(2)}, u32[]{:S(2)}) collective-permute-start(f32[112,256]{1,0:T(8,128)S(1)} %collective-permute-done.12.s4), channel_id=1, source_target_pairs={{0,224},{32,0},{64,32},{96,64},{128,96},{160,128},{192,160},{224,1... | collective-permute-start | bytes 344072 | tf_op jit(solution)/shard_map/gather_cross/ppermute | solution.py:425
  161.1 4.0 %collective-permute-done.15.s7 = f32[112,256]{1,0:T(8,128)S(1)} collective-permute-done((f32[112,256]{1,0:T(8,128)S(1)}, f32[112,256]{1,0:T(8,128)S(1)}, u32[]{:S(2)}, u32[]{:S(2)}) %collective-permute-start.15) | collective-permute-done | bytes 114720 | tf_op jit(solution)/shard_map/gather_cross/ppermute | solution.py:427
  168.8 10.8 %all-to-all-start.7 = ((f32[32,1,256]{2,1,0:T(1,128)}), f32[32,1,256]{2,1,0:T(1,128)S(1)}, u32[]{:S(2)}, u32[]{:S(2)}) async-start(f32[32,1,256]{2,1,0:T(1,128)} %broadcast_in_dim.9), calls=%async_computation.8 | async-start | bytes 65536 | tf_op jit(solution)/shard_map/norms/all_to_all | solution.py:53
  183.8 2.9 %update_momentum.1 = f32[1024,896]{1,0:T(8,128)} custom-call(f32[1024,896]{1,0:T(8,128)S(1)} %copy-done.2, f32[1024,256]{1,0:T(8,128)S(1)} %fusion.ortho, f32[896,256]{1,0:T(8,128)S(1)} %get-tuple-element.43.back), custom_call_target="tpu_custom_call" | custom-call | tf_op jit(solution)/shard_map/update_momentum/pallas_call | solution.py:220
  188.4 2.7 %update_weight.1 = (bf16[1024,896]{1,0:T(8,128)(2,1)}, f32[896,256]{1,0:T(8,128)}) custom-call(bf16[1024,896]{1,0:T(8,128)(2,1)S(1)} %copy-done.3, f32[1024,256]{1,0:T(8,128)S(1)} %fusion.ortho, f32[896,256]{1,0:T(8,128)S(1)} %get-tuple-element.43.back, f32[1,256]{1,0:T(1,128)S(1)} %bitcast.33), custom_call_target="tpu_custom_call" | custom-call | tf_op jit(solution)/shard_map/update_weight/pallas_call | solution.py:256
  (74 shorter events, 35.9 us)
Async XLA Ops:
  7.2 17.8 %copy-start.6 = (bf16[256,896]{1,0:T(8,128)(2,1)S(1)}, bf16[256,896]{1,0:T(8,128)(2,1)}, u32[]{:S(2)}) copy-start(bf16[256,896]{1,0:T(8,128)(2,1)} %refs_0_.1) | copy-start | bytes 1376260
  7.2 80.1 %all-gather.2.cloned.1.call-start = ((), (), s32[]{:S(2)}) async-start(), calls=%async_computation.9 | async-start | bytes 4325376 | tf_op jit(solution)/shard_map/gather_acts/all_gather | solution.py:358
  7.9 20.3 %collective-permute-start = (bf16[256,896]{1,0:T(8,128)(2,1)}, bf16[256,896]{1,0:T(8,128)(2,1)}, u32[]{:S(2)}, u32[]{:S(2)}) collective-permute-start(bf16[256,896]{1,0:T(8,128)(2,1)} %refs_0_.1), channel_id=1, source_target_pairs={{0,32},{32,64},{64,96},{96,128},{128,160},{160,192},{192,224},{224... | collective-permute-start | bytes 1376264 | tf_op jit(solution)/shard_map/proj/gather_grads/ppermute | solution.py:366
  10.5 17.7 %collective-permute-start.1 = (bf16[256,896]{1,0:T(8,128)(2,1)}, bf16[256,896]{1,0:T(8,128)(2,1)}, u32[]{:S(2)}, u32[]{:S(2)}) collective-permute-start(bf16[256,896]{1,0:T(8,128)(2,1)} %refs_0_.1), channel_id=1, source_target_pairs={{0,224},{32,0},{64,32},{96,64},{128,96},{160,128},{192,160},{224,1... | collective-permute-start | bytes 1376264 | tf_op jit(solution)/shard_map/proj/gather_grads/ppermute | solution.py:367
  14.5 13.7 %all-to-all-start = ((bf16[8,8,1024]{2,1,0:T(8,128)(2,1)}), bf16[8,8,1024]{2,1,0:T(8,128)(2,1)S(1)}, u32[]{:S(2)}, u32[]{:S(2)}) async-start(bf16[8,8,1024]{2,1,0:T(8,128)(2,1)} %bitcast.37), calls=%async_computation | async-start | bytes 262144 | tf_op jit(solution)/shard_map/proj/all_to_all | solution.py:375
  28.2 18.0 %collective-permute-start.2 = (bf16[256,896]{1,0:T(8,128)(2,1)}, bf16[256,896]{1,0:T(8,128)(2,1)S(1)}, u32[]{:S(2)}, u32[]{:S(2)}) collective-permute-start(bf16[256,896]{1,0:T(8,128)(2,1)} %collective-permute-done.refs_1_), channel_id=1, source_target_pairs={{0,32},{32,64},{64,96},{96,128},{128,160},{160,192},{192,224},{224... | collective-permute-start | bytes 1376264 | tf_op jit(solution)/shard_map/proj/gather_grads/ppermute | solution.py:366
  28.2 18.0 %collective-permute-start.3 = (bf16[256,896]{1,0:T(8,128)(2,1)}, bf16[256,896]{1,0:T(8,128)(2,1)S(1)}, u32[]{:S(2)}, u32[]{:S(2)}) collective-permute-start(bf16[256,896]{1,0:T(8,128)(2,1)} %collective-permute-done.1.refs_2_), channel_id=1, source_target_pairs={{0,224},{32,0},{64,32},{96,64},{128,96},{160,128},{192,160},{224,1... | collective-permute-start | bytes 1376264 | tf_op jit(solution)/shard_map/proj/gather_grads/ppermute | solution.py:367
  46.2 16.0 %copy-start.8 = (bf16[256,896]{1,0:T(8,128)(2,1)}, bf16[256,896]{1,0:T(8,128)(2,1)S(1)}, u32[]{:S(2)}) copy-start(bf16[256,896]{1,0:T(8,128)(2,1)S(1)} %collective-permute-done.3.refs_4_) | copy-start | bytes 1376260
  46.2 16.0 %collective-permute-start.4 = (bf16[256,896]{1,0:T(8,128)(2,1)S(1)}, bf16[256,896]{1,0:T(8,128)(2,1)S(1)}, u32[]{:S(2)}, u32[]{:S(2)}) collective-permute-start(bf16[256,896]{1,0:T(8,128)(2,1)S(1)} %collective-permute-done.2.refs_3_), channel_id=1, source_target_pairs={{0,32},{32,64},{64,96},{96,128},{128,160},{160,192},{192,224},{224... | collective-permute-start | bytes 1376264 | tf_op jit(solution)/shard_map/proj/gather_grads/ppermute | solution.py:366
  46.3 15.9 %collective-permute-start.5 = (bf16[256,896]{1,0:T(8,128)(2,1)S(1)}, bf16[256,896]{1,0:T(8,128)(2,1)S(1)}, u32[]{:S(2)}, u32[]{:S(2)}) collective-permute-start(bf16[256,896]{1,0:T(8,128)(2,1)S(1)} %collective-permute-done.3.refs_4_), channel_id=1, source_target_pairs={{0,224},{32,0},{64,32},{96,64},{128,96},{160,128},{192,160},{224,1... | collective-permute-start | bytes 1376264 | tf_op jit(solution)/shard_map/proj/gather_grads/ppermute | solution.py:367
  62.2 4.2 %collective-permute-start.6 = (f32[1024,256]{1,0:T(8,128)S(1)}, f32[1024,256]{1,0:T(8,128)S(1)}, u32[]{:S(2)}, u32[]{:S(2)}) collective-permute-start(f32[1024,256]{1,0:T(8,128)S(1)} %proj_part.1.part), channel_id=1, source_target_pairs={{0,1},{1,0},{2,3},{3,2},{4,5},{5,4},{6,7},{7,6},{8,9},{9,8},{10,11... | collective-permute-start | bytes 3145736 | tf_op jit(solution)/shard_map/sum_proj/ppermute | solution.py:393
  67.3 14.7 %all-to-all-start.3 = ((f32[16,32,256]{2,1,0:T(8,128)}), f32[16,32,256]{2,1,0:T(8,128)S(1)}, u32[]{:S(2)}, u32[]{:S(2)}) async-start(f32[16,32,256]{2,1,0:T(8,128)} %bitcast.7), calls=%async_computation.3 | async-start | bytes 1048576 | tf_op jit(solution)/shard_map/sum_proj/all_to_all | solution.py:396
  70.9 16.4 %collective-permute-start.7 = (bf16[256,896]{1,0:T(8,128)(2,1)S(1)}, bf16[256,896]{1,0:T(8,128)(2,1)S(1)}, u32[]{:S(2)}, u32[]{:S(2)}) collective-permute-start(bf16[256,896]{1,0:T(8,128)(2,1)S(1)} %copy-done.10), channel_id=1, source_target_pairs={{0,32},{32,64},{64,96},{96,128},{128,160},{160,192},{192,224},{224... | collective-permute-start | bytes 1376264 | tf_op jit(solution)/shard_map/gather_grads/ppermute | solution.py:387
  82.9 14.7 %all-to-all-start.4 = ((f32[16,32,256]{2,1,0:T(8,128)}), f32[16,32,256]{2,1,0:T(8,128)S(1)}, u32[]{:S(2)}, u32[]{:S(2)}) async-start(f32[16,32,256]{2,1,0:T(8,128)} %sum_copies.4), calls=%async_computation.4 | async-start | bytes 1048576 | tf_op jit(solution)/shard_map/sum_proj/all_to_all | solution.py:399
  86.5 58.1 %reduce-scatter.2.cloned.1.call-start = ((), (), s32[]{:S(2)}) async-start(), calls=%async_computation.10 | async-start | bytes 1032192 | tf_op jit(solution)/shard_map/cross/reduce_scatter | solution.py:406
  97.7 2.9 %collective-permute-start.8 = (f32[512,256]{1,0:T(8,128)S(1)}, f32[512,256]{1,0:T(8,128)S(1)}, u32[]{:S(2)}, u32[]{:S(2)}) collective-permute-start(f32[512,256]{1,0:T(8,128)S(1)} %bitcast.27), channel_id=1, source_target_pairs={{0,1},{1,0},{2,3},{3,2},{4,5},{5,4},{6,7},{7,6},{8,9},{9,8},{10,11... | collective-permute-start | bytes 1572872 | tf_op jit(solution)/shard_map/sum_proj/ppermute | solution.py:401
  144.6 5.9 %collective-permute-start.9 = (f32[112,256]{1,0:T(8,128)}, f32[112,256]{1,0:T(8,128)S(1)}, u32[]{:S(2)}, u32[]{:S(2)}) collective-permute-start(f32[112,256]{1,0:T(8,128)} %reduce-scatter.2.cloned.1.call-done.s0), channel_id=1, source_target_pairs={{0,32},{32,64},{64,96},{96,128},{128,160},{160,192},{192,224},{224... | collective-permute-start | bytes 344072 | tf_op jit(solution)/shard_map/gather_cross/ppermute | solution.py:424
  145.0 5.5 %collective-permute-start.10 = (f32[112,256]{1,0:T(8,128)}, f32[112,256]{1,0:T(8,128)S(1)}, u32[]{:S(2)}, u32[]{:S(2)}) collective-permute-start(f32[112,256]{1,0:T(8,128)} %reduce-scatter.2.cloned.1.call-done.s0), channel_id=1, source_target_pairs={{0,224},{32,0},{64,32},{96,64},{128,96},{160,128},{192,160},{224,1... | collective-permute-start | bytes 344072 | tf_op jit(solution)/shard_map/gather_cross/ppermute | solution.py:425
  150.5 4.9 %collective-permute-start.11 = (f32[112,256]{1,0:T(8,128)S(1)}, f32[112,256]{1,0:T(8,128)S(1)}, u32[]{:S(2)}, u32[]{:S(2)}) collective-permute-start(f32[112,256]{1,0:T(8,128)S(1)} %collective-permute-done.9.s1), channel_id=1, source_target_pairs={{0,32},{32,64},{64,96},{96,128},{128,160},{160,192},{192,224},{224... | collective-permute-start | bytes 344072 | tf_op jit(solution)/shard_map/gather_cross/ppermute | solution.py:424
  150.5 4.9 %collective-permute-start.12 = (f32[112,256]{1,0:T(8,128)S(1)}, f32[112,256]{1,0:T(8,128)S(1)}, u32[]{:S(2)}, u32[]{:S(2)}) collective-permute-start(f32[112,256]{1,0:T(8,128)S(1)} %collective-permute-done.10.s2), channel_id=1, source_target_pairs={{0,224},{32,0},{64,32},{96,64},{128,96},{160,128},{192,160},{224,1... | collective-permute-start | bytes 344072 | tf_op jit(solution)/shard_map/gather_cross/ppermute | solution.py:425
  155.4 4.9 %collective-permute-start.13 = (f32[112,256]{1,0:T(8,128)S(1)}, f32[112,256]{1,0:T(8,128)S(1)}, u32[]{:S(2)}, u32[]{:S(2)}) collective-permute-start(f32[112,256]{1,0:T(8,128)S(1)} %collective-permute-done.11.s3), channel_id=1, source_target_pairs={{0,32},{32,64},{64,96},{96,128},{128,160},{160,192},{192,224},{224... | collective-permute-start | bytes 344072 | tf_op jit(solution)/shard_map/gather_cross/ppermute | solution.py:424
  155.4 5.7 %collective-permute-start.14 = (f32[112,256]{1,0:T(8,128)S(1)}, f32[112,256]{1,0:T(8,128)S(1)}, u32[]{:S(2)}, u32[]{:S(2)}) collective-permute-start(f32[112,256]{1,0:T(8,128)S(1)} %collective-permute-done.12.s4), channel_id=1, source_target_pairs={{0,224},{32,0},{64,32},{96,64},{128,96},{160,128},{192,160},{224,1... | collective-permute-start | bytes 344072 | tf_op jit(solution)/shard_map/gather_cross/ppermute | solution.py:425
  160.2 4.9 %collective-permute-start.15 = (f32[112,256]{1,0:T(8,128)S(1)}, f32[112,256]{1,0:T(8,128)S(1)}, u32[]{:S(2)}, u32[]{:S(2)}) collective-permute-start(f32[112,256]{1,0:T(8,128)S(1)} %collective-permute-done.13.s5), channel_id=1, source_target_pairs={{0,32},{32,64},{64,96},{96,128},{128,160},{160,192},{192,224},{224... | collective-permute-start | bytes 344072 | tf_op jit(solution)/shard_map/gather_cross/ppermute | solution.py:427
  168.8 18.0 %all-to-all-start.7 = ((f32[32,1,256]{2,1,0:T(1,128)}), f32[32,1,256]{2,1,0:T(1,128)S(1)}, u32[]{:S(2)}, u32[]{:S(2)}) async-start(f32[32,1,256]{2,1,0:T(1,128)} %broadcast_in_dim.9), calls=%async_computation.8 | async-start | bytes 65536 | tf_op jit(solution)/shard_map/norms/all_to_all | solution.py:53
  (11 other events, 48.7 us)
Sparse Core Ops, SparseCore 0:
  10.6 56.3 all-gather.1
  105.3 32.8 reduce-scatter.1

commit v5 on v4

--- a/solution.py
+++ b/solution.py
@@ -19,7 +19,7 @@
 COLS = 32
 CHIPS = 16
 VMEM_LIMIT = 24 * 1024 * 1024
-VMEM_MOST = 60 * 1024 * 1024
+VMEM_MORE = 44 * 1024 * 1024
 BLOCK = 64
 STEP = 16
 TILES = 4
@@ -112,7 +112,7 @@
             pltpu.VMEM((rows, cols), jnp.float32),
             pltpu.SemaphoreType.DMA((len(pieces) + 3 * TILES,)),
         ],
-        compiler_params=pltpu.CompilerParams(vmem_limit_bytes=VMEM_MOST),
+        compiler_params=pltpu.CompilerParams(vmem_limit_bytes=VMEM_MORE),
         cost_estimate=pl.CostEstimate(
             flops=2 * tokens * rows * cols,
             bytes_accessed=2 * tokens * (rows + cols) + 8 * rows * cols,
@@ -202,30 +202,43 @@
     return call(back_kernel, "back_and_norms", [(cols, rank), (1, rank)], inverse, *shares)
 
 
-def momentum_kernel(buffer, ortho, back, new_momentum):
-    fix = lax.dot_general(
-        ortho[...].astype(jnp.bfloat16),
-        back[...].astype(jnp.bfloat16),
-        (((1,), (1,)), ((), ())),
-        preferred_element_type=jnp.float32,
-    )
-    new_momentum[...] = buffer[...] - (1.0 - keep_rate) * fix
-
-
-def update_momentum(buffer, ortho, back):
+def momentum_kernel(buffer, ortho, back, weight, new_momentum, held, moved, sems):
+    fetch = pltpu.make_async_copy(weight, held, sems.at[TILES])
+    fetch.start()
+    right = back[...].astype(jnp.bfloat16)
+    tile = buffer.shape[0] // TILES
+    stores = []
+    for n in range(TILES):
+        span = slice(n * tile, (n + 1) * tile)
+        fix = lax.dot_general(
+            ortho[span, :].astype(jnp.bfloat16),
+            right,
+            (((1,), (1,)), ((), ())),
+            preferred_element_type=jnp.float32,
+        )
+        moved[span, :] = buffer[span, :] - (1.0 - keep_rate) * fix
+        stores.append(pltpu.make_async_copy(moved.at[span, :], new_momentum.at[span, :], sems.at[n]))
+        stores[-1].start()
+    for copy in stores:
+        copy.wait()
+    fetch.wait()
+
+
+def update_momentum(buffer, ortho, back, weight):
     rows, cols = buffer.shape
-    rank = ortho.shape[1]
-    tile = rows // TILES
-    part = lambda width: pl.BlockSpec((tile, width), lambda i: (i, 0))
+    anywhere = pl.BlockSpec(memory_space=pl.ANY)
     return pl.pallas_call(
         momentum_kernel,
-        grid=(TILES,),
-        in_specs=[part(cols), part(rank), pl.BlockSpec(back.shape, lambda i: (0, 0))],
-        out_specs=part(cols),
-        out_shape=jax.ShapeDtypeStruct((rows, cols), jnp.float32),
+        in_specs=[in_vmem()] * 3 + [anywhere],
+        out_specs=[anywhere, in_vmem()],
+        out_shape=[
+            jax.ShapeDtypeStruct((rows, cols), jnp.float32),
+            jax.ShapeDtypeStruct(weight.shape, weight.dtype),
+        ],
+        scratch_shapes=[pltpu.VMEM((rows, cols), jnp.float32), pltpu.SemaphoreType.DMA((TILES + 1,))],
         compiler_params=pltpu.CompilerParams(vmem_limit_bytes=VMEM_LIMIT),
         name="update_momentum",
-    )(buffer, ortho, back)
+    )(buffer, ortho, back, weight)
 
 
 def weight_kernel(weight, ortho, back, scale, new_weight, new_basis, basis, stepped, sems):
@@ -420,9 +433,11 @@
     with jax.named_scope("gather_cross"):
         parts = [share]
         up = down = share
-        for _ in range(1, ROWS // 2):
+        for step in range(1, ROWS // 2):
             up = lax.ppermute(up, "row", UP)
             down = lax.ppermute(down, "row", DOWN)
+            if step == 1:
+                up, down, ortho = lax.optimization_barrier((up, down, ortho))
             parts += [up, down]
         parts.append(lax.ppermute(up, "row", UP))
 
@@ -432,7 +447,7 @@
         norms = jnp.sum(spread(norms, "col", COLS), axis=0)
         scale = 1.0 / jnp.sqrt(norms + norm_eps)
 
-    new_momentum = update_momentum(buffer, ortho, back)
+    new_momentum, weight = update_momentum(buffer, ortho, back, weight)
     new_weight, new_basis = update_weight(weight, ortho, back, scale)
     return (new_weight, new_momentum, new_basis)
 

time: 199 us -> 209 us (1.050)
  blocking collectives: 57 us -> 28.8 us
  local copies, waits for them, and re-layouts: 8.95 us -> 22.8 us
  waiting for transfers between devices: 27.5 us -> 41 us
  starting transfers between devices: 50.8 us -> 61.8 us
    all_to_all x2 -> x0, blocking collectives: 29 us -> none  [the longest x1 17.8 us: on_device(): gram = lax.all_to_all(gram, 'col', 0, 0).reshape(rank, rank)]
    all_to_all x0 -> x2, waiting for transfers between devices: none -> 16 us  [the longest x1 8.81 us: on_device(): gram = lax.all_to_all(gram, 'col', 0, 0).reshape(rank, rank)]
    all_to_all x0 -> x2, starting transfers between devices: none -> 13.3 us  [the longest x1 9.09 us: on_device(): gram = lax.all_to_all(gram, 'col', 0, 0).reshape(rank, rank)]
    unnamed x26 -> x50, local copies, waits for them, and re-layouts: 8.22 us -> 21.3 us
    all_to_all x1, starting transfers between devices: 10.8 us -> 8 us  [spread(): return lax.all_to_all(copies, axis, 0, 0, axis_index_groups=groups)]
  transfers between devices with their start and end apart: 22 -> 24, of which waited for: 9 -> 11; matrix products, arithmetic and copies ran while one was open for 4% -> 3% of each run, Pallas kernels for 13% -> 12%
where the time goes in v5:
time: 209 us; the launch traced here: 208 us
  starting transfers between devices  61.8 us (30%)
  waiting for transfers between devices  41 us (20%)
  Pallas kernels  32.3 us (15%)
  blocking collectives  28.8 us (14%)
  local copies, waits for them, and re-layouts  22.8 us (11%)
  between operations  14.4 us (7%)
  matrix products  6.25 us (3%)
    unnamed x50, local copies, waits for them, and re-layouts  21.3 us
    all_to_all x1, blocking collectives, on_device(): small = sum_copies(lax.all_to_all(small, 'col', 0, 0), ROWS)  16.1 us
    all_to_all x1, blocking collectives, on_device(): small = lax.all_to_all(small, 'row', 0, 0).reshape(-1, rank)  12.8 us
    pallas_call x1, Pallas kernels, add_grad(): pl.pallas_call(grad_kernel, in_specs=[pl.BlockSpec(memory_space=pltpu.SME...  9.53 us
    ppermute x3, starting transfers between devices, turn(): down = lax.ppermute(down, 'row', DOWN)  9.35 us
    all_to_all x1, starting transfers between devices, on_device(): gram = lax.all_to_all(gram, 'col', 0, 0).reshape(rank, rank)  9.09 us
    pallas_call x1, Pallas kernels, inverse_factor(): pl.pallas_call(factor_kernel, out_shape=jax.ShapeDtypeStruct((n, n), jnp....  8.91 us
    all_to_all x1, waiting for transfers between devices, on_device(): gram = lax.all_to_all(gram, 'col', 0, 0).reshape(rank, rank)  8.81 us
  transfers between devices with their start and end apart: 24, of which 11 were waited for; matrix products, arithmetic and copies ran while one was open for 3% of the time, Pallas kernels for 12%

profile of v5, /device:TPU:1, one launch (start us, length us, event | category | flops | bytes accessed | tf_op | source)
XLA Modules:
  0.0 207.5 jit_solution(15891201116948774905)
XLA Ops:
  7.9 2.5 %collective-permute-start = (bf16[256,896]{1,0:T(8,128)(2,1)}, bf16[256,896]{1,0:T(8,128)(2,1)S(1)}, u32[]{:S(2)}, u32[]{:S(2)}) collective-permute-start(bf16[256,896]{1,0:T(8,128)(2,1)} %refs_0_.1), channel_id=1, source_target_pairs={{0,32},{32,64},{64,96},{96,128},{128,160},{160,192},{192,224},{224... | collective-permute-start | bytes 1376264 | tf_op jit(solution)/shard_map/proj/gather_grads/ppermute | solution.py:379
  10.5 4.0 %collective-permute-start.1 = (bf16[256,896]{1,0:T(8,128)(2,1)}, bf16[256,896]{1,0:T(8,128)(2,1)S(1)}, u32[]{:S(2)}, u32[]{:S(2)}) collective-permute-start(bf16[256,896]{1,0:T(8,128)(2,1)} %refs_0_.1), channel_id=1, source_target_pairs={{0,224},{32,0},{64,32},{96,64},{128,96},{160,128},{192,160},{224,1... | collective-permute-start | bytes 1376264 | tf_op jit(solution)/shard_map/proj/gather_grads/ppermute | solution.py:380
  14.5 6.7 %all-to-all-start = ((bf16[8,8,1024]{2,1,0:T(8,128)(2,1)}), bf16[8,8,1024]{2,1,0:T(8,128)(2,1)S(1)}, u32[]{:S(2)}, u32[]{:S(2)}) async-start(bf16[8,8,1024]{2,1,0:T(8,128)(2,1)} %bitcast.37), calls=%async_computation | async-start | bytes 262144 | tf_op jit(solution)/shard_map/proj/all_to_all | solution.py:388
  21.2 3.8 %fusion.7.local = f32[1024,256]{1,0:T(8,128)S(1)} fusion(f32[1024,896]{1,0:T(8,128)} %refs_8_.1, f32[896,256]{1,0:T(8,128)S(1)} %copy-done), kind=kOutput, calls=%fused_computation.13 | convolution fusion | flops 1409286144 | bytes 5636096 | tf_op jit(solution)/shard_map/proj/dot_general | solution.py:391
  28.3 2.7 %collective-permute-start.3 = (bf16[256,896]{1,0:T(8,128)(2,1)S(1)}, bf16[256,896]{1,0:T(8,128)(2,1)S(1)}, u32[]{:S(2)}, u32[]{:S(2)}) collective-permute-start(bf16[256,896]{1,0:T(8,128)(2,1)S(1)} %collective-permute-done.1.refs_2_), channel_id=1, source_target_pairs={{0,224},{32,0},{64,32},{96,64},{128,96},{160,128},{192,160},{224,1... | collective-permute-start | bytes 1376264 | tf_op jit(solution)/shard_map/proj/gather_grads/ppermute | solution.py:380
  31.7 16.1 %all_to_all.40.shares = f32[32,8,256]{2,1,0:T(8,128)S(1)} all-to-all(f32[32,8,256]{2,1,0:T(8,128)} %bitcast.36), channel_id=1, replica_groups=mesh['row'=8,'col'=32] {'col'}, dimensions={0} | all-to-all | bytes 524288 | tf_op jit(solution)/shard_map/proj/all_to_all | solution.py:393
  48.0 2.7 %collective-permute-start.5 = (bf16[256,896]{1,0:T(8,128)(2,1)S(1)}, bf16[256,896]{1,0:T(8,128)(2,1)S(1)}, u32[]{:S(2)}, u32[]{:S(2)}) collective-permute-start(bf16[256,896]{1,0:T(8,128)(2,1)S(1)} %collective-permute-done.3.refs_4_), channel_id=1, source_target_pairs={{0,224},{32,0},{64,32},{96,64},{128,96},{160,128},{192,160},{224,1... | collective-permute-start | bytes 1376264 | tf_op jit(solution)/shard_map/proj/gather_grads/ppermute | solution.py:380
  50.6 12.8 %all_to_all.41 = f32[8,8,256]{2,1,0:T(8,128)S(1)} all-to-all(f32[8,8,256]{2,1,0:T(8,128)S(1)} %sum_copies.3), channel_id=1, replica_groups=mesh['row'=8,'col'=32] {'row'}, dimensions={0} | all-to-all | bytes 131072 | tf_op jit(solution)/shard_map/proj/all_to_all | solution.py:395
  70.4 3.6 %all-to-all-start.3 = ((f32[16,32,256]{2,1,0:T(8,128)}), f32[16,32,256]{2,1,0:T(8,128)S(1)}, u32[]{:S(2)}, u32[]{:S(2)}) async-start(f32[16,32,256]{2,1,0:T(8,128)} %bitcast.7), calls=%async_computation.3 | async-start | bytes 1048576 | tf_op jit(solution)/shard_map/sum_proj/all_to_all | solution.py:409
  74.0 3.0 %collective-permute-start.7 = (bf16[256,896]{1,0:T(8,128)(2,1)}, bf16[256,896]{1,0:T(8,128)(2,1)S(1)}, u32[]{:S(2)}, u32[]{:S(2)}) collective-permute-start(bf16[256,896]{1,0:T(8,128)(2,1)} %copy-done.19), channel_id=1, source_target_pairs={{0,32},{32,64},{64,96},{96,128},{128,160},{160,192},{192,224},{224... | collective-permute-start | bytes 1376264 | tf_op jit(solution)/shard_map/gather_grads/ppermute | solution.py:400
  77.1 7.7 %all-to-all-done.3.shares = f32[16,32,256]{2,1,0:T(8,128)S(1)} async-done(((f32[16,32,256]{2,1,0:T(8,128)}), f32[16,32,256]{2,1,0:T(8,128)S(1)}, u32[]{:S(2)}, u32[]{:S(2)}) %all-to-all-start.3) | async-done | bytes 524320 | tf_op jit(solution)/shard_map/sum_proj/all_to_all | solution.py:409
  85.7 3.6 %all-to-all-start.4 = ((f32[16,32,256]{2,1,0:T(8,128)}), f32[16,32,256]{2,1,0:T(8,128)S(1)}, u32[]{:S(2)}, u32[]{:S(2)}) async-start(f32[16,32,256]{2,1,0:T(8,128)} %sum_copies.4), calls=%async_computation.4 | async-start | bytes 1048576 | tf_op jit(solution)/shard_map/sum_proj/all_to_all | solution.py:412
  95.7 9.5 %add_grad.1.buffer = f32[1024,896]{1,0:T(8,128)S(1)} custom-call(s32[8]{0:T(128)S(1)} %and_select_fusion.place, bf16[2048,1024]{1,0:T(8,128)(2,1)} %all-gather.2.cloned.1.call-done.acts, bf16[256,896]{1,0:T(8,128)(2,1)S(1)} %copy-done.7, bf16[256,896]{1,0:T(8,128)(2,1)S(1)} %copy-done.12, bf16[256,896]{1,0:T(8,128)(2,1)S(1)} %copy-done.14, ...), custom_call_target="tpu_custom_call" | custom-call | flops 3758096384 | bytes 15204352 | tf_op jit(solution)/shard_map/sum_proj/add_grad/pallas_call | solution.py:104
  112.3 2.6 %cross.1 = f32[896,256]{1,0:T(8,128)} custom-call(s32[1]{0:T(128)} %bitcast.core, f32[1024,896]{1,0:T(8,128)S(1)} %copy-done.2, f32[512,256]{1,0:T(8,128)S(1)} %bitcast.28, f32[512,256]{1,0:T(8,128)S(1)} %collective-permute-done.8.other), custom_call_target="tpu_custom_call" | custom-call | tf_op jit(solution)/shard_map/cross/cross/pallas_call | solution.py:289
  116.9 4.2 %all-to-all-start.5 = ((f32[8,8,256]{2,1,0:T(8,128)}), f32[8,8,256]{2,1,0:T(8,128)S(1)}, u32[]{:S(2)}, u32[]{:S(2)}) async-start(f32[8,8,256]{2,1,0:T(8,128)} %gram.1), calls=%async_computation.6 | async-start | bytes 131072 | tf_op jit(solution)/shard_map/gram/all_to_all | solution.py:424
  121.2 7.2 %all-to-all-done.5.shares = f32[8,8,256]{2,1,0:T(8,128)S(1)} async-done(((f32[8,8,256]{2,1,0:T(8,128)}), f32[8,8,256]{2,1,0:T(8,128)S(1)}, u32[]{:S(2)}, u32[]{:S(2)}) %all-to-all-start.5) | async-done | bytes 65568 | tf_op jit(solution)/shard_map/gram/all_to_all | solution.py:424
  129.1 9.1 %all-to-all-start.6 = ((f32[32,8,256]{2,1,0:T(8,128)}), f32[32,8,256]{2,1,0:T(8,128)S(1)}, u32[]{:S(2)}, u32[]{:S(2)}) async-start(f32[32,8,256]{2,1,0:T(8,128)} %sum_copies.5), calls=%async_computation.7 | async-start | bytes 524288 | tf_op jit(solution)/shard_map/gram/all_to_all | solution.py:425
  138.3 8.8 %all-to-all-done.6 = f32[32,8,256]{2,1,0:T(8,128)S(1)} async-done(((f32[32,8,256]{2,1,0:T(8,128)}), f32[32,8,256]{2,1,0:T(8,128)S(1)}, u32[]{:S(2)}, u32[]{:S(2)}) %all-to-all-start.6) | async-done | bytes 262176 | tf_op jit(solution)/shard_map/gram/all_to_all | solution.py:425
  147.8 8.9 %inverse_factor.1.inverse = f32[256,256]{1,0:T(8,128)} custom-call(f32[256,256]{1,0:T(8,128)} %bitcast.38), custom_call_target="tpu_custom_call" | custom-call | flops 10000000000 | bytes 524288 | tf_op jit(solution)/shard_map/inverse_factor/pallas_call | solution.py:179
  162.7 2.7 %collective-permute-start.12 = (f32[112,256]{1,0:T(8,128)S(1)}, f32[112,256]{1,0:T(8,128)S(1)}, u32[]{:S(2)}, u32[]{:S(2)}) collective-permute-start(f32[112,256]{1,0:T(8,128)S(1)} %collective-permute-done.10.s2), channel_id=1, source_target_pairs={{0,224},{32,0},{64,32},{96,64},{128,96},{160,128},{192,160},{224,1... | collective-permute-start | bytes 344072 | tf_op jit(solution)/shard_map/gather_cross/ppermute | solution.py:438
  167.5 2.7 %collective-permute-start.14 = (f32[112,256]{1,0:T(8,128)S(1)}, f32[112,256]{1,0:T(8,128)S(1)}, u32[]{:S(2)}, u32[]{:S(2)}) collective-permute-start(f32[112,256]{1,0:T(8,128)S(1)} %collective-permute-done.12.s4), channel_id=1, source_target_pairs={{0,224},{32,0},{64,32},{96,64},{128,96},{160,128},{192,160},{224,1... | collective-permute-start | bytes 344072 | tf_op jit(solution)/shard_map/gather_cross/ppermute | solution.py:438
  172.4 4.8 %collective-permute-done.15.s7 = f32[112,256]{1,0:T(8,128)S(1)} collective-permute-done((f32[112,256]{1,0:T(8,128)S(1)}, f32[112,256]{1,0:T(8,128)S(1)}, u32[]{:S(2)}, u32[]{:S(2)}) %collective-permute-start.15) | collective-permute-done | bytes 114720 | tf_op jit(solution)/shard_map/gather_cross/ppermute | solution.py:442
  181.0 8.0 %all-to-all-start.7 = ((f32[32,1,256]{2,1,0:T(1,128)}), f32[32,1,256]{2,1,0:T(1,128)S(1)}, u32[]{:S(2)}, u32[]{:S(2)}) async-start(f32[32,1,256]{2,1,0:T(1,128)} %broadcast_in_dim.9), calls=%async_computation.8 | async-start | bytes 65536 | tf_op jit(solution)/shard_map/norms/all_to_all | solution.py:53
  197.9 2.7 %update_weight.1 = (bf16[1024,896]{1,0:T(8,128)(2,1)}, f32[896,256]{1,0:T(8,128)}) custom-call(bf16[1024,896]{1,0:T(8,128)(2,1)S(1)} %copy-done.6, f32[1024,256]{1,0:T(8,128)S(1)} %fusion.ortho, f32[896,256]{1,0:T(8,128)S(1)} %get-tuple-element.51.back, f32[1,256]{1,0:T(1,128)S(1)} %bitcast.33), custom_call_target="tpu_custom_call" | custom-call | tf_op jit(solution)/shard_map/update_weight/pallas_call | solution.py:269
  (100 shorter events, 52.8 us)
Async XLA Ops:
  7.2 82.3 %all-gather.2.cloned.1.call-start = ((), (), s32[]{:S(2)}) async-start(), calls=%async_computation.9 | async-start | bytes 4325376 | tf_op jit(solution)/shard_map/gather_acts/all_gather | solution.py:371
  7.9 20.3 %collective-permute-start = (bf16[256,896]{1,0:T(8,128)(2,1)}, bf16[256,896]{1,0:T(8,128)(2,1)S(1)}, u32[]{:S(2)}, u32[]{:S(2)}) collective-permute-start(bf16[256,896]{1,0:T(8,128)(2,1)} %refs_0_.1), channel_id=1, source_target_pairs={{0,32},{32,64},{64,96},{96,128},{128,160},{160,192},{192,224},{224... | collective-permute-start | bytes 1376264 | tf_op jit(solution)/shard_map/proj/gather_grads/ppermute | solution.py:379
  10.5 17.7 %collective-permute-start.1 = (bf16[256,896]{1,0:T(8,128)(2,1)}, bf16[256,896]{1,0:T(8,128)(2,1)S(1)}, u32[]{:S(2)}, u32[]{:S(2)}) collective-permute-start(bf16[256,896]{1,0:T(8,128)(2,1)} %refs_0_.1), channel_id=1, source_target_pairs={{0,224},{32,0},{64,32},{96,64},{128,96},{160,128},{192,160},{224,1... | collective-permute-start | bytes 1376264 | tf_op jit(solution)/shard_map/proj/gather_grads/ppermute | solution.py:380
  14.5 13.7 %all-to-all-start = ((bf16[8,8,1024]{2,1,0:T(8,128)(2,1)}), bf16[8,8,1024]{2,1,0:T(8,128)(2,1)S(1)}, u32[]{:S(2)}, u32[]{:S(2)}) async-start(bf16[8,8,1024]{2,1,0:T(8,128)(2,1)} %bitcast.37), calls=%async_computation | async-start | bytes 262144 | tf_op jit(solution)/shard_map/proj/all_to_all | solution.py:388
  28.2 19.6 %collective-permute-start.2 = (bf16[256,896]{1,0:T(8,128)(2,1)S(1)}, bf16[256,896]{1,0:T(8,128)(2,1)S(1)}, u32[]{:S(2)}, u32[]{:S(2)}) collective-permute-start(bf16[256,896]{1,0:T(8,128)(2,1)S(1)} %collective-permute-done.refs_1_), channel_id=1, source_target_pairs={{0,32},{32,64},{64,96},{96,128},{128,160},{160,192},{192,224},{224... | collective-permute-start | bytes 1376264 | tf_op jit(solution)/shard_map/proj/gather_grads/ppermute | solution.py:379
  28.3 19.6 %collective-permute-start.3 = (bf16[256,896]{1,0:T(8,128)(2,1)S(1)}, bf16[256,896]{1,0:T(8,128)(2,1)S(1)}, u32[]{:S(2)}, u32[]{:S(2)}) collective-permute-start(bf16[256,896]{1,0:T(8,128)(2,1)S(1)} %collective-permute-done.1.refs_2_), channel_id=1, source_target_pairs={{0,224},{32,0},{64,32},{96,64},{128,96},{160,128},{192,160},{224,1... | collective-permute-start | bytes 1376264 | tf_op jit(solution)/shard_map/proj/gather_grads/ppermute | solution.py:380
  47.9 16.9 %collective-permute-start.4 = (bf16[256,896]{1,0:T(8,128)(2,1)S(1)}, bf16[256,896]{1,0:T(8,128)(2,1)S(1)}, u32[]{:S(2)}, u32[]{:S(2)}) collective-permute-start(bf16[256,896]{1,0:T(8,128)(2,1)S(1)} %collective-permute-done.2.refs_3_), channel_id=1, source_target_pairs={{0,32},{32,64},{64,96},{96,128},{128,160},{160,192},{192,224},{224... | collective-permute-start | bytes 1376264 | tf_op jit(solution)/shard_map/proj/gather_grads/ppermute | solution.py:379
  48.0 16.9 %collective-permute-start.5 = (bf16[256,896]{1,0:T(8,128)(2,1)S(1)}, bf16[256,896]{1,0:T(8,128)(2,1)S(1)}, u32[]{:S(2)}, u32[]{:S(2)}) collective-permute-start(bf16[256,896]{1,0:T(8,128)(2,1)S(1)} %collective-permute-done.3.refs_4_), channel_id=1, source_target_pairs={{0,224},{32,0},{64,32},{96,64},{128,96},{160,128},{192,160},{224,1... | collective-permute-start | bytes 1376264 | tf_op jit(solution)/shard_map/proj/gather_grads/ppermute | solution.py:380
  65.7 3.9 %collective-permute-start.6 = (f32[1024,256]{1,0:T(8,128)S(1)}, f32[1024,256]{1,0:T(8,128)S(1)}, u32[]{:S(2)}, u32[]{:S(2)}) collective-permute-start(f32[1024,256]{1,0:T(8,128)S(1)} %proj_part.1.part), channel_id=1, source_target_pairs={{0,1},{1,0},{2,3},{3,2},{4,5},{5,4},{6,7},{7,6},{8,9},{9,8},{10,11... | collective-permute-start | bytes 3145736 | tf_op jit(solution)/shard_map/sum_proj/ppermute | solution.py:406
  70.4 14.4 %all-to-all-start.3 = ((f32[16,32,256]{2,1,0:T(8,128)}), f32[16,32,256]{2,1,0:T(8,128)S(1)}, u32[]{:S(2)}, u32[]{:S(2)}) async-start(f32[16,32,256]{2,1,0:T(8,128)} %bitcast.7), calls=%async_computation.3 | async-start | bytes 1048576 | tf_op jit(solution)/shard_map/sum_proj/all_to_all | solution.py:409
  74.0 15.5 %collective-permute-start.7 = (bf16[256,896]{1,0:T(8,128)(2,1)}, bf16[256,896]{1,0:T(8,128)(2,1)S(1)}, u32[]{:S(2)}, u32[]{:S(2)}) collective-permute-start(bf16[256,896]{1,0:T(8,128)(2,1)} %copy-done.19), channel_id=1, source_target_pairs={{0,32},{32,64},{64,96},{96,128},{128,160},{160,192},{192,224},{224... | collective-permute-start | bytes 1376264 | tf_op jit(solution)/shard_map/gather_grads/ppermute | solution.py:400
  85.7 21.4 %all-to-all-start.4 = ((f32[16,32,256]{2,1,0:T(8,128)}), f32[16,32,256]{2,1,0:T(8,128)S(1)}, u32[]{:S(2)}, u32[]{:S(2)}) async-start(f32[16,32,256]{2,1,0:T(8,128)} %sum_copies.4), calls=%async_computation.4 | async-start | bytes 1048576 | tf_op jit(solution)/shard_map/sum_proj/all_to_all | solution.py:412
  89.3 67.5 %reduce-scatter.2.cloned.1.call-start = ((), (), s32[]{:S(2)}) async-start(), calls=%async_computation.10 | async-start | bytes 1032192 | tf_op jit(solution)/shard_map/cross/reduce_scatter | solution.py:419
  107.0 3.2 %collective-permute-start.8 = (f32[512,256]{1,0:T(8,128)S(1)}, f32[512,256]{1,0:T(8,128)S(1)}, u32[]{:S(2)}, u32[]{:S(2)}) collective-permute-start(f32[512,256]{1,0:T(8,128)S(1)} %bitcast.27), channel_id=1, source_target_pairs={{0,1},{1,0},{2,3},{3,2},{4,5},{5,4},{6,7},{7,6},{8,9},{9,8},{10,11... | collective-permute-start | bytes 1572872 | tf_op jit(solution)/shard_map/sum_proj/ppermute | solution.py:414
  116.9 11.5 %all-to-all-start.5 = ((f32[8,8,256]{2,1,0:T(8,128)}), f32[8,8,256]{2,1,0:T(8,128)S(1)}, u32[]{:S(2)}, u32[]{:S(2)}) async-start(f32[8,8,256]{2,1,0:T(8,128)} %gram.1), calls=%async_computation.6 | async-start | bytes 131072 | tf_op jit(solution)/shard_map/gram/all_to_all | solution.py:424
  129.1 18.0 %all-to-all-start.6 = ((f32[32,8,256]{2,1,0:T(8,128)}), f32[32,8,256]{2,1,0:T(8,128)S(1)}, u32[]{:S(2)}, u32[]{:S(2)}) async-start(f32[32,8,256]{2,1,0:T(8,128)} %sum_copies.5), calls=%async_computation.7 | async-start | bytes 524288 | tf_op jit(solution)/shard_map/gram/all_to_all | solution.py:425
  156.8 5.9 %collective-permute-start.9 = (f32[112,256]{1,0:T(8,128)}, f32[112,256]{1,0:T(8,128)S(1)}, u32[]{:S(2)}, u32[]{:S(2)}) collective-permute-start(f32[112,256]{1,0:T(8,128)} %reduce-scatter.2.cloned.1.call-done.s0), channel_id=1, source_target_pairs={{0,32},{32,64},{64,96},{96,128},{128,160},{160,192},{192,224},{224... | collective-permute-start | bytes 344072 | tf_op jit(solution)/shard_map/gather_cross/ppermute | solution.py:437
  156.9 5.7 %collective-permute-start.10 = (f32[112,256]{1,0:T(8,128)}, f32[112,256]{1,0:T(8,128)S(1)}, u32[]{:S(2)}, u32[]{:S(2)}) collective-permute-start(f32[112,256]{1,0:T(8,128)} %reduce-scatter.2.cloned.1.call-done.s0), channel_id=1, source_target_pairs={{0,224},{32,0},{64,32},{96,64},{128,96},{160,128},{192,160},{224,1... | collective-permute-start | bytes 344072 | tf_op jit(solution)/shard_map/gather_cross/ppermute | solution.py:438
  162.7 4.9 %collective-permute-start.11 = (f32[112,256]{1,0:T(8,128)S(1)}, f32[112,256]{1,0:T(8,128)S(1)}, u32[]{:S(2)}, u32[]{:S(2)}) collective-permute-start(f32[112,256]{1,0:T(8,128)S(1)} %collective-permute-done.9.s1), channel_id=1, source_target_pairs={{0,32},{32,64},{64,96},{96,128},{128,160},{160,192},{192,224},{224... | collective-permute-start | bytes 344072 | tf_op jit(solution)/shard_map/gather_cross/ppermute | solution.py:437
  162.7 4.9 %collective-permute-start.12 = (f32[112,256]{1,0:T(8,128)S(1)}, f32[112,256]{1,0:T(8,128)S(1)}, u32[]{:S(2)}, u32[]{:S(2)}) collective-permute-start(f32[112,256]{1,0:T(8,128)S(1)} %collective-permute-done.10.s2), channel_id=1, source_target_pairs={{0,224},{32,0},{64,32},{96,64},{128,96},{160,128},{192,160},{224,1... | collective-permute-start | bytes 344072 | tf_op jit(solution)/shard_map/gather_cross/ppermute | solution.py:438
  167.5 4.9 %collective-permute-start.13 = (f32[112,256]{1,0:T(8,128)S(1)}, f32[112,256]{1,0:T(8,128)S(1)}, u32[]{:S(2)}, u32[]{:S(2)}) collective-permute-start(f32[112,256]{1,0:T(8,128)S(1)} %collective-permute-done.11.s3), channel_id=1, source_target_pairs={{0,32},{32,64},{64,96},{96,128},{128,160},{160,192},{192,224},{224... | collective-permute-start | bytes 344072 | tf_op jit(solution)/shard_map/gather_cross/ppermute | solution.py:437
  167.5 4.9 %collective-permute-start.14 = (f32[112,256]{1,0:T(8,128)S(1)}, f32[112,256]{1,0:T(8,128)S(1)}, u32[]{:S(2)}, u32[]{:S(2)}) collective-permute-start(f32[112,256]{1,0:T(8,128)S(1)} %collective-permute-done.12.s4), channel_id=1, source_target_pairs={{0,224},{32,0},{64,32},{96,64},{128,96},{160,128},{192,160},{224,1... | collective-permute-start | bytes 344072 | tf_op jit(solution)/shard_map/gather_cross/ppermute | solution.py:438
  172.4 4.9 %collective-permute-start.15 = (f32[112,256]{1,0:T(8,128)S(1)}, f32[112,256]{1,0:T(8,128)S(1)}, u32[]{:S(2)}, u32[]{:S(2)}) collective-permute-start(f32[112,256]{1,0:T(8,128)S(1)} %collective-permute-done.13.s5), channel_id=1, source_target_pairs={{0,32},{32,64},{64,96},{96,128},{128,160},{160,192},{192,224},{224... | collective-permute-start | bytes 344072 | tf_op jit(solution)/shard_map/gather_cross/ppermute | solution.py:442
  181.0 15.4 %all-to-all-start.7 = ((f32[32,1,256]{2,1,0:T(1,128)}), f32[32,1,256]{2,1,0:T(1,128)S(1)}, u32[]{:S(2)}, u32[]{:S(2)}) async-start(f32[32,1,256]{2,1,0:T(1,128)} %broadcast_in_dim.9), calls=%async_computation.8 | async-start | bytes 65536 | tf_op jit(solution)/shard_map/norms/all_to_all | solution.py:53
  (25 other events, 160.0 us)
Sparse Core Ops, SparseCore 0:
  10.6 55.2 all-gather.1
  115.0 32.8 reduce-scatter.1

commit v6 on v4

--- a/solution.py
+++ b/solution.py
@@ -48,23 +48,23 @@
     return mul(a_high, b_high) + (mul(a_high, b_low) + mul(a_low, b_high))
 
 
-def spread(x, axis, size, groups=None):
-    copies = jnp.broadcast_to(x[None], (size,) + x.shape)
-    return lax.all_to_all(copies, axis, 0, 0, axis_index_groups=groups)
-
-
 def in_vmem():
     return pl.BlockSpec(memory_space=pltpu.VMEM)
 
 
-def grad_kernel(place, acts, *refs):
+def shift(n):
+    return (n + 1) // 2 if n % 2 == 0 else ROWS - (n + 1) // 2
+
+
+def grad_kernel(acts, *refs):
     pieces, (momentum, buffer, left, right, total, sems) = refs[:-6], refs[-6:]
     tokens = right.shape[0] // len(pieces)
     rows = total.shape[0]
     tile = rows // TILES
+    row = lax.axis_index("row")
     fetches = []
     for n, g in enumerate(pieces):
-        span = pl.ds(pl.multiple_of(place[n] * tokens, tokens), tokens)
+        span = pl.ds(pl.multiple_of(lax.rem(row + shift(n), ROWS) * tokens, tokens), tokens)
         fetches.append(pltpu.make_async_copy(g, right.at[span, :], sems.at[n]))
     spans = [pl.ds(n * tile, tile) for n in range(TILES)]
     lefts = [pltpu.make_async_copy(acts.at[:, at], left.at[n], sems.at[len(pieces) + n]) for n, at in enumerate(spans)]
@@ -97,13 +97,13 @@
         copy.wait()
 
 
-def add_grad(place, acts, pieces, momentum):
+def add_grad(acts, pieces, momentum):
     rows, cols = momentum.shape
     tokens = acts.shape[0]
     anywhere = pl.BlockSpec(memory_space=pl.ANY)
     return pl.pallas_call(
         grad_kernel,
-        in_specs=[pl.BlockSpec(memory_space=pltpu.SMEM)] + [anywhere] * (len(pieces) + 2),
+        in_specs=[anywhere] * (len(pieces) + 2),
         out_specs=anywhere,
         out_shape=jax.ShapeDtypeStruct((rows, cols), jnp.float32),
         scratch_shapes=[
@@ -119,7 +119,7 @@
             transcendentals=0,
         ),
         name="add_grad",
-    )(place, acts, *pieces, momentum)
+    )(acts, *pieces, momentum)
 
 
 def cross_kernel(core, buffer, mine, other, cross):
@@ -189,17 +189,18 @@
     row = lax.axis_index("row")
     for n, share in enumerate((s0, s1, s2, s3, s4, s5, s6, s7)):
         height = share.shape[0]
-        shift = (n + 1) // 2 if n % 2 == 0 else ROWS - (n + 1) // 2
-        start = pl.multiple_of(lax.rem(row + shift, ROWS) * height, height)
+        start = pl.multiple_of(lax.rem(row + shift(n), ROWS) * height, height)
         back[pl.ds(start, height), :] = dot3(share[...], inverse[...], ((1,), (1,)))
     whole = back[...]
-    norms[...] = jnp.sum(whole * whole, axis=0, keepdims=True)
+    total = jnp.sum(whole * whole, axis=0, keepdims=True)
+    for n in range(norms.shape[0]):
+        norms[n] = total
 
 
 def back_and_norms(inverse, shares):
     rank = inverse.shape[0]
     cols = len(shares) * shares[0].shape[0]
-    return call(back_kernel, "back_and_norms", [(cols, rank), (1, rank)], inverse, *shares)
+    return call(back_kernel, "back_and_norms", [(cols, rank), (COLS, 1, rank)], inverse, *shares)
 
 
 def momentum_kernel(buffer, ortho, back, new_momentum):
@@ -349,7 +350,6 @@
 def on_device(acts, out_grads, weight, momentum, basis):
     high = lax.Precision.HIGH
     highest = lax.Precision.HIGHEST
-    row = lax.axis_index("row")
     col = lax.axis_index("col")
     core = (col % 2).reshape(1)
     rank = basis.shape[1]
@@ -357,16 +357,15 @@
     with jax.named_scope("gather_acts"):
         acts_all = lax.all_gather(acts, "col", axis=0, tiled=True)
 
-    pieces, places = [out_grads], [row]
+    pieces = [out_grads]
     up = down = out_grads
 
-    def turn(step, *others):
+    def turn(*others):
         nonlocal up, down
         with jax.named_scope("gather_grads"):
             up = lax.ppermute(up, "row", UP)
             down = lax.ppermute(down, "row", DOWN)
             pieces.extend([up, down])
-            places.extend([row - step, row + step])
             up, down, *others = lax.optimization_barrier((up, down, *others))
             return others
 
@@ -376,17 +375,15 @@
         small = jnp.dot(out_grads.astype(jnp.float32), basis, precision=high)
         small = small.reshape(GROUPS, ROWS, -1, rank).swapaxes(0, 1).reshape(COLS, -1, rank)
         local = jnp.dot(momentum, basis, precision=high)
-        small, mixed, local = turn(1, small, mixed, local)
+        small, mixed, local = turn(small, mixed, local)
         small = sum_copies(lax.all_to_all(small, "col", 0, 0), ROWS)
-        small, mixed = turn(2, small, mixed)
+        small, mixed = turn(small, mixed)
         small = lax.all_to_all(small, "row", 0, 0).reshape(-1, rank)
         part = proj_part(local, mixed.reshape(-1, acts.shape[1]), small)
-        (part,) = turn(3, part)
+        (part,) = turn(part)
 
     with jax.named_scope("gather_grads"):
         pieces.append(lax.ppermute(up, "row", UP))
-        places.append(row + ROWS // 2)
-        place = jnp.stack(places).astype(jnp.int32) % ROWS
 
     with jax.named_scope("sum_proj"):
         cut = part.shape[0] // 2
@@ -394,7 +391,7 @@
         mine = call(pick_kernel, "pick", (cut, rank), core, part, other, scalars=1)
         shares = mine.reshape(CHIPS, cut // CHIPS, rank)
         shares = lax.all_to_all(shares, "col", 0, 0, axis_index_groups=SAME_CORE)
-        buffer = add_grad(place, acts_all, pieces, momentum)
+        buffer = add_grad(acts_all, pieces, momentum)
         mine = sum_copies(shares, CHIPS)
         mine = lax.all_to_all(mine, "col", 0, 0, axis_index_groups=SAME_CORE).reshape(cut, rank)
         mine, buffer = lax.optimization_barrier((mine, buffer))
@@ -420,16 +417,18 @@
     with jax.named_scope("gather_cross"):
         parts = [share]
         up = down = share
-        for _ in range(1, ROWS // 2):
+        for step in range(1, ROWS // 2):
             up = lax.ppermute(up, "row", UP)
             down = lax.ppermute(down, "row", DOWN)
+            if step == 1:
+                up, down, ortho = lax.optimization_barrier((up, down, ortho))
             parts += [up, down]
         parts.append(lax.ppermute(up, "row", UP))
 
     back, norms = back_and_norms(inverse, parts)
 
     with jax.named_scope("norms"):
-        norms = jnp.sum(spread(norms, "col", COLS), axis=0)
+        norms = jnp.sum(lax.all_to_all(norms, "col", 0, 0), axis=0)
         scale = 1.0 / jnp.sqrt(norms + norm_eps)
 
     new_momentum = update_momentum(buffer, ortho, back)

time: 199 us -> 198 us (level)
  blocking collectives: 57 us -> 28 us
  waiting for transfers between devices: 27.5 us -> 45.3 us
  starting transfers between devices: 50.8 us -> 60.8 us
    all_to_all x2 -> x0, blocking collectives: 29 us -> none  [the longest x1 17.8 us: on_device(): gram = lax.all_to_all(gram, 'col', 0, 0).reshape(rank, rank)]
    all_to_all x1 -> x3, waiting for transfers between devices: 0.22 us -> 18.6 us  [the longest x1 8.81 us: on_device(): gram = lax.all_to_all(gram, 'col', 0, 0).reshape(rank, rank)]
    all_to_all x1 -> x3, starting transfers between devices: 10.8 us -> 20.1 us  [the longest x1 8.01 us: on_device(): norms = jnp.sum(lax.all_to_all(norms, 'col', 0, 0), axis=0)]
    unnamed x26 -> x28, local copies, waits for them, and re-layouts: 8.22 us -> 8.9 us
  transfers between devices with their start and end apart: 22 -> 24, of which waited for: 9 -> 12; matrix products, arithmetic and copies ran while one was open for 4% -> 3% of each run, Pallas kernels for 13% -> 13%
where the time goes in v6:
time: 198 us; the launch traced here: 197 us
  starting transfers between devices  60.8 us (31%)
  waiting for transfers between devices  45.3 us (23%)
  Pallas kernels  32.9 us (17%)
  blocking collectives  28 us (14%)
  between operations  14.3 us (7%)
  local copies, waits for them, and re-layouts  8.92 us (5%)
  matrix products  6.26 us (3%)
    all_to_all x1, blocking collectives, on_device(): small = sum_copies(lax.all_to_all(small, 'col', 0, 0), ROWS)  15.2 us
    all_to_all x1, blocking collectives, on_device(): small = lax.all_to_all(small, 'row', 0, 0).reshape(-1, rank)  12.7 us
    ppermute x3, starting transfers between devices, turn(): down = lax.ppermute(down, 'row', DOWN)  9.36 us
    pallas_call x7, Pallas kernels, call(): pl.pallas_call(kernel, in_specs=[pl.BlockSpec(memory_space=pltpu.SMEM)] *...  9 us
    pallas_call x1, Pallas kernels, add_grad(): pl.pallas_call(grad_kernel, in_specs=[anywhere] * (len(pieces) + 2), out_...  8.92 us
    pallas_call x1, Pallas kernels, inverse_factor(): pl.pallas_call(factor_kernel, out_shape=jax.ShapeDtypeStruct((n, n), jnp....  8.92 us
    unnamed x28, local copies, waits for them, and re-layouts  8.9 us
    all_to_all x1, waiting for transfers between devices, on_device(): gram = lax.all_to_all(gram, 'col', 0, 0).reshape(rank, rank)  8.81 us
  transfers between devices with their start and end apart: 24, of which 12 were waited for; matrix products, arithmetic and copies ran while one was open for 3% of the time, Pallas kernels for 13%

profile of v6, /device:TPU:1, one launch (start us, length us, event | category | flops | bytes accessed | tf_op | source)
XLA Modules:
  0.0 196.6 jit_solution(13147122265553928495)
XLA Ops:
  10.5 4.0 %collective-permute-start.1 = (bf16[256,896]{1,0:T(8,128)(2,1)}, bf16[256,896]{1,0:T(8,128)(2,1)}, u32[]{:S(2)}, u32[]{:S(2)}) collective-permute-start(bf16[256,896]{1,0:T(8,128)(2,1)} %refs_0_.1), channel_id=1, source_target_pairs={{0,224},{32,0},{64,32},{96,64},{128,96},{160,128},{192,160},{224,1... | collective-permute-start | bytes 1376264 | tf_op jit(solution)/shard_map/proj/gather_grads/ppermute | solution.py:367
  14.5 6.7 %all-to-all-start = ((bf16[8,8,1024]{2,1,0:T(8,128)(2,1)}), bf16[8,8,1024]{2,1,0:T(8,128)(2,1)S(1)}, u32[]{:S(2)}, u32[]{:S(2)}) async-start(bf16[8,8,1024]{2,1,0:T(8,128)(2,1)} %bitcast.27), calls=%async_computation | async-start | bytes 262144 | tf_op jit(solution)/shard_map/proj/all_to_all | solution.py:374
  21.2 3.8 %fusion.6.local = f32[1024,256]{1,0:T(8,128)S(1)} fusion(f32[1024,896]{1,0:T(8,128)} %refs_8_.1, f32[896,256]{1,0:T(8,128)S(1)} %copy-done), kind=kOutput, calls=%fused_computation.9 | convolution fusion | flops 1409286144 | bytes 5636096 | tf_op jit(solution)/shard_map/proj/dot_general | solution.py:377
  25.5 2.7 %all-to-all-done = bf16[8,8,1024]{2,1,0:T(8,128)(2,1)S(1)} async-done(((bf16[8,8,1024]{2,1,0:T(8,128)(2,1)}), bf16[8,8,1024]{2,1,0:T(8,128)(2,1)S(1)}, u32[]{:S(2)}, u32[]{:S(2)}) %all-to-all-start) | async-done | bytes 131104 | tf_op jit(solution)/shard_map/proj/all_to_all | solution.py:374
  28.2 2.7 %collective-permute-start.3 = (bf16[256,896]{1,0:T(8,128)(2,1)}, bf16[256,896]{1,0:T(8,128)(2,1)S(1)}, u32[]{:S(2)}, u32[]{:S(2)}) collective-permute-start(bf16[256,896]{1,0:T(8,128)(2,1)} %collective-permute-done.1.refs_2_), channel_id=1, source_target_pairs={{0,224},{32,0},{64,32},{96,64},{128,96},{160,128},{192,160},{224,1... | collective-permute-start | bytes 1376264 | tf_op jit(solution)/shard_map/proj/gather_grads/ppermute | solution.py:367
  30.9 15.2 %all_to_all.40.shares = f32[32,8,256]{2,1,0:T(8,128)S(1)} all-to-all(f32[32,8,256]{2,1,0:T(8,128)S(1)} %bitcast.26), channel_id=1, replica_groups=mesh['row'=8,'col'=32] {'col'}, dimensions={0} | all-to-all | bytes 524288 | tf_op jit(solution)/shard_map/proj/all_to_all | solution.py:379
  46.3 2.7 %collective-permute-start.5 = (bf16[256,896]{1,0:T(8,128)(2,1)S(1)}, bf16[256,896]{1,0:T(8,128)(2,1)S(1)}, u32[]{:S(2)}, u32[]{:S(2)}) collective-permute-start(bf16[256,896]{1,0:T(8,128)(2,1)S(1)} %collective-permute-done.3.refs_4_), channel_id=1, source_target_pairs={{0,224},{32,0},{64,32},{96,64},{128,96},{160,128},{192,160},{224,1... | collective-permute-start | bytes 1376264 | tf_op jit(solution)/shard_map/proj/gather_grads/ppermute | solution.py:367
  49.0 12.7 %all_to_all.41 = f32[8,8,256]{2,1,0:T(8,128)S(1)} all-to-all(f32[8,8,256]{2,1,0:T(8,128)S(1)} %sum_copies.3), channel_id=1, replica_groups=mesh['row'=8,'col'=32] {'row'}, dimensions={0} | all-to-all | bytes 131072 | tf_op jit(solution)/shard_map/proj/all_to_all | solution.py:381
  67.3 3.6 %all-to-all-start.3 = ((f32[16,32,256]{2,1,0:T(8,128)}), f32[16,32,256]{2,1,0:T(8,128)S(1)}, u32[]{:S(2)}, u32[]{:S(2)}) async-start(f32[16,32,256]{2,1,0:T(8,128)} %bitcast.7), calls=%async_computation.3 | async-start | bytes 1048576 | tf_op jit(solution)/shard_map/sum_proj/all_to_all | solution.py:393
  70.9 2.8 %collective-permute-start.7 = (bf16[256,896]{1,0:T(8,128)(2,1)S(1)}, bf16[256,896]{1,0:T(8,128)(2,1)S(1)}, u32[]{:S(2)}, u32[]{:S(2)}) collective-permute-start(bf16[256,896]{1,0:T(8,128)(2,1)S(1)} %copy-done.10), channel_id=1, source_target_pairs={{0,32},{32,64},{64,96},{96,128},{128,160},{160,192},{192,224},{224... | collective-permute-start | bytes 1376264 | tf_op jit(solution)/shard_map/gather_grads/ppermute | solution.py:386
  73.7 8.3 %all-to-all-done.3.shares = f32[16,32,256]{2,1,0:T(8,128)S(1)} async-done(((f32[16,32,256]{2,1,0:T(8,128)}), f32[16,32,256]{2,1,0:T(8,128)S(1)}, u32[]{:S(2)}, u32[]{:S(2)}) %all-to-all-start.3) | async-done | bytes 524320 | tf_op jit(solution)/shard_map/sum_proj/all_to_all | solution.py:393
  82.9 3.6 %all-to-all-start.4 = ((f32[16,32,256]{2,1,0:T(8,128)}), f32[16,32,256]{2,1,0:T(8,128)S(1)}, u32[]{:S(2)}, u32[]{:S(2)}) async-start(f32[16,32,256]{2,1,0:T(8,128)} %sum_copies.4), calls=%async_computation.4 | async-start | bytes 1048576 | tf_op jit(solution)/shard_map/sum_proj/all_to_all | solution.py:396
  87.5 8.9 %add_grad.1.buffer = f32[1024,896]{1,0:T(8,128)} custom-call(bf16[2048,1024]{1,0:T(8,128)(2,1)} %all-gather.2.cloned.1.call-done.acts, bf16[256,896]{1,0:T(8,128)(2,1)} %refs_0_.1, bf16[256,896]{1,0:T(8,128)(2,1)} %collective-permute-done.refs_1_, bf16[256,896]{1,0:T(8,128)(2,1)} %collective-permute-done.1.refs_2_, bf16[256,896]{1,0:T(8,128)(2,1)} %copy-done.7, ...), custom_call_target="tpu_custom_call" | custom-call | flops 3758096384 | bytes 15204352 | tf_op jit(solution)/shard_map/sum_proj/add_grad/pallas_call | solution.py:104
  107.2 4.2 %all-to-all-start.5 = ((f32[8,8,256]{2,1,0:T(8,128)}), f32[8,8,256]{2,1,0:T(8,128)S(1)}, u32[]{:S(2)}, u32[]{:S(2)}) async-start(f32[8,8,256]{2,1,0:T(8,128)} %gram.1), calls=%async_computation.6 | async-start | bytes 131072 | tf_op jit(solution)/shard_map/gram/all_to_all | solution.py:408
  111.4 7.3 %all-to-all-done.5.shares = f32[8,8,256]{2,1,0:T(8,128)S(1)} async-done(((f32[8,8,256]{2,1,0:T(8,128)}), f32[8,8,256]{2,1,0:T(8,128)S(1)}, u32[]{:S(2)}, u32[]{:S(2)}) %all-to-all-start.5) | async-done | bytes 65568 | tf_op jit(solution)/shard_map/gram/all_to_all | solution.py:408
  119.5 7.9 %all-to-all-start.6 = ((f32[32,8,256]{2,1,0:T(8,128)}), f32[32,8,256]{2,1,0:T(8,128)S(1)}, u32[]{:S(2)}, u32[]{:S(2)}) async-start(f32[32,8,256]{2,1,0:T(8,128)} %sum_copies.5), calls=%async_computation.7 | async-start | bytes 524288 | tf_op jit(solution)/shard_map/gram/all_to_all | solution.py:409
  127.4 8.8 %all-to-all-done.6 = f32[32,8,256]{2,1,0:T(8,128)S(1)} async-done(((f32[32,8,256]{2,1,0:T(8,128)}), f32[32,8,256]{2,1,0:T(8,128)S(1)}, u32[]{:S(2)}, u32[]{:S(2)}) %all-to-all-start.6) | async-done | bytes 262176 | tf_op jit(solution)/shard_map/gram/all_to_all | solution.py:409
  136.9 8.9 %inverse_factor.1.inverse = f32[256,256]{1,0:T(8,128)} custom-call(f32[256,256]{1,0:T(8,128)} %bitcast.28), custom_call_target="tpu_custom_call" | custom-call | flops 10000000000 | bytes 524288 | tf_op jit(solution)/shard_map/inverse_factor/pallas_call | solution.py:179
  151.8 2.7 %collective-permute-start.12 = (f32[112,256]{1,0:T(8,128)S(1)}, f32[112,256]{1,0:T(8,128)S(1)}, u32[]{:S(2)}, u32[]{:S(2)}) collective-permute-start(f32[112,256]{1,0:T(8,128)S(1)} %collective-permute-done.10.s2), channel_id=1, source_target_pairs={{0,224},{32,0},{64,32},{96,64},{128,96},{160,128},{192,160},{224,1... | collective-permute-start | bytes 344072 | tf_op jit(solution)/shard_map/gather_cross/ppermute | solution.py:422
  156.7 2.7 %collective-permute-start.14 = (f32[112,256]{1,0:T(8,128)S(1)}, f32[112,256]{1,0:T(8,128)S(1)}, u32[]{:S(2)}, u32[]{:S(2)}) collective-permute-start(f32[112,256]{1,0:T(8,128)S(1)} %collective-permute-done.12.s4), channel_id=1, source_target_pairs={{0,224},{32,0},{64,32},{96,64},{128,96},{160,128},{192,160},{224,1... | collective-permute-start | bytes 344072 | tf_op jit(solution)/shard_map/gather_cross/ppermute | solution.py:422
  161.5 4.8 %collective-permute-done.15.s7 = f32[112,256]{1,0:T(8,128)S(1)} collective-permute-done((f32[112,256]{1,0:T(8,128)S(1)}, f32[112,256]{1,0:T(8,128)S(1)}, u32[]{:S(2)}, u32[]{:S(2)}) %collective-permute-start.15) | collective-permute-done | bytes 114720 | tf_op jit(solution)/shard_map/gather_cross/ppermute | solution.py:426
  170.1 8.0 %all-to-all-start.7 = ((f32[32,1,256]{2,1,0:T(1,128)}), f32[32,1,256]{2,1,0:T(1,128)S(1)}, u32[]{:S(2)}, u32[]{:S(2)}) async-start(f32[32,1,256]{2,1,0:T(1,128)} %get-tuple-element.50), calls=%async_computation.8 | async-start | bytes 65536 | tf_op jit(solution)/shard_map/norms/all_to_all | solution.py:431
  180.2 2.9 %update_momentum.1 = f32[1024,896]{1,0:T(8,128)} custom-call(f32[1024,896]{1,0:T(8,128)S(1)} %copy-done.2, f32[1024,256]{1,0:T(8,128)S(1)} %fusion.ortho, f32[896,256]{1,0:T(8,128)S(1)} %get-tuple-element.49.back), custom_call_target="tpu_custom_call" | custom-call | tf_op jit(solution)/shard_map/update_momentum/pallas_call | solution.py:221
  187.0 2.7 %update_weight.1 = (bf16[1024,896]{1,0:T(8,128)(2,1)}, f32[896,256]{1,0:T(8,128)}) custom-call(bf16[1024,896]{1,0:T(8,128)(2,1)S(1)} %copy-done.3, f32[1024,256]{1,0:T(8,128)S(1)} %fusion.ortho, f32[896,256]{1,0:T(8,128)S(1)} %get-tuple-element.49.back, f32[1,256]{1,0:T(1,128)S(1)} %bitcast.24), custom_call_target="tpu_custom_call" | custom-call | tf_op jit(solution)/shard_map/update_weight/pallas_call | solution.py:257
  (75 shorter events, 43.6 us)
Async XLA Ops:
  7.2 79.6 %all-gather.2.cloned.1.call-start = ((), (), s32[]{:S(2)}) async-start(), calls=%async_computation.9 | async-start | bytes 4325376 | tf_op jit(solution)/shard_map/gather_acts/all_gather | solution.py:358
  7.9 20.3 %collective-permute-start = (bf16[256,896]{1,0:T(8,128)(2,1)}, bf16[256,896]{1,0:T(8,128)(2,1)}, u32[]{:S(2)}, u32[]{:S(2)}) collective-permute-start(bf16[256,896]{1,0:T(8,128)(2,1)} %refs_0_.1), channel_id=1, source_target_pairs={{0,32},{32,64},{64,96},{96,128},{128,160},{160,192},{192,224},{224... | collective-permute-start | bytes 1376264 | tf_op jit(solution)/shard_map/proj/gather_grads/ppermute | solution.py:366
  10.5 17.7 %collective-permute-start.1 = (bf16[256,896]{1,0:T(8,128)(2,1)}, bf16[256,896]{1,0:T(8,128)(2,1)}, u32[]{:S(2)}, u32[]{:S(2)}) collective-permute-start(bf16[256,896]{1,0:T(8,128)(2,1)} %refs_0_.1), channel_id=1, source_target_pairs={{0,224},{32,0},{64,32},{96,64},{128,96},{160,128},{192,160},{224,1... | collective-permute-start | bytes 1376264 | tf_op jit(solution)/shard_map/proj/gather_grads/ppermute | solution.py:367
  14.5 13.7 %all-to-all-start = ((bf16[8,8,1024]{2,1,0:T(8,128)(2,1)}), bf16[8,8,1024]{2,1,0:T(8,128)(2,1)S(1)}, u32[]{:S(2)}, u32[]{:S(2)}) async-start(bf16[8,8,1024]{2,1,0:T(8,128)(2,1)} %bitcast.27), calls=%async_computation | async-start | bytes 262144 | tf_op jit(solution)/shard_map/proj/all_to_all | solution.py:374
  28.2 18.0 %collective-permute-start.2 = (bf16[256,896]{1,0:T(8,128)(2,1)}, bf16[256,896]{1,0:T(8,128)(2,1)S(1)}, u32[]{:S(2)}, u32[]{:S(2)}) collective-permute-start(bf16[256,896]{1,0:T(8,128)(2,1)} %collective-permute-done.refs_1_), channel_id=1, source_target_pairs={{0,32},{32,64},{64,96},{96,128},{128,160},{160,192},{192,224},{224... | collective-permute-start | bytes 1376264 | tf_op jit(solution)/shard_map/proj/gather_grads/ppermute | solution.py:366
  28.2 18.0 %collective-permute-start.3 = (bf16[256,896]{1,0:T(8,128)(2,1)}, bf16[256,896]{1,0:T(8,128)(2,1)S(1)}, u32[]{:S(2)}, u32[]{:S(2)}) collective-permute-start(bf16[256,896]{1,0:T(8,128)(2,1)} %collective-permute-done.1.refs_2_), channel_id=1, source_target_pairs={{0,224},{32,0},{64,32},{96,64},{128,96},{160,128},{192,160},{224,1... | collective-permute-start | bytes 1376264 | tf_op jit(solution)/shard_map/proj/gather_grads/ppermute | solution.py:367
  46.2 16.0 %collective-permute-start.4 = (bf16[256,896]{1,0:T(8,128)(2,1)S(1)}, bf16[256,896]{1,0:T(8,128)(2,1)S(1)}, u32[]{:S(2)}, u32[]{:S(2)}) collective-permute-start(bf16[256,896]{1,0:T(8,128)(2,1)S(1)} %collective-permute-done.2.refs_3_), channel_id=1, source_target_pairs={{0,32},{32,64},{64,96},{96,128},{128,160},{160,192},{192,224},{224... | collective-permute-start | bytes 1376264 | tf_op jit(solution)/shard_map/proj/gather_grads/ppermute | solution.py:366
  46.3 15.9 %collective-permute-start.5 = (bf16[256,896]{1,0:T(8,128)(2,1)S(1)}, bf16[256,896]{1,0:T(8,128)(2,1)S(1)}, u32[]{:S(2)}, u32[]{:S(2)}) collective-permute-start(bf16[256,896]{1,0:T(8,128)(2,1)S(1)} %collective-permute-done.3.refs_4_), channel_id=1, source_target_pairs={{0,224},{32,0},{64,32},{96,64},{128,96},{160,128},{192,160},{224,1... | collective-permute-start | bytes 1376264 | tf_op jit(solution)/shard_map/proj/gather_grads/ppermute | solution.py:367
  62.2 4.2 %collective-permute-start.6 = (f32[1024,256]{1,0:T(8,128)S(1)}, f32[1024,256]{1,0:T(8,128)S(1)}, u32[]{:S(2)}, u32[]{:S(2)}) collective-permute-start(f32[1024,256]{1,0:T(8,128)S(1)} %proj_part.1.part), channel_id=1, source_target_pairs={{0,1},{1,0},{2,3},{3,2},{4,5},{5,4},{6,7},{7,6},{8,9},{9,8},{10,11... | collective-permute-start | bytes 3145736 | tf_op jit(solution)/shard_map/sum_proj/ppermute | solution.py:390
  67.3 14.7 %all-to-all-start.3 = ((f32[16,32,256]{2,1,0:T(8,128)}), f32[16,32,256]{2,1,0:T(8,128)S(1)}, u32[]{:S(2)}, u32[]{:S(2)}) async-start(f32[16,32,256]{2,1,0:T(8,128)} %bitcast.7), calls=%async_computation.3 | async-start | bytes 1048576 | tf_op jit(solution)/shard_map/sum_proj/all_to_all | solution.py:393
  70.9 15.8 %collective-permute-start.7 = (bf16[256,896]{1,0:T(8,128)(2,1)S(1)}, bf16[256,896]{1,0:T(8,128)(2,1)S(1)}, u32[]{:S(2)}, u32[]{:S(2)}) collective-permute-start(bf16[256,896]{1,0:T(8,128)(2,1)S(1)} %copy-done.10), channel_id=1, source_target_pairs={{0,32},{32,64},{64,96},{96,128},{128,160},{160,192},{192,224},{224... | collective-permute-start | bytes 1376264 | tf_op jit(solution)/shard_map/gather_grads/ppermute | solution.py:386
  82.9 13.9 %all-to-all-start.4 = ((f32[16,32,256]{2,1,0:T(8,128)}), f32[16,32,256]{2,1,0:T(8,128)S(1)}, u32[]{:S(2)}, u32[]{:S(2)}) async-start(f32[16,32,256]{2,1,0:T(8,128)} %sum_copies.4), calls=%async_computation.4 | async-start | bytes 1048576 | tf_op jit(solution)/shard_map/sum_proj/all_to_all | solution.py:396
  86.5 59.3 %reduce-scatter.2.cloned.1.call-start = ((), (), s32[]{:S(2)}) async-start(), calls=%async_computation.10 | async-start | bytes 1032192 | tf_op jit(solution)/shard_map/cross/reduce_scatter | solution.py:403
  96.8 3.7 %collective-permute-start.8 = (f32[512,256]{1,0:T(8,128)S(1)}, f32[512,256]{1,0:T(8,128)S(1)}, u32[]{:S(2)}, u32[]{:S(2)}) collective-permute-start(f32[512,256]{1,0:T(8,128)S(1)} %bitcast.18), channel_id=1, source_target_pairs={{0,1},{1,0},{2,3},{3,2},{4,5},{5,4},{6,7},{7,6},{8,9},{9,8},{10,11... | collective-permute-start | bytes 1572872 | tf_op jit(solution)/shard_map/sum_proj/ppermute | solution.py:398
  107.2 11.5 %all-to-all-start.5 = ((f32[8,8,256]{2,1,0:T(8,128)}), f32[8,8,256]{2,1,0:T(8,128)S(1)}, u32[]{:S(2)}, u32[]{:S(2)}) async-start(f32[8,8,256]{2,1,0:T(8,128)} %gram.1), calls=%async_computation.6 | async-start | bytes 131072 | tf_op jit(solution)/shard_map/gram/all_to_all | solution.py:408
  119.5 16.8 %all-to-all-start.6 = ((f32[32,8,256]{2,1,0:T(8,128)}), f32[32,8,256]{2,1,0:T(8,128)S(1)}, u32[]{:S(2)}, u32[]{:S(2)}) async-start(f32[32,8,256]{2,1,0:T(8,128)} %sum_copies.5), calls=%async_computation.7 | async-start | bytes 524288 | tf_op jit(solution)/shard_map/gram/all_to_all | solution.py:409
  145.9 5.9 %collective-permute-start.9 = (f32[112,256]{1,0:T(8,128)}, f32[112,256]{1,0:T(8,128)S(1)}, u32[]{:S(2)}, u32[]{:S(2)}) collective-permute-start(f32[112,256]{1,0:T(8,128)} %reduce-scatter.2.cloned.1.call-done.s0), channel_id=1, source_target_pairs={{0,32},{32,64},{64,96},{96,128},{128,160},{160,192},{192,224},{224... | collective-permute-start | bytes 344072 | tf_op jit(solution)/shard_map/gather_cross/ppermute | solution.py:421
  146.0 5.8 %collective-permute-start.10 = (f32[112,256]{1,0:T(8,128)}, f32[112,256]{1,0:T(8,128)S(1)}, u32[]{:S(2)}, u32[]{:S(2)}) collective-permute-start(f32[112,256]{1,0:T(8,128)} %reduce-scatter.2.cloned.1.call-done.s0), channel_id=1, source_target_pairs={{0,224},{32,0},{64,32},{96,64},{128,96},{160,128},{192,160},{224,1... | collective-permute-start | bytes 344072 | tf_op jit(solution)/shard_map/gather_cross/ppermute | solution.py:422
  151.8 4.9 %collective-permute-start.11 = (f32[112,256]{1,0:T(8,128)S(1)}, f32[112,256]{1,0:T(8,128)S(1)}, u32[]{:S(2)}, u32[]{:S(2)}) collective-permute-start(f32[112,256]{1,0:T(8,128)S(1)} %collective-permute-done.9.s1), channel_id=1, source_target_pairs={{0,32},{32,64},{64,96},{96,128},{128,160},{160,192},{192,224},{224... | collective-permute-start | bytes 344072 | tf_op jit(solution)/shard_map/gather_cross/ppermute | solution.py:421
  151.8 4.9 %collective-permute-start.12 = (f32[112,256]{1,0:T(8,128)S(1)}, f32[112,256]{1,0:T(8,128)S(1)}, u32[]{:S(2)}, u32[]{:S(2)}) collective-permute-start(f32[112,256]{1,0:T(8,128)S(1)} %collective-permute-done.10.s2), channel_id=1, source_target_pairs={{0,224},{32,0},{64,32},{96,64},{128,96},{160,128},{192,160},{224,1... | collective-permute-start | bytes 344072 | tf_op jit(solution)/shard_map/gather_cross/ppermute | solution.py:422
  156.7 4.9 %collective-permute-start.13 = (f32[112,256]{1,0:T(8,128)S(1)}, f32[112,256]{1,0:T(8,128)S(1)}, u32[]{:S(2)}, u32[]{:S(2)}) collective-permute-start(f32[112,256]{1,0:T(8,128)S(1)} %collective-permute-done.11.s3), channel_id=1, source_target_pairs={{0,32},{32,64},{64,96},{96,128},{128,160},{160,192},{192,224},{224... | collective-permute-start | bytes 344072 | tf_op jit(solution)/shard_map/gather_cross/ppermute | solution.py:421
  156.7 4.9 %collective-permute-start.14 = (f32[112,256]{1,0:T(8,128)S(1)}, f32[112,256]{1,0:T(8,128)S(1)}, u32[]{:S(2)}, u32[]{:S(2)}) collective-permute-start(f32[112,256]{1,0:T(8,128)S(1)} %collective-permute-done.12.s4), channel_id=1, source_target_pairs={{0,224},{32,0},{64,32},{96,64},{128,96},{160,128},{192,160},{224,1... | collective-permute-start | bytes 344072 | tf_op jit(solution)/shard_map/gather_cross/ppermute | solution.py:422
  161.5 4.9 %collective-permute-start.15 = (f32[112,256]{1,0:T(8,128)S(1)}, f32[112,256]{1,0:T(8,128)S(1)}, u32[]{:S(2)}, u32[]{:S(2)}) collective-permute-start(f32[112,256]{1,0:T(8,128)S(1)} %collective-permute-done.13.s5), channel_id=1, source_target_pairs={{0,32},{32,64},{64,96},{96,128},{128,160},{160,192},{192,224},{224... | collective-permute-start | bytes 344072 | tf_op jit(solution)/shard_map/gather_cross/ppermute | solution.py:426
  170.1 15.4 %all-to-all-start.7 = ((f32[32,1,256]{2,1,0:T(1,128)}), f32[32,1,256]{2,1,0:T(1,128)S(1)}, u32[]{:S(2)}, u32[]{:S(2)}) async-start(f32[32,1,256]{2,1,0:T(1,128)} %get-tuple-element.50), calls=%async_computation.8 | async-start | bytes 65536 | tf_op jit(solution)/shard_map/norms/all_to_all | solution.py:431
  (14 other events, 83.2 us)
Sparse Core Ops, SparseCore 0:
  10.6 56.3 all-gather.1
  105.3 31.6 reduce-scatter.1

commit v7 on v6

--- a/solution.py
+++ b/solution.py
@@ -397,14 +397,16 @@
         mine, buffer = lax.optimization_barrier((mine, buffer))
         other = lax.ppermute(mine, "col", CORE_SWAP)
 
+    with jax.named_scope("gram"):
+        gram = call(gram_kernel, "gram", (ROWS, rank // COLS, rank), col.reshape(1), mine, other, scalars=1)
+        gram, mine, other = lax.optimization_barrier((gram, mine, other))
+
     with jax.named_scope("cross"):
         cross = call(cross_kernel, "cross", (buffer.shape[1], rank), core, buffer, mine, other, scalars=1)
-        cross, mine, other = lax.optimization_barrier((cross, mine, other))
+        cross, gram = lax.optimization_barrier((cross, gram))
         share = lax.psum_scatter(cross, "row", scatter_dimension=0, tiled=True)
 
     with jax.named_scope("gram"):
-        height = rank // COLS
-        gram = call(gram_kernel, "gram", (ROWS, height, rank), col.reshape(1), mine, other, scalars=1)
         gram = sum_copies(lax.all_to_all(gram, "row", 0, 0), COLS)
         gram = lax.all_to_all(gram, "col", 0, 0).reshape(rank, rank)
 

time: 198 us -> 199 us (level)
  transfers between devices with their start and end apart: 24 -> 24, of which waited for: 12 -> 12; matrix products, arithmetic and copies ran while one was open for 3% -> 3% of each run, Pallas kernels for 13% -> 12%
where the time goes in v7:
time: 199 us; the launch traced here: 198 us
  starting transfers between devices  62.7 us (32%)
  waiting for transfers between devices  45 us (23%)
  Pallas kernels  32.9 us (17%)
  blocking collectives  28 us (14%)
  between operations  14.3 us (7%)
  local copies, waits for them, and re-layouts  8.92 us (4%)
  matrix products  6.26 us (3%)
    all_to_all x1, blocking collectives, on_device(): small = sum_copies(lax.all_to_all(small, 'col', 0, 0), ROWS)  15.2 us
    all_to_all x1, blocking collectives, on_device(): small = lax.all_to_all(small, 'row', 0, 0).reshape(-1, rank)  12.7 us
    all_to_all x1, starting transfers between devices, on_device(): norms = jnp.sum(lax.all_to_all(norms, 'col', 0, 0), axis=0)  9.84 us
    ppermute x3, starting transfers between devices, turn(): down = lax.ppermute(down, 'row', DOWN)  9.36 us
    pallas_call x7, Pallas kernels, call(): pl.pallas_call(kernel, in_specs=[pl.BlockSpec(memory_space=pltpu.SMEM)] *...  9 us
    pallas_call x1, Pallas kernels, inverse_factor(): pl.pallas_call(factor_kernel, out_shape=jax.ShapeDtypeStruct((n, n), jnp....  8.92 us
    pallas_call x1, Pallas kernels, add_grad(): pl.pallas_call(grad_kernel, in_specs=[anywhere] * (len(pieces) + 2), out_...  8.92 us
    unnamed x28, local copies, waits for them, and re-layouts  8.9 us
  transfers between devices with their start and end apart: 24, of which 12 were waited for; matrix products, arithmetic and copies ran while one was open for 3% of the time, Pallas kernels for 12%

profile of v7, /device:TPU:1, one launch (start us, length us, event | category | flops | bytes accessed | tf_op | source)
XLA Modules:
  0.0 198.3 jit_solution(16034900935810978567)
XLA Ops:
  10.5 4.0 %collective-permute-start.1 = (bf16[256,896]{1,0:T(8,128)(2,1)}, bf16[256,896]{1,0:T(8,128)(2,1)}, u32[]{:S(2)}, u32[]{:S(2)}) collective-permute-start(bf16[256,896]{1,0:T(8,128)(2,1)} %refs_0_.1), channel_id=1, source_target_pairs={{0,224},{32,0},{64,32},{96,64},{128,96},{160,128},{192,160},{224,1... | collective-permute-start | bytes 1376264 | tf_op jit(solution)/shard_map/proj/gather_grads/ppermute | solution.py:367
  14.5 6.7 %all-to-all-start = ((bf16[8,8,1024]{2,1,0:T(8,128)(2,1)}), bf16[8,8,1024]{2,1,0:T(8,128)(2,1)S(1)}, u32[]{:S(2)}, u32[]{:S(2)}) async-start(bf16[8,8,1024]{2,1,0:T(8,128)(2,1)} %bitcast.27), calls=%async_computation | async-start | bytes 262144 | tf_op jit(solution)/shard_map/proj/all_to_all | solution.py:374
  21.2 3.8 %fusion.6.local = f32[1024,256]{1,0:T(8,128)S(1)} fusion(f32[1024,896]{1,0:T(8,128)} %refs_8_.1, f32[896,256]{1,0:T(8,128)S(1)} %copy-done), kind=kOutput, calls=%fused_computation.9 | convolution fusion | flops 1409286144 | bytes 5636096 | tf_op jit(solution)/shard_map/proj/dot_general | solution.py:377
  25.5 2.7 %all-to-all-done = bf16[8,8,1024]{2,1,0:T(8,128)(2,1)S(1)} async-done(((bf16[8,8,1024]{2,1,0:T(8,128)(2,1)}), bf16[8,8,1024]{2,1,0:T(8,128)(2,1)S(1)}, u32[]{:S(2)}, u32[]{:S(2)}) %all-to-all-start) | async-done | bytes 131104 | tf_op jit(solution)/shard_map/proj/all_to_all | solution.py:374
  28.2 2.7 %collective-permute-start.3 = (bf16[256,896]{1,0:T(8,128)(2,1)}, bf16[256,896]{1,0:T(8,128)(2,1)S(1)}, u32[]{:S(2)}, u32[]{:S(2)}) collective-permute-start(bf16[256,896]{1,0:T(8,128)(2,1)} %collective-permute-done.1.refs_2_), channel_id=1, source_target_pairs={{0,224},{32,0},{64,32},{96,64},{128,96},{160,128},{192,160},{224,1... | collective-permute-start | bytes 1376264 | tf_op jit(solution)/shard_map/proj/gather_grads/ppermute | solution.py:367
  30.9 15.2 %all_to_all.40.shares = f32[32,8,256]{2,1,0:T(8,128)S(1)} all-to-all(f32[32,8,256]{2,1,0:T(8,128)S(1)} %bitcast.26), channel_id=1, replica_groups=mesh['row'=8,'col'=32] {'col'}, dimensions={0} | all-to-all | bytes 524288 | tf_op jit(solution)/shard_map/proj/all_to_all | solution.py:379
  46.3 2.7 %collective-permute-start.5 = (bf16[256,896]{1,0:T(8,128)(2,1)S(1)}, bf16[256,896]{1,0:T(8,128)(2,1)S(1)}, u32[]{:S(2)}, u32[]{:S(2)}) collective-permute-start(bf16[256,896]{1,0:T(8,128)(2,1)S(1)} %collective-permute-done.3.refs_4_), channel_id=1, source_target_pairs={{0,224},{32,0},{64,32},{96,64},{128,96},{160,128},{192,160},{224,1... | collective-permute-start | bytes 1376264 | tf_op jit(solution)/shard_map/proj/gather_grads/ppermute | solution.py:367
  49.0 12.7 %all_to_all.41 = f32[8,8,256]{2,1,0:T(8,128)S(1)} all-to-all(f32[8,8,256]{2,1,0:T(8,128)S(1)} %sum_copies.3), channel_id=1, replica_groups=mesh['row'=8,'col'=32] {'row'}, dimensions={0} | all-to-all | bytes 131072 | tf_op jit(solution)/shard_map/proj/all_to_all | solution.py:381
  67.3 3.6 %all-to-all-start.3 = ((f32[16,32,256]{2,1,0:T(8,128)}), f32[16,32,256]{2,1,0:T(8,128)S(1)}, u32[]{:S(2)}, u32[]{:S(2)}) async-start(f32[16,32,256]{2,1,0:T(8,128)} %bitcast.7), calls=%async_computation.3 | async-start | bytes 1048576 | tf_op jit(solution)/shard_map/sum_proj/all_to_all | solution.py:393
  70.9 2.8 %collective-permute-start.7 = (bf16[256,896]{1,0:T(8,128)(2,1)S(1)}, bf16[256,896]{1,0:T(8,128)(2,1)S(1)}, u32[]{:S(2)}, u32[]{:S(2)}) collective-permute-start(bf16[256,896]{1,0:T(8,128)(2,1)S(1)} %copy-done.10), channel_id=1, source_target_pairs={{0,32},{32,64},{64,96},{96,128},{128,160},{160,192},{192,224},{224... | collective-permute-start | bytes 1376264 | tf_op jit(solution)/shard_map/gather_grads/ppermute | solution.py:386
  73.7 8.3 %all-to-all-done.3.shares = f32[16,32,256]{2,1,0:T(8,128)S(1)} async-done(((f32[16,32,256]{2,1,0:T(8,128)}), f32[16,32,256]{2,1,0:T(8,128)S(1)}, u32[]{:S(2)}, u32[]{:S(2)}) %all-to-all-start.3) | async-done | bytes 524320 | tf_op jit(solution)/shard_map/sum_proj/all_to_all | solution.py:393
  82.9 3.6 %all-to-all-start.4 = ((f32[16,32,256]{2,1,0:T(8,128)}), f32[16,32,256]{2,1,0:T(8,128)S(1)}, u32[]{:S(2)}, u32[]{:S(2)}) async-start(f32[16,32,256]{2,1,0:T(8,128)} %sum_copies.4), calls=%async_computation.4 | async-start | bytes 1048576 | tf_op jit(solution)/shard_map/sum_proj/all_to_all | solution.py:396
  87.5 8.9 %add_grad.1.buffer = f32[1024,896]{1,0:T(8,128)} custom-call(bf16[2048,1024]{1,0:T(8,128)(2,1)} %all-gather.2.cloned.1.call-done.acts, bf16[256,896]{1,0:T(8,128)(2,1)} %refs_0_.1, bf16[256,896]{1,0:T(8,128)(2,1)} %collective-permute-done.refs_1_, bf16[256,896]{1,0:T(8,128)(2,1)} %collective-permute-done.1.refs_2_, bf16[256,896]{1,0:T(8,128)(2,1)} %copy-done.7, ...), custom_call_target="tpu_custom_call" | custom-call | flops 3758096384 | bytes 15204352 | tf_op jit(solution)/shard_map/sum_proj/add_grad/pallas_call | solution.py:104
  107.2 4.2 %all-to-all-start.5 = ((f32[8,8,256]{2,1,0:T(8,128)}), f32[8,8,256]{2,1,0:T(8,128)S(1)}, u32[]{:S(2)}, u32[]{:S(2)}) async-start(f32[8,8,256]{2,1,0:T(8,128)} %gram.1), calls=%async_computation.6 | async-start | bytes 131072 | tf_op jit(solution)/shard_map/gram/all_to_all | solution.py:410
  111.4 7.2 %all-to-all-done.5.shares = f32[8,8,256]{2,1,0:T(8,128)S(1)} async-done(((f32[8,8,256]{2,1,0:T(8,128)}), f32[8,8,256]{2,1,0:T(8,128)S(1)}, u32[]{:S(2)}, u32[]{:S(2)}) %all-to-all-start.5) | async-done | bytes 65568 | tf_op jit(solution)/shard_map/gram/all_to_all | solution.py:410
  119.4 7.8 %all-to-all-start.6 = ((f32[32,8,256]{2,1,0:T(8,128)}), f32[32,8,256]{2,1,0:T(8,128)S(1)}, u32[]{:S(2)}, u32[]{:S(2)}) async-start(f32[32,8,256]{2,1,0:T(8,128)} %sum_copies.5), calls=%async_computation.7 | async-start | bytes 524288 | tf_op jit(solution)/shard_map/gram/all_to_all | solution.py:411
  127.3 8.8 %all-to-all-done.6 = f32[32,8,256]{2,1,0:T(8,128)S(1)} async-done(((f32[32,8,256]{2,1,0:T(8,128)}), f32[32,8,256]{2,1,0:T(8,128)S(1)}, u32[]{:S(2)}, u32[]{:S(2)}) %all-to-all-start.6) | async-done | bytes 262176 | tf_op jit(solution)/shard_map/gram/all_to_all | solution.py:411
  136.8 8.9 %inverse_factor.1.inverse = f32[256,256]{1,0:T(8,128)} custom-call(f32[256,256]{1,0:T(8,128)} %bitcast.28), custom_call_target="tpu_custom_call" | custom-call | flops 10000000000 | bytes 524288 | tf_op jit(solution)/shard_map/inverse_factor/pallas_call | solution.py:179
  151.7 2.7 %collective-permute-start.12 = (f32[112,256]{1,0:T(8,128)S(1)}, f32[112,256]{1,0:T(8,128)S(1)}, u32[]{:S(2)}, u32[]{:S(2)}) collective-permute-start(f32[112,256]{1,0:T(8,128)S(1)} %collective-permute-done.10.s2), channel_id=1, source_target_pairs={{0,224},{32,0},{64,32},{96,64},{128,96},{160,128},{192,160},{224,1... | collective-permute-start | bytes 344072 | tf_op jit(solution)/shard_map/gather_cross/ppermute | solution.py:424
  156.6 2.7 %collective-permute-start.14 = (f32[112,256]{1,0:T(8,128)S(1)}, f32[112,256]{1,0:T(8,128)S(1)}, u32[]{:S(2)}, u32[]{:S(2)}) collective-permute-start(f32[112,256]{1,0:T(8,128)S(1)} %collective-permute-done.12.s4), channel_id=1, source_target_pairs={{0,224},{32,0},{64,32},{96,64},{128,96},{160,128},{192,160},{224,1... | collective-permute-start | bytes 344072 | tf_op jit(solution)/shard_map/gather_cross/ppermute | solution.py:424
  161.4 4.8 %collective-permute-done.15.s7 = f32[112,256]{1,0:T(8,128)S(1)} collective-permute-done((f32[112,256]{1,0:T(8,128)S(1)}, f32[112,256]{1,0:T(8,128)S(1)}, u32[]{:S(2)}, u32[]{:S(2)}) %collective-permute-start.15) | collective-permute-done | bytes 114720 | tf_op jit(solution)/shard_map/gather_cross/ppermute | solution.py:428
  170.0 9.8 %all-to-all-start.7 = ((f32[32,1,256]{2,1,0:T(1,128)}), f32[32,1,256]{2,1,0:T(1,128)S(1)}, u32[]{:S(2)}, u32[]{:S(2)}) async-start(f32[32,1,256]{2,1,0:T(1,128)} %get-tuple-element.54), calls=%async_computation.8 | async-start | bytes 65536 | tf_op jit(solution)/shard_map/norms/all_to_all | solution.py:433
  181.9 2.9 %update_momentum.1 = f32[1024,896]{1,0:T(8,128)} custom-call(f32[1024,896]{1,0:T(8,128)S(1)} %copy-done.2, f32[1024,256]{1,0:T(8,128)S(1)} %fusion.ortho, f32[896,256]{1,0:T(8,128)S(1)} %get-tuple-element.53.back), custom_call_target="tpu_custom_call" | custom-call | tf_op jit(solution)/shard_map/update_momentum/pallas_call | solution.py:221
  188.7 2.7 %update_weight.1 = (bf16[1024,896]{1,0:T(8,128)(2,1)}, f32[896,256]{1,0:T(8,128)}) custom-call(bf16[1024,896]{1,0:T(8,128)(2,1)S(1)} %copy-done.3, f32[1024,256]{1,0:T(8,128)S(1)} %fusion.ortho, f32[896,256]{1,0:T(8,128)S(1)} %get-tuple-element.53.back, f32[1,256]{1,0:T(1,128)S(1)} %bitcast.24), custom_call_target="tpu_custom_call" | custom-call | tf_op jit(solution)/shard_map/update_weight/pallas_call | solution.py:257
  (75 shorter events, 43.5 us)
Async XLA Ops:
  7.2 79.6 %all-gather.2.cloned.1.call-start = ((), (), s32[]{:S(2)}) async-start(), calls=%async_computation.9 | async-start | bytes 4325376 | tf_op jit(solution)/shard_map/gather_acts/all_gather | solution.py:358
  7.9 20.3 %collective-permute-start = (bf16[256,896]{1,0:T(8,128)(2,1)}, bf16[256,896]{1,0:T(8,128)(2,1)}, u32[]{:S(2)}, u32[]{:S(2)}) collective-permute-start(bf16[256,896]{1,0:T(8,128)(2,1)} %refs_0_.1), channel_id=1, source_target_pairs={{0,32},{32,64},{64,96},{96,128},{128,160},{160,192},{192,224},{224... | collective-permute-start | bytes 1376264 | tf_op jit(solution)/shard_map/proj/gather_grads/ppermute | solution.py:366
  10.5 17.7 %collective-permute-start.1 = (bf16[256,896]{1,0:T(8,128)(2,1)}, bf16[256,896]{1,0:T(8,128)(2,1)}, u32[]{:S(2)}, u32[]{:S(2)}) collective-permute-start(bf16[256,896]{1,0:T(8,128)(2,1)} %refs_0_.1), channel_id=1, source_target_pairs={{0,224},{32,0},{64,32},{96,64},{128,96},{160,128},{192,160},{224,1... | collective-permute-start | bytes 1376264 | tf_op jit(solution)/shard_map/proj/gather_grads/ppermute | solution.py:367
  14.5 13.7 %all-to-all-start = ((bf16[8,8,1024]{2,1,0:T(8,128)(2,1)}), bf16[8,8,1024]{2,1,0:T(8,128)(2,1)S(1)}, u32[]{:S(2)}, u32[]{:S(2)}) async-start(bf16[8,8,1024]{2,1,0:T(8,128)(2,1)} %bitcast.27), calls=%async_computation | async-start | bytes 262144 | tf_op jit(solution)/shard_map/proj/all_to_all | solution.py:374
  28.2 18.0 %collective-permute-start.2 = (bf16[256,896]{1,0:T(8,128)(2,1)}, bf16[256,896]{1,0:T(8,128)(2,1)S(1)}, u32[]{:S(2)}, u32[]{:S(2)}) collective-permute-start(bf16[256,896]{1,0:T(8,128)(2,1)} %collective-permute-done.refs_1_), channel_id=1, source_target_pairs={{0,32},{32,64},{64,96},{96,128},{128,160},{160,192},{192,224},{224... | collective-permute-start | bytes 1376264 | tf_op jit(solution)/shard_map/proj/gather_grads/ppermute | solution.py:366
  28.2 18.0 %collective-permute-start.3 = (bf16[256,896]{1,0:T(8,128)(2,1)}, bf16[256,896]{1,0:T(8,128)(2,1)S(1)}, u32[]{:S(2)}, u32[]{:S(2)}) collective-permute-start(bf16[256,896]{1,0:T(8,128)(2,1)} %collective-permute-done.1.refs_2_), channel_id=1, source_target_pairs={{0,224},{32,0},{64,32},{96,64},{128,96},{160,128},{192,160},{224,1... | collective-permute-start | bytes 1376264 | tf_op jit(solution)/shard_map/proj/gather_grads/ppermute | solution.py:367
  46.2 16.0 %collective-permute-start.4 = (bf16[256,896]{1,0:T(8,128)(2,1)S(1)}, bf16[256,896]{1,0:T(8,128)(2,1)S(1)}, u32[]{:S(2)}, u32[]{:S(2)}) collective-permute-start(bf16[256,896]{1,0:T(8,128)(2,1)S(1)} %collective-permute-done.2.refs_3_), channel_id=1, source_target_pairs={{0,32},{32,64},{64,96},{96,128},{128,160},{160,192},{192,224},{224... | collective-permute-start | bytes 1376264 | tf_op jit(solution)/shard_map/proj/gather_grads/ppermute | solution.py:366
  46.3 15.9 %collective-permute-start.5 = (bf16[256,896]{1,0:T(8,128)(2,1)S(1)}, bf16[256,896]{1,0:T(8,128)(2,1)S(1)}, u32[]{:S(2)}, u32[]{:S(2)}) collective-permute-start(bf16[256,896]{1,0:T(8,128)(2,1)S(1)} %collective-permute-done.3.refs_4_), channel_id=1, source_target_pairs={{0,224},{32,0},{64,32},{96,64},{128,96},{160,128},{192,160},{224,1... | collective-permute-start | bytes 1376264 | tf_op jit(solution)/shard_map/proj/gather_grads/ppermute | solution.py:367
  62.2 4.2 %collective-permute-start.6 = (f32[1024,256]{1,0:T(8,128)S(1)}, f32[1024,256]{1,0:T(8,128)S(1)}, u32[]{:S(2)}, u32[]{:S(2)}) collective-permute-start(f32[1024,256]{1,0:T(8,128)S(1)} %proj_part.1.part), channel_id=1, source_target_pairs={{0,1},{1,0},{2,3},{3,2},{4,5},{5,4},{6,7},{7,6},{8,9},{9,8},{10,11... | collective-permute-start | bytes 3145736 | tf_op jit(solution)/shard_map/sum_proj/ppermute | solution.py:390
  67.3 14.7 %all-to-all-start.3 = ((f32[16,32,256]{2,1,0:T(8,128)}), f32[16,32,256]{2,1,0:T(8,128)S(1)}, u32[]{:S(2)}, u32[]{:S(2)}) async-start(f32[16,32,256]{2,1,0:T(8,128)} %bitcast.7), calls=%async_computation.3 | async-start | bytes 1048576 | tf_op jit(solution)/shard_map/sum_proj/all_to_all | solution.py:393
  70.9 15.8 %collective-permute-start.7 = (bf16[256,896]{1,0:T(8,128)(2,1)S(1)}, bf16[256,896]{1,0:T(8,128)(2,1)S(1)}, u32[]{:S(2)}, u32[]{:S(2)}) collective-permute-start(bf16[256,896]{1,0:T(8,128)(2,1)S(1)} %copy-done.10), channel_id=1, source_target_pairs={{0,32},{32,64},{64,96},{96,128},{128,160},{160,192},{192,224},{224... | collective-permute-start | bytes 1376264 | tf_op jit(solution)/shard_map/gather_grads/ppermute | solution.py:386
  82.9 13.9 %all-to-all-start.4 = ((f32[16,32,256]{2,1,0:T(8,128)}), f32[16,32,256]{2,1,0:T(8,128)S(1)}, u32[]{:S(2)}, u32[]{:S(2)}) async-start(f32[16,32,256]{2,1,0:T(8,128)} %sum_copies.4), calls=%async_computation.4 | async-start | bytes 1048576 | tf_op jit(solution)/shard_map/sum_proj/all_to_all | solution.py:396
  86.5 59.2 %reduce-scatter.2.cloned.1.call-start = ((), (), s32[]{:S(2)}) async-start(), calls=%async_computation.10 | async-start | bytes 1032192 | tf_op jit(solution)/shard_map/cross/reduce_scatter | solution.py:407
  96.8 3.7 %collective-permute-start.8 = (f32[512,256]{1,0:T(8,128)S(1)}, f32[512,256]{1,0:T(8,128)S(1)}, u32[]{:S(2)}, u32[]{:S(2)}) collective-permute-start(f32[512,256]{1,0:T(8,128)S(1)} %bitcast.18), channel_id=1, source_target_pairs={{0,1},{1,0},{2,3},{3,2},{4,5},{5,4},{6,7},{7,6},{8,9},{9,8},{10,11... | collective-permute-start | bytes 1572872 | tf_op jit(solution)/shard_map/sum_proj/ppermute | solution.py:398
  107.2 11.5 %all-to-all-start.5 = ((f32[8,8,256]{2,1,0:T(8,128)}), f32[8,8,256]{2,1,0:T(8,128)S(1)}, u32[]{:S(2)}, u32[]{:S(2)}) async-start(f32[8,8,256]{2,1,0:T(8,128)} %gram.1), calls=%async_computation.6 | async-start | bytes 131072 | tf_op jit(solution)/shard_map/gram/all_to_all | solution.py:410
  119.4 16.8 %all-to-all-start.6 = ((f32[32,8,256]{2,1,0:T(8,128)}), f32[32,8,256]{2,1,0:T(8,128)S(1)}, u32[]{:S(2)}, u32[]{:S(2)}) async-start(f32[32,8,256]{2,1,0:T(8,128)} %sum_copies.5), calls=%async_computation.7 | async-start | bytes 524288 | tf_op jit(solution)/shard_map/gram/all_to_all | solution.py:411
  145.8 5.9 %collective-permute-start.9 = (f32[112,256]{1,0:T(8,128)}, f32[112,256]{1,0:T(8,128)S(1)}, u32[]{:S(2)}, u32[]{:S(2)}) collective-permute-start(f32[112,256]{1,0:T(8,128)} %reduce-scatter.2.cloned.1.call-done.s0), channel_id=1, source_target_pairs={{0,32},{32,64},{64,96},{96,128},{128,160},{160,192},{192,224},{224... | collective-permute-start | bytes 344072 | tf_op jit(solution)/shard_map/gather_cross/ppermute | solution.py:423
  146.0 5.7 %collective-permute-start.10 = (f32[112,256]{1,0:T(8,128)}, f32[112,256]{1,0:T(8,128)S(1)}, u32[]{:S(2)}, u32[]{:S(2)}) collective-permute-start(f32[112,256]{1,0:T(8,128)} %reduce-scatter.2.cloned.1.call-done.s0), channel_id=1, source_target_pairs={{0,224},{32,0},{64,32},{96,64},{128,96},{160,128},{192,160},{224,1... | collective-permute-start | bytes 344072 | tf_op jit(solution)/shard_map/gather_cross/ppermute | solution.py:424
  151.7 4.9 %collective-permute-start.11 = (f32[112,256]{1,0:T(8,128)S(1)}, f32[112,256]{1,0:T(8,128)S(1)}, u32[]{:S(2)}, u32[]{:S(2)}) collective-permute-start(f32[112,256]{1,0:T(8,128)S(1)} %collective-permute-done.9.s1), channel_id=1, source_target_pairs={{0,32},{32,64},{64,96},{96,128},{128,160},{160,192},{192,224},{224... | collective-permute-start | bytes 344072 | tf_op jit(solution)/shard_map/gather_cross/ppermute | solution.py:423
  151.7 4.9 %collective-permute-start.12 = (f32[112,256]{1,0:T(8,128)S(1)}, f32[112,256]{1,0:T(8,128)S(1)}, u32[]{:S(2)}, u32[]{:S(2)}) collective-permute-start(f32[112,256]{1,0:T(8,128)S(1)} %collective-permute-done.10.s2), channel_id=1, source_target_pairs={{0,224},{32,0},{64,32},{96,64},{128,96},{160,128},{192,160},{224,1... | collective-permute-start | bytes 344072 | tf_op jit(solution)/shard_map/gather_cross/ppermute | solution.py:424
  156.6 4.9 %collective-permute-start.13 = (f32[112,256]{1,0:T(8,128)S(1)}, f32[112,256]{1,0:T(8,128)S(1)}, u32[]{:S(2)}, u32[]{:S(2)}) collective-permute-start(f32[112,256]{1,0:T(8,128)S(1)} %collective-permute-done.11.s3), channel_id=1, source_target_pairs={{0,32},{32,64},{64,96},{96,128},{128,160},{160,192},{192,224},{224... | collective-permute-start | bytes 344072 | tf_op jit(solution)/shard_map/gather_cross/ppermute | solution.py:423
  156.6 4.9 %collective-permute-start.14 = (f32[112,256]{1,0:T(8,128)S(1)}, f32[112,256]{1,0:T(8,128)S(1)}, u32[]{:S(2)}, u32[]{:S(2)}) collective-permute-start(f32[112,256]{1,0:T(8,128)S(1)} %collective-permute-done.12.s4), channel_id=1, source_target_pairs={{0,224},{32,0},{64,32},{96,64},{128,96},{160,128},{192,160},{224,1... | collective-permute-start | bytes 344072 | tf_op jit(solution)/shard_map/gather_cross/ppermute | solution.py:424
  161.4 4.9 %collective-permute-start.15 = (f32[112,256]{1,0:T(8,128)S(1)}, f32[112,256]{1,0:T(8,128)S(1)}, u32[]{:S(2)}, u32[]{:S(2)}) collective-permute-start(f32[112,256]{1,0:T(8,128)S(1)} %collective-permute-done.13.s5), channel_id=1, source_target_pairs={{0,32},{32,64},{64,96},{96,128},{128,160},{160,192},{192,224},{224... | collective-permute-start | bytes 344072 | tf_op jit(solution)/shard_map/gather_cross/ppermute | solution.py:428
  170.0 17.1 %all-to-all-start.7 = ((f32[32,1,256]{2,1,0:T(1,128)}), f32[32,1,256]{2,1,0:T(1,128)S(1)}, u32[]{:S(2)}, u32[]{:S(2)}) async-start(f32[32,1,256]{2,1,0:T(1,128)} %get-tuple-element.54), calls=%async_computation.8 | async-start | bytes 65536 | tf_op jit(solution)/shard_map/norms/all_to_all | solution.py:433
  (14 other events, 83.2 us)
Sparse Core Ops, SparseCore 0:
  10.6 56.3 all-gather.1
  107.3 31.4 reduce-scatter.1

commit v8 on v7

--- a/solution.py
+++ b/solution.py
@@ -185,22 +185,32 @@
     )(gram)
 
 
-def back_kernel(inverse, s0, s1, s2, s3, s4, s5, s6, s7, back, norms):
+def early_kernel(inverse, s0, s1, s2, s3, s4, s5, s6, early, sums):
+    total = jnp.zeros(sums.shape, jnp.float32)
+    for n, share in enumerate((s0, s1, s2, s3, s4, s5, s6)):
+        part = dot3(share[...], inverse[...], ((1,), (1,)))
+        early[n] = part
+        total = total + jnp.sum(part * part, axis=0, keepdims=True)
+    sums[...] = total
+
+
+def late_kernel(inverse, share, early, sums, back, norms):
     row = lax.axis_index("row")
-    for n, share in enumerate((s0, s1, s2, s3, s4, s5, s6, s7)):
-        height = share.shape[0]
+    part = dot3(share[...], inverse[...], ((1,), (1,)))
+    height = share.shape[0]
+    for n in range(ROWS):
         start = pl.multiple_of(lax.rem(row + shift(n), ROWS) * height, height)
-        back[pl.ds(start, height), :] = dot3(share[...], inverse[...], ((1,), (1,)))
-    whole = back[...]
-    total = jnp.sum(whole * whole, axis=0, keepdims=True)
+        back[pl.ds(start, height), :] = part if n == ROWS - 1 else early[n]
+    total = sums[...] + jnp.sum(part * part, axis=0, keepdims=True)
     for n in range(norms.shape[0]):
         norms[n] = total
 
 
 def back_and_norms(inverse, shares):
     rank = inverse.shape[0]
-    cols = len(shares) * shares[0].shape[0]
-    return call(back_kernel, "back_and_norms", [(cols, rank), (COLS, 1, rank)], inverse, *shares)
+    height = shares[0].shape[0]
+    early, sums = call(early_kernel, "early", [(ROWS - 1, height, rank), (1, rank)], inverse, *shares[:-1])
+    return call(late_kernel, "late", [(ROWS * height, rank), (COLS, 1, rank)], inverse, shares[-1], early, sums)
 
 
 def momentum_kernel(buffer, ortho, back, new_momentum):

time: 199 us -> 196 us (0.985)
  waiting for transfers between devices: 45 us -> 42.2 us
    ppermute x1, waiting for transfers between devices: 4.85 us -> 1.96 us  [on_device(): parts.append(lax.ppermute(up, 'row', UP))]
    pallas_call x7 -> x8, Pallas kernels: 9 us -> 9.06 us  [call(): pl.pallas_call(kernel, in_specs=[pl.BlockSpec(memory_space=pltpu.SMEM)] *...]
  transfers between devices with their start and end apart: 24 -> 24, of which waited for: 12 -> 12; matrix products, arithmetic and copies ran while one was open for 3% -> 3% of each run, Pallas kernels for 12% -> 13%
where the time goes in v8:
time: 196 us; the launch traced here: 195 us
  starting transfers between devices  62.6 us (32%)
  waiting for transfers between devices  42.2 us (22%)
  Pallas kernels  32.9 us (17%)
  blocking collectives  28 us (14%)
  between operations  14.3 us (7%)
  local copies, waits for them, and re-layouts  8.92 us (5%)
  matrix products  6.26 us (3%)
    all_to_all x1, blocking collectives, on_device(): small = sum_copies(lax.all_to_all(small, 'col', 0, 0), ROWS)  15.2 us
    all_to_all x1, blocking collectives, on_device(): small = lax.all_to_all(small, 'row', 0, 0).reshape(-1, rank)  12.7 us
    all_to_all x1, starting transfers between devices, on_device(): norms = jnp.sum(lax.all_to_all(norms, 'col', 0, 0), axis=0)  9.82 us
    ppermute x3, starting transfers between devices, turn(): down = lax.ppermute(down, 'row', DOWN)  9.36 us
    pallas_call x8, Pallas kernels, call(): pl.pallas_call(kernel, in_specs=[pl.BlockSpec(memory_space=pltpu.SMEM)] *...  9.06 us
    pallas_call x1, Pallas kernels, inverse_factor(): pl.pallas_call(factor_kernel, out_shape=jax.ShapeDtypeStruct((n, n), jnp....  8.94 us
    pallas_call x1, Pallas kernels, add_grad(): pl.pallas_call(grad_kernel, in_specs=[anywhere] * (len(pieces) + 2), out_...  8.9 us
    unnamed x28, local copies, waits for them, and re-layouts  8.9 us
  transfers between devices with their start and end apart: 24, of which 12 were waited for; matrix products, arithmetic and copies ran while one was open for 3% of the time, Pallas kernels for 13%

profile of v8, /device:TPU:1, one launch (start us, length us, event | category | flops | bytes accessed | tf_op | source)
XLA Modules:
  0.0 195.4 jit_solution(5203706134951261875)
XLA Ops:
  10.5 4.0 %collective-permute-start.1 = (bf16[256,896]{1,0:T(8,128)(2,1)}, bf16[256,896]{1,0:T(8,128)(2,1)}, u32[]{:S(2)}, u32[]{:S(2)}) collective-permute-start(bf16[256,896]{1,0:T(8,128)(2,1)} %refs_0_.1), channel_id=1, source_target_pairs={{0,224},{32,0},{64,32},{96,64},{128,96},{160,128},{192,160},{224,1... | collective-permute-start | bytes 1376264 | tf_op jit(solution)/shard_map/proj/gather_grads/ppermute | solution.py:377
  14.5 6.7 %all-to-all-start = ((bf16[8,8,1024]{2,1,0:T(8,128)(2,1)}), bf16[8,8,1024]{2,1,0:T(8,128)(2,1)S(1)}, u32[]{:S(2)}, u32[]{:S(2)}) async-start(bf16[8,8,1024]{2,1,0:T(8,128)(2,1)} %bitcast.27), calls=%async_computation | async-start | bytes 262144 | tf_op jit(solution)/shard_map/proj/all_to_all | solution.py:384
  21.2 3.8 %fusion.6.local = f32[1024,256]{1,0:T(8,128)S(1)} fusion(f32[1024,896]{1,0:T(8,128)} %refs_8_.1, f32[896,256]{1,0:T(8,128)S(1)} %copy-done), kind=kOutput, calls=%fused_computation.9 | convolution fusion | flops 1409286144 | bytes 5636096 | tf_op jit(solution)/shard_map/proj/dot_general | solution.py:387
  25.5 2.7 %all-to-all-done = bf16[8,8,1024]{2,1,0:T(8,128)(2,1)S(1)} async-done(((bf16[8,8,1024]{2,1,0:T(8,128)(2,1)}), bf16[8,8,1024]{2,1,0:T(8,128)(2,1)S(1)}, u32[]{:S(2)}, u32[]{:S(2)}) %all-to-all-start) | async-done | bytes 131104 | tf_op jit(solution)/shard_map/proj/all_to_all | solution.py:384
  28.2 2.7 %collective-permute-start.3 = (bf16[256,896]{1,0:T(8,128)(2,1)}, bf16[256,896]{1,0:T(8,128)(2,1)S(1)}, u32[]{:S(2)}, u32[]{:S(2)}) collective-permute-start(bf16[256,896]{1,0:T(8,128)(2,1)} %collective-permute-done.1.refs_2_), channel_id=1, source_target_pairs={{0,224},{32,0},{64,32},{96,64},{128,96},{160,128},{192,160},{224,1... | collective-permute-start | bytes 1376264 | tf_op jit(solution)/shard_map/proj/gather_grads/ppermute | solution.py:377
  30.9 15.2 %all_to_all.40.shares = f32[32,8,256]{2,1,0:T(8,128)S(1)} all-to-all(f32[32,8,256]{2,1,0:T(8,128)S(1)} %bitcast.26), channel_id=1, replica_groups=mesh['row'=8,'col'=32] {'col'}, dimensions={0} | all-to-all | bytes 524288 | tf_op jit(solution)/shard_map/proj/all_to_all | solution.py:389
  46.3 2.7 %collective-permute-start.5 = (bf16[256,896]{1,0:T(8,128)(2,1)S(1)}, bf16[256,896]{1,0:T(8,128)(2,1)S(1)}, u32[]{:S(2)}, u32[]{:S(2)}) collective-permute-start(bf16[256,896]{1,0:T(8,128)(2,1)S(1)} %collective-permute-done.3.refs_4_), channel_id=1, source_target_pairs={{0,224},{32,0},{64,32},{96,64},{128,96},{160,128},{192,160},{224,1... | collective-permute-start | bytes 1376264 | tf_op jit(solution)/shard_map/proj/gather_grads/ppermute | solution.py:377
  49.0 12.7 %all_to_all.41 = f32[8,8,256]{2,1,0:T(8,128)S(1)} all-to-all(f32[8,8,256]{2,1,0:T(8,128)S(1)} %sum_copies.3), channel_id=1, replica_groups=mesh['row'=8,'col'=32] {'row'}, dimensions={0} | all-to-all | bytes 131072 | tf_op jit(solution)/shard_map/proj/all_to_all | solution.py:391
  67.3 3.6 %all-to-all-start.3 = ((f32[16,32,256]{2,1,0:T(8,128)}), f32[16,32,256]{2,1,0:T(8,128)S(1)}, u32[]{:S(2)}, u32[]{:S(2)}) async-start(f32[16,32,256]{2,1,0:T(8,128)} %bitcast.7), calls=%async_computation.3 | async-start | bytes 1048576 | tf_op jit(solution)/shard_map/sum_proj/all_to_all | solution.py:403
  70.9 2.8 %collective-permute-start.7 = (bf16[256,896]{1,0:T(8,128)(2,1)S(1)}, bf16[256,896]{1,0:T(8,128)(2,1)S(1)}, u32[]{:S(2)}, u32[]{:S(2)}) collective-permute-start(bf16[256,896]{1,0:T(8,128)(2,1)S(1)} %copy-done.10), channel_id=1, source_target_pairs={{0,32},{32,64},{64,96},{96,128},{128,160},{160,192},{192,224},{224... | collective-permute-start | bytes 1376264 | tf_op jit(solution)/shard_map/gather_grads/ppermute | solution.py:396
  73.7 8.3 %all-to-all-done.3.shares = f32[16,32,256]{2,1,0:T(8,128)S(1)} async-done(((f32[16,32,256]{2,1,0:T(8,128)}), f32[16,32,256]{2,1,0:T(8,128)S(1)}, u32[]{:S(2)}, u32[]{:S(2)}) %all-to-all-start.3) | async-done | bytes 524320 | tf_op jit(solution)/shard_map/sum_proj/all_to_all | solution.py:403
  82.9 3.6 %all-to-all-start.4 = ((f32[16,32,256]{2,1,0:T(8,128)}), f32[16,32,256]{2,1,0:T(8,128)S(1)}, u32[]{:S(2)}, u32[]{:S(2)}) async-start(f32[16,32,256]{2,1,0:T(8,128)} %sum_copies.4), calls=%async_computation.4 | async-start | bytes 1048576 | tf_op jit(solution)/shard_map/sum_proj/all_to_all | solution.py:406
  87.5 8.9 %add_grad.1.buffer = f32[1024,896]{1,0:T(8,128)} custom-call(bf16[2048,1024]{1,0:T(8,128)(2,1)} %all-gather.2.cloned.1.call-done.acts, bf16[256,896]{1,0:T(8,128)(2,1)} %refs_0_.1, bf16[256,896]{1,0:T(8,128)(2,1)} %collective-permute-done.refs_1_, bf16[256,896]{1,0:T(8,128)(2,1)} %collective-permute-done.1.refs_2_, bf16[256,896]{1,0:T(8,128)(2,1)} %copy-done.7, ...), custom_call_target="tpu_custom_call" | custom-call | flops 3758096384 | bytes 15204352 | tf_op jit(solution)/shard_map/sum_proj/add_grad/pallas_call | solution.py:104
  104.6 2.6 %cross.1 = f32[896,256]{1,0:T(8,128)} custom-call(s32[1]{0:T(128)} %bitcast.core, f32[1024,896]{1,0:T(8,128)S(1)} %copy-done.1, f32[512,256]{1,0:T(8,128)S(1)} %bitcast.20, f32[512,256]{1,0:T(8,128)S(1)} %collective-permute-done.8.other), custom_call_target="tpu_custom_call" | custom-call | tf_op jit(solution)/shard_map/cross/cross/pallas_call | solution.py:287
  107.2 4.2 %all-to-all-start.5 = ((f32[8,8,256]{2,1,0:T(8,128)}), f32[8,8,256]{2,1,0:T(8,128)S(1)}, u32[]{:S(2)}, u32[]{:S(2)}) async-start(f32[8,8,256]{2,1,0:T(8,128)} %gram.1), calls=%async_computation.6 | async-start | bytes 131072 | tf_op jit(solution)/shard_map/gram/all_to_all | solution.py:420
  111.4 7.2 %all-to-all-done.5.shares = f32[8,8,256]{2,1,0:T(8,128)S(1)} async-done(((f32[8,8,256]{2,1,0:T(8,128)}), f32[8,8,256]{2,1,0:T(8,128)S(1)}, u32[]{:S(2)}, u32[]{:S(2)}) %all-to-all-start.5) | async-done | bytes 65568 | tf_op jit(solution)/shard_map/gram/all_to_all | solution.py:420
  119.4 7.8 %all-to-all-start.6 = ((f32[32,8,256]{2,1,0:T(8,128)}), f32[32,8,256]{2,1,0:T(8,128)S(1)}, u32[]{:S(2)}, u32[]{:S(2)}) async-start(f32[32,8,256]{2,1,0:T(8,128)} %sum_copies.5), calls=%async_computation.7 | async-start | bytes 524288 | tf_op jit(solution)/shard_map/gram/all_to_all | solution.py:421
  127.3 8.8 %all-to-all-done.6 = f32[32,8,256]{2,1,0:T(8,128)S(1)} async-done(((f32[32,8,256]{2,1,0:T(8,128)}), f32[32,8,256]{2,1,0:T(8,128)S(1)}, u32[]{:S(2)}, u32[]{:S(2)}) %all-to-all-start.6) | async-done | bytes 262176 | tf_op jit(solution)/shard_map/gram/all_to_all | solution.py:421
  136.8 8.9 %inverse_factor.1.inverse = f32[256,256]{1,0:T(8,128)} custom-call(f32[256,256]{1,0:T(8,128)} %bitcast.28), custom_call_target="tpu_custom_call" | custom-call | flops 10000000000 | bytes 524288 | tf_op jit(solution)/shard_map/inverse_factor/pallas_call | solution.py:179
  151.7 2.7 %collective-permute-start.14 = (f32[112,256]{1,0:T(8,128)S(1)}, f32[112,256]{1,0:T(8,128)S(1)}, u32[]{:S(2)}, u32[]{:S(2)}) collective-permute-start(f32[112,256]{1,0:T(8,128)S(1)} %collective-permute-done.10.s2), channel_id=1, source_target_pairs={{0,224},{32,0},{64,32},{96,64},{128,96},{160,128},{192,160},{224,1... | collective-permute-start | bytes 344072 | tf_op jit(solution)/shard_map/gather_cross/ppermute | solution.py:434
  156.5 2.7 %collective-permute-start.15 = (f32[112,256]{1,0:T(8,128)S(1)}, f32[112,256]{1,0:T(8,128)S(1)}, u32[]{:S(2)}, u32[]{:S(2)}) collective-permute-start(f32[112,256]{1,0:T(8,128)S(1)} %collective-permute-done.14.s4), channel_id=1, source_target_pairs={{0,224},{32,0},{64,32},{96,64},{128,96},{160,128},{192,160},{224,1... | collective-permute-start | bytes 344072 | tf_op jit(solution)/shard_map/gather_cross/ppermute | solution.py:434
  167.2 9.8 %all-to-all-start.7 = ((f32[32,1,256]{2,1,0:T(1,128)}), f32[32,1,256]{2,1,0:T(1,128)S(1)}, u32[]{:S(2)}, u32[]{:S(2)}) async-start(f32[32,1,256]{2,1,0:T(1,128)} %get-tuple-element.58), calls=%async_computation.8 | async-start | bytes 65536 | tf_op jit(solution)/shard_map/norms/all_to_all | solution.py:443
  179.0 2.9 %update_momentum.1 = f32[1024,896]{1,0:T(8,128)} custom-call(f32[1024,896]{1,0:T(8,128)S(1)} %copy-done.2, f32[1024,256]{1,0:T(8,128)S(1)} %fusion.ortho, f32[896,256]{1,0:T(8,128)S(1)} %get-tuple-element.57.back), custom_call_target="tpu_custom_call" | custom-call | tf_op jit(solution)/shard_map/update_momentum/pallas_call | solution.py:231
  185.8 2.7 %update_weight.1 = (bf16[1024,896]{1,0:T(8,128)(2,1)}, f32[896,256]{1,0:T(8,128)}) custom-call(bf16[1024,896]{1,0:T(8,128)(2,1)S(1)} %copy-done.4, f32[1024,256]{1,0:T(8,128)S(1)} %fusion.ortho, f32[896,256]{1,0:T(8,128)S(1)} %get-tuple-element.57.back, f32[1,256]{1,0:T(1,128)S(1)} %bitcast.24), custom_call_target="tpu_custom_call" | custom-call | tf_op jit(solution)/shard_map/update_weight/pallas_call | solution.py:267
  (76 shorter events, 43.0 us)
Async XLA Ops:
  7.2 79.6 %all-gather.2.cloned.1.call-start = ((), (), s32[]{:S(2)}) async-start(), calls=%async_computation.9 | async-start | bytes 4325376 | tf_op jit(solution)/shard_map/gather_acts/all_gather | solution.py:368
  7.9 20.3 %collective-permute-start = (bf16[256,896]{1,0:T(8,128)(2,1)}, bf16[256,896]{1,0:T(8,128)(2,1)}, u32[]{:S(2)}, u32[]{:S(2)}) collective-permute-start(bf16[256,896]{1,0:T(8,128)(2,1)} %refs_0_.1), channel_id=1, source_target_pairs={{0,32},{32,64},{64,96},{96,128},{128,160},{160,192},{192,224},{224... | collective-permute-start | bytes 1376264 | tf_op jit(solution)/shard_map/proj/gather_grads/ppermute | solution.py:376
  10.5 17.7 %collective-permute-start.1 = (bf16[256,896]{1,0:T(8,128)(2,1)}, bf16[256,896]{1,0:T(8,128)(2,1)}, u32[]{:S(2)}, u32[]{:S(2)}) collective-permute-start(bf16[256,896]{1,0:T(8,128)(2,1)} %refs_0_.1), channel_id=1, source_target_pairs={{0,224},{32,0},{64,32},{96,64},{128,96},{160,128},{192,160},{224,1... | collective-permute-start | bytes 1376264 | tf_op jit(solution)/shard_map/proj/gather_grads/ppermute | solution.py:377
  14.5 13.7 %all-to-all-start = ((bf16[8,8,1024]{2,1,0:T(8,128)(2,1)}), bf16[8,8,1024]{2,1,0:T(8,128)(2,1)S(1)}, u32[]{:S(2)}, u32[]{:S(2)}) async-start(bf16[8,8,1024]{2,1,0:T(8,128)(2,1)} %bitcast.27), calls=%async_computation | async-start | bytes 262144 | tf_op jit(solution)/shard_map/proj/all_to_all | solution.py:384
  28.2 18.0 %collective-permute-start.2 = (bf16[256,896]{1,0:T(8,128)(2,1)}, bf16[256,896]{1,0:T(8,128)(2,1)S(1)}, u32[]{:S(2)}, u32[]{:S(2)}) collective-permute-start(bf16[256,896]{1,0:T(8,128)(2,1)} %collective-permute-done.refs_1_), channel_id=1, source_target_pairs={{0,32},{32,64},{64,96},{96,128},{128,160},{160,192},{192,224},{224... | collective-permute-start | bytes 1376264 | tf_op jit(solution)/shard_map/proj/gather_grads/ppermute | solution.py:376
  28.2 18.0 %collective-permute-start.3 = (bf16[256,896]{1,0:T(8,128)(2,1)}, bf16[256,896]{1,0:T(8,128)(2,1)S(1)}, u32[]{:S(2)}, u32[]{:S(2)}) collective-permute-start(bf16[256,896]{1,0:T(8,128)(2,1)} %collective-permute-done.1.refs_2_), channel_id=1, source_target_pairs={{0,224},{32,0},{64,32},{96,64},{128,96},{160,128},{192,160},{224,1... | collective-permute-start | bytes 1376264 | tf_op jit(solution)/shard_map/proj/gather_grads/ppermute | solution.py:377
  46.2 16.0 %collective-permute-start.4 = (bf16[256,896]{1,0:T(8,128)(2,1)S(1)}, bf16[256,896]{1,0:T(8,128)(2,1)S(1)}, u32[]{:S(2)}, u32[]{:S(2)}) collective-permute-start(bf16[256,896]{1,0:T(8,128)(2,1)S(1)} %collective-permute-done.2.refs_3_), channel_id=1, source_target_pairs={{0,32},{32,64},{64,96},{96,128},{128,160},{160,192},{192,224},{224... | collective-permute-start | bytes 1376264 | tf_op jit(solution)/shard_map/proj/gather_grads/ppermute | solution.py:376
  46.3 15.9 %collective-permute-start.5 = (bf16[256,896]{1,0:T(8,128)(2,1)S(1)}, bf16[256,896]{1,0:T(8,128)(2,1)S(1)}, u32[]{:S(2)}, u32[]{:S(2)}) collective-permute-start(bf16[256,896]{1,0:T(8,128)(2,1)S(1)} %collective-permute-done.3.refs_4_), channel_id=1, source_target_pairs={{0,224},{32,0},{64,32},{96,64},{128,96},{160,128},{192,160},{224,1... | collective-permute-start | bytes 1376264 | tf_op jit(solution)/shard_map/proj/gather_grads/ppermute | solution.py:377
  62.2 4.2 %collective-permute-start.6 = (f32[1024,256]{1,0:T(8,128)S(1)}, f32[1024,256]{1,0:T(8,128)S(1)}, u32[]{:S(2)}, u32[]{:S(2)}) collective-permute-start(f32[1024,256]{1,0:T(8,128)S(1)} %proj_part.1.part), channel_id=1, source_target_pairs={{0,1},{1,0},{2,3},{3,2},{4,5},{5,4},{6,7},{7,6},{8,9},{9,8},{10,11... | collective-permute-start | bytes 3145736 | tf_op jit(solution)/shard_map/sum_proj/ppermute | solution.py:400
  67.3 14.7 %all-to-all-start.3 = ((f32[16,32,256]{2,1,0:T(8,128)}), f32[16,32,256]{2,1,0:T(8,128)S(1)}, u32[]{:S(2)}, u32[]{:S(2)}) async-start(f32[16,32,256]{2,1,0:T(8,128)} %bitcast.7), calls=%async_computation.3 | async-start | bytes 1048576 | tf_op jit(solution)/shard_map/sum_proj/all_to_all | solution.py:403
  70.9 15.8 %collective-permute-start.7 = (bf16[256,896]{1,0:T(8,128)(2,1)S(1)}, bf16[256,896]{1,0:T(8,128)(2,1)S(1)}, u32[]{:S(2)}, u32[]{:S(2)}) collective-permute-start(bf16[256,896]{1,0:T(8,128)(2,1)S(1)} %copy-done.10), channel_id=1, source_target_pairs={{0,32},{32,64},{64,96},{96,128},{128,160},{160,192},{192,224},{224... | collective-permute-start | bytes 1376264 | tf_op jit(solution)/shard_map/gather_grads/ppermute | solution.py:396
  82.9 13.9 %all-to-all-start.4 = ((f32[16,32,256]{2,1,0:T(8,128)}), f32[16,32,256]{2,1,0:T(8,128)S(1)}, u32[]{:S(2)}, u32[]{:S(2)}) async-start(f32[16,32,256]{2,1,0:T(8,128)} %sum_copies.4), calls=%async_computation.4 | async-start | bytes 1048576 | tf_op jit(solution)/shard_map/sum_proj/all_to_all | solution.py:406
  86.5 59.2 %reduce-scatter.2.cloned.1.call-start = ((), (), s32[]{:S(2)}) async-start(), calls=%async_computation.10 | async-start | bytes 1032192 | tf_op jit(solution)/shard_map/cross/reduce_scatter | solution.py:417
  96.8 3.7 %collective-permute-start.8 = (f32[512,256]{1,0:T(8,128)S(1)}, f32[512,256]{1,0:T(8,128)S(1)}, u32[]{:S(2)}, u32[]{:S(2)}) collective-permute-start(f32[512,256]{1,0:T(8,128)S(1)} %bitcast.18), channel_id=1, source_target_pairs={{0,1},{1,0},{2,3},{3,2},{4,5},{5,4},{6,7},{7,6},{8,9},{9,8},{10,11... | collective-permute-start | bytes 1572872 | tf_op jit(solution)/shard_map/sum_proj/ppermute | solution.py:408
  107.2 11.5 %all-to-all-start.5 = ((f32[8,8,256]{2,1,0:T(8,128)}), f32[8,8,256]{2,1,0:T(8,128)S(1)}, u32[]{:S(2)}, u32[]{:S(2)}) async-start(f32[8,8,256]{2,1,0:T(8,128)} %gram.1), calls=%async_computation.6 | async-start | bytes 131072 | tf_op jit(solution)/shard_map/gram/all_to_all | solution.py:420
  119.4 16.7 %all-to-all-start.6 = ((f32[32,8,256]{2,1,0:T(8,128)}), f32[32,8,256]{2,1,0:T(8,128)S(1)}, u32[]{:S(2)}, u32[]{:S(2)}) async-start(f32[32,8,256]{2,1,0:T(8,128)} %sum_copies.5), calls=%async_computation.7 | async-start | bytes 524288 | tf_op jit(solution)/shard_map/gram/all_to_all | solution.py:421
  145.7 5.9 %collective-permute-start.9 = (f32[112,256]{1,0:T(8,128)}, f32[112,256]{1,0:T(8,128)S(1)}, u32[]{:S(2)}, u32[]{:S(2)}) collective-permute-start(f32[112,256]{1,0:T(8,128)} %reduce-scatter.2.cloned.1.call-done.s0), channel_id=1, source_target_pairs={{0,32},{32,64},{64,96},{96,128},{128,160},{160,192},{192,224},{224... | collective-permute-start | bytes 344072 | tf_op jit(solution)/shard_map/gather_cross/ppermute | solution.py:433
  146.0 5.7 %collective-permute-start.10 = (f32[112,256]{1,0:T(8,128)}, f32[112,256]{1,0:T(8,128)S(1)}, u32[]{:S(2)}, u32[]{:S(2)}) collective-permute-start(f32[112,256]{1,0:T(8,128)} %reduce-scatter.2.cloned.1.call-done.s0), channel_id=1, source_target_pairs={{0,224},{32,0},{64,32},{96,64},{128,96},{160,128},{192,160},{224,1... | collective-permute-start | bytes 344072 | tf_op jit(solution)/shard_map/gather_cross/ppermute | solution.py:434
  151.7 4.9 %collective-permute-start.11 = (f32[112,256]{1,0:T(8,128)S(1)}, f32[112,256]{1,0:T(8,128)S(1)}, u32[]{:S(2)}, u32[]{:S(2)}) collective-permute-start(f32[112,256]{1,0:T(8,128)S(1)} %collective-permute-done.9.s1), channel_id=1, source_target_pairs={{0,32},{32,64},{64,96},{96,128},{128,160},{160,192},{192,224},{224... | collective-permute-start | bytes 344072 | tf_op jit(solution)/shard_map/gather_cross/ppermute | solution.py:433
  151.7 4.9 %collective-permute-start.14 = (f32[112,256]{1,0:T(8,128)S(1)}, f32[112,256]{1,0:T(8,128)S(1)}, u32[]{:S(2)}, u32[]{:S(2)}) collective-permute-start(f32[112,256]{1,0:T(8,128)S(1)} %collective-permute-done.10.s2), channel_id=1, source_target_pairs={{0,224},{32,0},{64,32},{96,64},{128,96},{160,128},{192,160},{224,1... | collective-permute-start | bytes 344072 | tf_op jit(solution)/shard_map/gather_cross/ppermute | solution.py:434
  156.5 4.9 %collective-permute-start.12 = (f32[112,256]{1,0:T(8,128)S(1)}, f32[112,256]{1,0:T(8,128)S(1)}, u32[]{:S(2)}, u32[]{:S(2)}) collective-permute-start(f32[112,256]{1,0:T(8,128)S(1)} %collective-permute-done.11.s3), channel_id=1, source_target_pairs={{0,32},{32,64},{64,96},{96,128},{128,160},{160,192},{192,224},{224... | collective-permute-start | bytes 344072 | tf_op jit(solution)/shard_map/gather_cross/ppermute | solution.py:433
  156.5 4.9 %collective-permute-start.15 = (f32[112,256]{1,0:T(8,128)S(1)}, f32[112,256]{1,0:T(8,128)S(1)}, u32[]{:S(2)}, u32[]{:S(2)}) collective-permute-start(f32[112,256]{1,0:T(8,128)S(1)} %collective-permute-done.14.s4), channel_id=1, source_target_pairs={{0,224},{32,0},{64,32},{96,64},{128,96},{160,128},{192,160},{224,1... | collective-permute-start | bytes 344072 | tf_op jit(solution)/shard_map/gather_cross/ppermute | solution.py:434
  161.4 4.9 %collective-permute-start.13 = (f32[112,256]{1,0:T(8,128)S(1)}, f32[112,256]{1,0:T(8,128)S(1)}, u32[]{:S(2)}, u32[]{:S(2)}) collective-permute-start(f32[112,256]{1,0:T(8,128)S(1)} %collective-permute-done.12.s5), channel_id=1, source_target_pairs={{0,32},{32,64},{64,96},{96,128},{128,160},{160,192},{192,224},{224... | collective-permute-start | bytes 344072 | tf_op jit(solution)/shard_map/gather_cross/ppermute | solution.py:438
  167.2 17.1 %all-to-all-start.7 = ((f32[32,1,256]{2,1,0:T(1,128)}), f32[32,1,256]{2,1,0:T(1,128)S(1)}, u32[]{:S(2)}, u32[]{:S(2)}) async-start(f32[32,1,256]{2,1,0:T(1,128)} %get-tuple-element.58), calls=%async_computation.8 | async-start | bytes 65536 | tf_op jit(solution)/shard_map/norms/all_to_all | solution.py:443
  (14 other events, 83.2 us)
Sparse Core Ops, SparseCore 0:
  10.6 56.3 all-gather.1
  107.3 31.4 reduce-scatter.1
